TPU v7x, 32 devices: a whole 2x2x4 slice. The times are simulated.
32 devices in a mesh: slides: 2 (over y), rows: 8 (over z, x), cols: 2 (over core).
Axes of the slice: x: 2, y: 2, z: 4, core: 2. Of those that a mesh axis runs over, the one named last changes fastest.
Arguments:
- tokens: bfloat16 [512, 32, 512], P(('slides', 'cols'), 'rows'), parts along dimension 0, may hold values from -6 to 6
- norm_gain: float32 [512], replicated, may hold values from 0.5 to 1.5
- w_in: bfloat16 [512, 2048], replicated, may hold values from -0.25 to 0.25
- w_bc: bfloat16 [512, 64], replicated, may hold values from -0.046875 to 0.046875
- rate_row: float32 [16, 1024], replicated, may hold values from 0.002 to 0.08
- rate_col: float32 [16, 1024], replicated, may hold values from 0.002 to 0.08
- skip_gain: float32 [1024], replicated, may hold values from 0.5 to 1.5
- w_out: bfloat16 [1024, 512], replicated, may hold values from -0.1875 to 0.1875
Outputs:
- mixed: bfloat16 [512, 32, 512], P(('slides', 'cols'), 'rows'), parts along dimension 0
There are 2 independent parts, one for each index of `slides`. A program takes and returns all parts, laid end to end along the dimension named above; an argument that names none is the same for every part. Nothing has to cross between parts.
All inputs are finite; a program needn't handle non-finite values.
Results may differ from a plain program's by a relative error of at most 0.013.
Values may be sent and summed in bfloat16 or wider, within the bound.
No kernel may reach another device: no remote copies, remote signals or barrier semaphores. Data moves between devices by JAX's collectives and lax.ppermute only.
A program may use at most 64 MiB of HBM per device.

v0:
```python
import jax
import jax.numpy as jnp
from jax import lax
from jax.sharding import PartitionSpec as P


def prefix(shard, axis, combine, identity):
    size, here = (lax.axis_size(axis), lax.axis_index(axis))
    everything = jax.tree.map(
        lambda part, kind: lax.all_gather(part.astype(kind), axis),
        shard,
        (jnp.bfloat16, jnp.bfloat16),
    )
    start = jax.tree.map(
        lambda part, zero: jnp.broadcast_to(jnp.asarray(zero, part.dtype), part.shape),
        shard,
        identity,
    )

    def turn(k, before):
        reached = k < here
        new = combine(
            before, jax.tree.map(lambda part, own: part[k].astype(own.dtype), everything, shard)
        )
        return jax.tree.map(lambda a, b: jnp.where(reached, a, b), new, before)

    return lax.fori_loop(0, size, turn, start)


def block_scan(series, inject, readout, decay_factor, skip_weight, scan_axis):
    block_len = 16
    other_axis = 1 - scan_axis
    item_count = series.shape[other_axis]
    start_state = jnp.zeros((item_count, decay_factor.shape[0], decay_factor.shape[1]), jnp.float32)
    start_out = jnp.zeros(series.shape, jnp.float32)

    def one_block(block_id, carry):
        carried, outputs = carry
        first_row = block_id * block_len
        series_part = lax.dynamic_slice_in_dim(series, first_row, block_len, scan_axis).astype(
            jnp.float32
        )
        inject_part = lax.dynamic_slice_in_dim(inject, first_row, block_len, scan_axis).astype(
            jnp.float32
        )
        readout_part = lax.dynamic_slice_in_dim(readout, first_row, block_len, scan_axis).astype(
            jnp.float32
        )
        results = []
        for offset in range(block_len):
            value_now = lax.index_in_dim(series_part, offset, scan_axis, keepdims=False)
            inject_now = lax.index_in_dim(inject_part, offset, scan_axis, keepdims=False)
            read_now = lax.index_in_dim(readout_part, offset, scan_axis, keepdims=False)
            carried = decay_factor[None] * carried + inject_now[:, :, None] * value_now[:, None, :]
            results.append(
                jnp.einsum("ine,in->ie", carried, read_now, precision=lax.Precision.HIGHEST)
                + skip_weight * value_now
            )
        stacked = jnp.stack(results, axis=scan_axis)
        outputs = lax.dynamic_update_slice_in_dim(outputs, stacked, first_row, scan_axis)
        return (carried, outputs)

    carried, outputs = lax.fori_loop(
        0, series.shape[scan_axis] // block_len, one_block, (start_state, start_out)
    )
    return (outputs, carried)


def chain_join(earlier, later):
    return (earlier[0] * later[0], later[0][None] * earlier[1] + later[1])


def per_device(tokens, norm_gain, w_in, w_bc, rate_row, rate_col, skip_gain, w_out):
    inner_width = w_out.shape[0]
    state_width = rate_row.shape[0]
    as_float = tokens.astype(jnp.float32)
    scale_now = lax.rsqrt(jnp.mean(as_float * as_float, axis=-1, keepdims=True) + 1e-05)
    normed = (as_float * scale_now * norm_gain).astype(jnp.bfloat16)
    project = jnp.dot(normed, w_in, preferred_element_type=jnp.float32)
    inputs_u = project[..., :inner_width].astype(jnp.bfloat16)
    gate_z = project[..., inner_width:].astype(jnp.bfloat16)
    mixers = jnp.dot(normed, w_bc, preferred_element_type=jnp.float32).astype(jnp.bfloat16)
    col_vectors = mixers[..., 2 * state_width :]
    moved_u, moved_vectors = (
        lax.all_to_all(inputs_u, "rows", split_axis=0, concat_axis=1, tiled=True),
        lax.all_to_all(
            mixers[..., : 2 * state_width], "rows", split_axis=0, concat_axis=1, tiled=True
        ),
    )
    row_out, _ = block_scan(
        moved_u,
        moved_vectors[..., :state_width],
        moved_vectors[..., state_width:],
        jnp.exp(-rate_row),
        skip_gain,
        1,
    )
    row_mixed = row_out.astype(jnp.bfloat16)
    back_home = lax.all_to_all(row_mixed, "rows", split_axis=1, concat_axis=0, tiled=True)
    col_readout = col_vectors[..., state_width:]
    col_out, end_state = block_scan(
        back_home, col_vectors[..., :state_width], col_readout, jnp.exp(-rate_col), 1.0, 0
    )
    height = back_home.shape[0]
    total_decay = jnp.exp(-rate_col * height)
    incoming = prefix(
        (total_decay, end_state),
        "cols",
        chain_join,
        (jnp.ones_like(total_decay), jnp.zeros_like(end_state)),
    )[1]

    def correct(block_id, outputs):
        first_row = block_id * 16
        read_part = lax.dynamic_slice_in_dim(col_readout, first_row, 16, 0).astype(jnp.float32)
        steps_ahead = (first_row + 1 + jnp.arange(16, dtype=jnp.int32)).astype(jnp.float32)
        powers = jnp.exp(-rate_col[None] * steps_ahead[:, None, None])
        carried_part = jnp.einsum(
            "lwn,lne,wne->lwe", read_part, powers, incoming, precision=lax.Precision.HIGHEST
        )
        updated = lax.dynamic_slice_in_dim(outputs, first_row, 16, 0) + carried_part
        return lax.dynamic_update_slice_in_dim(outputs, updated, first_row, 0)

    col_out = lax.fori_loop(0, height // 16, correct, col_out)
    gated = (col_out * jax.nn.silu(gate_z.astype(jnp.float32))).astype(jnp.bfloat16)
    return jnp.dot(gated, w_out, preferred_element_type=jnp.float32).astype(jnp.bfloat16)


def solution(mesh):
    placed = (P(("slides", "cols"), "rows", None), P(), P(), P(), P(), P(), P(), P())
    return jax.shard_map(
        per_device,
        mesh=mesh,
        in_specs=placed,
        out_specs=P(("slides", "cols"), "rows", None),
        check_vma=False,
    )
```

profile of v0, /device:TPU:0, one launch (start us, length us, event | category | flops | bytes accessed | tf_op | source)
XLA Modules:
  0.0 232.9 jit_solution(4700963122558836914)
XLA Ops:
  0.0 1.5 fusion.184
  5.0 7.3 %all-to-all-start = ((bf16[8,2,1024]{2,1,0:T(2,128)(2,1)}), bf16[8,2,1024]{2,1,0:T(2,128)(2,1)S(1)}, u32[]{:S(2)}, u32[]{:S(2)}) async-start(bf16[8,2,1024]{2,1,0:T(2,128)(2,1)} %reshape.149), calls=%async_computation | async-start | bytes 65536 | tf_op jit(solution)/shard_map/all_to_all | solution.py:86
  15.0 1.8 copy.78
  16.8 2.2 all-to-all-done
  19.0 3.8 %all-to-all-start.1 = ((bf16[128,4,1024]{2,1,0:T(4,128)(2,1)}), bf16[128,4,1024]{2,1,0:T(4,128)(2,1)S(1)}, u32[]{:S(2)}, u32[]{:S(2)}) async-start(bf16[128,4,1024]{2,1,0:T(4,128)(2,1)} %copy.78), calls=%async_computation.1 | async-start | bytes 2097152 | tf_op jit(solution)/shard_map/all_to_all | solution.py:85
  23.8 24.4 %all-to-all-done.1 = bf16[128,4,1024]{2,1,0:T(4,128)(2,1)S(1)} async-done(((bf16[128,4,1024]{2,1,0:T(4,128)(2,1)}), bf16[128,4,1024]{2,1,0:T(4,128)(2,1)S(1)}, u32[]{:S(2)}, u32[]{:S(2)}) %all-to-all-start.1) | async-done | bytes 1048608 | tf_op jit(solution)/shard_map/all_to_all | solution.py:85
  50.7 44.3 %while.62 = (s32[]{:T(128)}, f32[16,16,1024]{2,1,0:T(8,128)}, bf16[16,32,1024]{2,0,1:T(8,128)(2,1)}, f32[16,1024]{1,0:T(8,128)S(1)}, bf16[16,32,16]{2,0,1:T(8,12...) while((s32[]{:T(128)}, f32[16,16,1024]{2,1,0:T(8,128)}, ...), condition=%wide.region_2.0_spmd.clone, body=%wide.region_1.0_spmd.clone.sunk | while | flops 94638096 | bytes 42889080 | solution.py:63
  50.7 1.5 fusion.296
  54.0 1.4 fusion.297
  55.5 1.5 fusion.298
  61.7 2.3 multiply_add_fusion.115
  72.3 1.5 fusion.296
  75.6 2.0 fusion.297
  77.6 2.0 fusion.298
  84.3 2.3 multiply_add_fusion.115
  95.0 4.4 %all-to-all-start.2 = ((bf16[16,32,1024]{2,0,1:T(8,128)(2,1)}), bf16[16,32,1024]{2,0,1:T(8,128)(2,1)}, u32[]{:S(2)}, u32[]{:S(2)}) async-start(bf16[16,32,1024]{2,0,1:T(8,128)(2,1)} %get-tuple-element.491), calls=%async_computation.2 | async-start | bytes 2097152 | tf_op jit(solution)/shard_map/all_to_all | solution.py:99
  99.6 1.9 all-gather
  101.5 23.3 %all-to-all-done.2 = bf16[16,32,1024]{2,0,1:T(8,128)(2,1)} async-done(((bf16[16,32,1024]{2,0,1:T(8,128)(2,1)}), bf16[16,32,1024]{2,0,1:T(8,128)(2,1)}, u32[]{:S(2)}, u32[]{:S(2)}) %all-to-all-start.2) | async-done | bytes 1048608 | tf_op jit(solution)/shard_map/all_to_all | solution.py:99
  124.8 3.0 %copy.80 = bf16[16,8,4,1024]{3,2,0,1:T(4,128)(2,1)} copy(bf16[16,8,4,1024]{3,0,2,1:T(8,128)(2,1)} %bitcast.13) | data formatting | bytes 2097152 | tf_op jit(solution)/shard_map/all_to_all | solution.py:99
  127.8 1.8 broadcast_in_dim.18
  129.7 69.7 %while.63 = (s32[]{:T(128)}, f32[4,16,1024]{2,1,0:T(8,128)S(1)}, f32[128,4,1024]{2,1,0:T(4,128)}, f32[16,1024]{1,0:T(8,128)S(1)}, bf16[128,4,16]{0,2,1:T(8,128)(...) while((s32[]{:T(128)}, f32[4,16,1024]{2,1,0:T(8,128)S(1)}, ...), condition=%wide.region_4.0_spmd.clone, body=%wide.region_3.0_spmd.clone.sunk | while | flops 27526164 | bytes 9698083 | solution.py:63
  199.4 2.0 all-gather.1
  201.8 26.2 %while.61 = (s32[]{:T(128)}, f32[128,4,1024]{2,1,0:T(4,128)}, f32[1,16,1024]{2,1,0:T(8,128)S(1)}, bf16[128,4,16]{2,1,0:T(4,128)(2,1)S(1)}, f32[4,16,1024]{2,1,0:...) while((s32[]{:T(128)}, f32[128,4,1024]{2,1,0:T(4,128)}, f32[1,16,1024]{2,1,0:T(8,128)S(1)}, ...), condition=%wide.region_8.9_spmd, body=%wide.region_7.8_spmd.sunk | while | flops 3408935 | bytes 3483939 | solution.py:124
  203.4 1.7 fusion.275
  206.6 1.8 fusion.275
  209.9 1.7 fusion.275
  213.2 1.7 fusion.275
  216.5 1.8 fusion.275
  219.8 1.7 fusion.275
  223.0 1.7 fusion.275
  226.3 1.7 fusion.275
  228.0 3.7 %convolution_convert_fusion.1 = bf16[128,4,512]{2,0,1:T(8,128)(2,1)S(1)} fusion(bf16[1024,512]{1,0:T(8,128)(2,1)} %param.23, f32[128,4,1024]{2,1,0:T(4,128)} %get-tuple-element.495, bf16[128,4,2048]{2,0,1:T(8,128)(2,1)} %copy-done.5), kind=kOutput, calls=%fused_computation.390 | convolution fusion | flops 540803072 | bytes 4718592 | tf_op jit(solution)/shard_map/dot_general | solution.py:126
  (520 shorter events, 120.5 us)
Async XLA Ops:
  0.0 12.3 %copy-start = (bf16[512,2048]{1,0:T(8,128)(2,1)S(1)}, bf16[512,2048]{1,0:T(8,128)(2,1)}, u32[]{:S(2)}) copy-start(bf16[512,2048]{1,0:T(8,128)(2,1)} %param.18) | copy-start | bytes 6291460
  4.1 0.9 copy-start.17
  5.0 13.9 %all-to-all-start = ((bf16[8,2,1024]{2,1,0:T(2,128)(2,1)}), bf16[8,2,1024]{2,1,0:T(2,128)(2,1)S(1)}, u32[]{:S(2)}, u32[]{:S(2)}) async-start(bf16[8,2,1024]{2,1,0:T(2,128)(2,1)} %reshape.149), calls=%async_computation | async-start | bytes 65536 | tf_op jit(solution)/shard_map/all_to_all | solution.py:86
  13.6 1.4 copy-start.5
  15.0 7.8 %copy-start.16 = (f32[16,1024]{1,0:T(8,128)S(1)}, f32[16,1024]{1,0:T(8,128)}, u32[]{:S(2)}) copy-start(f32[16,1024]{1,0:T(8,128)} %param.20) | copy-start | bytes 196612
  19.0 29.3 %all-to-all-start.1 = ((bf16[128,4,1024]{2,1,0:T(4,128)(2,1)}), bf16[128,4,1024]{2,1,0:T(4,128)(2,1)S(1)}, u32[]{:S(2)}, u32[]{:S(2)}) async-start(bf16[128,4,1024]{2,1,0:T(4,128)(2,1)} %copy.78), calls=%async_computation.1 | async-start | bytes 2097152 | tf_op jit(solution)/shard_map/all_to_all | solution.py:85
  23.0 27.7 %copy-start.3 = (f32[1024]{0:T(1024)S(1)}, f32[1024]{0:T(1024)}, u32[]{:S(2)}) copy-start(f32[1024]{0:T(1024)} %param.22) | copy-start | bytes 12292
  54.0 3.0 %copy-start.1 = (f32[16,16,1024]{2,1,0:T(8,128)S(1)}, f32[16,16,1024]{2,1,0:T(8,128)}, u32[]{:S(2)}) copy-start(f32[16,16,1024]{2,1,0:T(8,128)} %get-tuple-element.1202) | copy-start | bytes 3145732 | tf_op jit(solution)/shard_map/while
  54.0 3.0 %copy-start.4 = (f32[16,16]{1,0:T(8,128)S(1)}, f32[16,16]{1,0:T(8,128)}, u32[]{:S(2)}) copy-start(f32[16,16]{1,0:T(8,128)} %get-tuple-element.1055) | copy-start | bytes 3076 | tf_op jit(solution)/shard_map/while
  54.0 3.0 %copy-start.14 = (bf16[16,16,1]{1,0,2:T(8,128)(2,1)S(1)}, bf16[16,16,1]{1,0,2:T(8,128)(2,1)}, u32[]{:S(2)}) copy-start(bf16[16,16,1]{1,0,2:T(8,128)(2,1)} %get-tuple-element.1058) | copy-start | bytes 1540 | tf_op jit(solution)/shard_map/while
  57.0 1.0 copy-start.13
  58.0 1.1 copy-start.12
  59.1 1.2 copy-start.11
  61.6 2.3 %copy-start.10 = (bf16[16,16,1]{1,0,2:T(8,128)(2,1)S(1)}, bf16[16,16,1]{1,0,2:T(8,128)(2,1)}, u32[]{:S(2)}) copy-start(bf16[16,16,1]{1,0,2:T(8,128)(2,1)} %get-tuple-element.1105) | copy-start | bytes 1540 | tf_op jit(solution)/shard_map/while
  64.0 7.0 %copy-start.2 = (f32[16,16,1024]{2,1,0:T(8,128)}, f32[16,16,1024]{2,1,0:T(8,128)S(1)}, u32[]{:S(2)}) copy-start(f32[16,16,1024]{2,1,0:T(8,128)S(1)} %get-tuple-element.1229) | copy-start | bytes 3145732 | tf_op jit(solution)/shard_map/while
  64.0 1.0 copy-start.9
  65.9 1.5 copy-start.7
  66.7 1.6 copy-start.6
  75.6 4.1 %copy-start.1 = (f32[16,16,1024]{2,1,0:T(8,128)S(1)}, f32[16,16,1024]{2,1,0:T(8,128)}, u32[]{:S(2)}) copy-start(f32[16,16,1024]{2,1,0:T(8,128)} %get-tuple-element.1202) | copy-start | bytes 3145732 | tf_op jit(solution)/shard_map/while
  75.6 4.1 %copy-start.4 = (f32[16,16]{1,0:T(8,128)S(1)}, f32[16,16]{1,0:T(8,128)}, u32[]{:S(2)}) copy-start(f32[16,16]{1,0:T(8,128)} %get-tuple-element.1055) | copy-start | bytes 3076 | tf_op jit(solution)/shard_map/while
  75.6 4.1 %copy-start.14 = (bf16[16,16,1]{1,0,2:T(8,128)(2,1)S(1)}, bf16[16,16,1]{1,0,2:T(8,128)(2,1)}, u32[]{:S(2)}) copy-start(bf16[16,16,1]{1,0,2:T(8,128)(2,1)} %get-tuple-element.1058) | copy-start | bytes 1540 | tf_op jit(solution)/shard_map/while
  79.7 1.0 copy-start.13
  80.7 1.1 copy-start.12
  81.8 1.2 copy-start.11
  84.3 2.3 %copy-start.10 = (bf16[16,16,1]{1,0,2:T(8,128)(2,1)S(1)}, bf16[16,16,1]{1,0,2:T(8,128)(2,1)}, u32[]{:S(2)}) copy-start(bf16[16,16,1]{1,0,2:T(8,128)(2,1)} %get-tuple-element.1105) | copy-start | bytes 1540 | tf_op jit(solution)/shard_map/while
  86.6 7.0 %copy-start.2 = (f32[16,16,1024]{2,1,0:T(8,128)}, f32[16,16,1024]{2,1,0:T(8,128)S(1)}, u32[]{:S(2)}) copy-start(f32[16,16,1024]{2,1,0:T(8,128)S(1)} %get-tuple-element.1229) | copy-start | bytes 3145732 | tf_op jit(solution)/shard_map/while
  86.6 1.0 copy-start.9
  88.6 1.5 copy-start.7
  89.4 1.6 copy-start.6
  95.0 4.4 %copy-start.18 = (bf16[128,4,64]{0,2,1:T(8,128)(2,1)S(1)}, bf16[128,4,64]{0,2,1:T(8,128)(2,1)}, u32[]{:S(2)}) copy-start(bf16[128,4,64]{0,2,1:T(8,128)(2,1)} %copy-done.17) | copy-start | bytes 196612
  95.0 4.6 %copy-start.15 = (f32[16,1024]{1,0:T(8,128)S(1)}, f32[16,1024]{1,0:T(8,128)}, u32[]{:S(2)}) copy-start(f32[16,1024]{1,0:T(8,128)} %param.21) | copy-start | bytes 196612
  95.0 29.8 %all-to-all-start.2 = ((bf16[16,32,1024]{2,0,1:T(8,128)(2,1)}), bf16[16,32,1024]{2,0,1:T(8,128)(2,1)}, u32[]{:S(2)}, u32[]{:S(2)}) async-start(bf16[16,32,1024]{2,0,1:T(8,128)(2,1)} %get-tuple-element.491), calls=%async_computation.2 | async-start | bytes 2097152 | tf_op jit(solution)/shard_map/all_to_all | solution.py:99
  (2 other events, 1.9 us)
where the time goes:
time: 234 us; the launch traced here: 233 us
  matrix products  81.9 us (35%)
  other arithmetic  51.2 us (22%)
  waiting for transfers between devices  49.9 us (21%)
  local copies, waits for them, and re-layouts  27.4 us (12%)
  starting transfers between devices  15.5 us (7%)
  blocking collectives  3.85 us (2%)
  loops' own time  3.01 us (1%)
    dot_general x160, matrix products, one_block(): jnp.einsum('ine,in->ie', carried, read_now, precision=lax.Precision.HIGHEST)  75.8 us
    all_to_all x1, waiting for transfers between devices, per_device(): lax.all_to_all(inputs_u, 'rows', split_axis=0, concat_axis=1, tiled=True)  24.4 us
    all_to_all x1, waiting for transfers between devices, per_device(): lax.all_to_all(row_mixed, 'rows', split_axis=1, concat_axis=0, tiled=True)  23.3 us
    dynamic_update_slice x8, other arithmetic, correct(): return lax.dynamic_update_slice_in_dim(outputs, updated, first_row, 0)  13.9 us
    dot_general x8, other arithmetic, correct(): jnp.einsum('lwn,lne,wne->lwe', read_part, powers, incoming, precision=lax...  10.4 us
    convert_element_type x10, other arithmetic, one_block(): lax.dynamic_slice_in_dim(series, first_row, block_len, scan_axis)  9.74 us
    add x10, other arithmetic, one_block(): decay_factor[None] * carried  9.09 us
    dynamic_update_slice x10, local copies, waits for them, and re-layouts, one_block(): lax.dynamic_update_slice_in_dim(outputs, stacked, first_row, scan_axis)  7.58 us
  transfers between devices with their start and end apart: 3, of which 3 were waited for; matrix products, arithmetic and copies ran while one was open for 2% of the time, Pallas kernels for 0%

commit v1 on v0

v1 whole, which is shorter than its diff:
```python
import functools

import jax
import jax.numpy as jnp
import numpy as np
from jax import lax
from jax.experimental import pallas as pl
from jax.experimental.pallas import tpu as pltpu
from jax.sharding import PartitionSpec as P

F32 = jnp.float32
BF16 = jnp.bfloat16
VMEM = pl.BlockSpec(memory_space=pltpu.VMEM)
LANES = 128


def normalise(tokens, gain):
    as_float = tokens.astype(F32)
    scale_now = lax.rsqrt(jnp.mean(as_float * as_float, axis=-1, keepdims=True) + 1e-05)
    return (as_float * scale_now * gain).astype(BF16)


def dot(a, b):
    return jnp.dot(a, b, preferred_element_type=F32)


def params():
    return pltpu.CompilerParams(vmem_limit_bytes=40 << 20)


def selection(shape, sources):
    matrix = np.zeros(shape, np.float32)
    matrix[np.arange(shape[0]), sources] = 1.0
    return jnp.asarray(matrix, BF16)


def row_order(items, columns):
    c, i = np.divmod(np.arange(items * columns), items)
    return selection((items * columns,) * 2, i * columns + c)


def spread_order(items, folds, columns):
    i, rest = np.divmod(np.arange(items * folds * columns), folds * columns)
    return selection((items * folds * columns,) * 2, rest * items + i)


def repeat_order(items, folds, columns):
    i, rest = np.divmod(np.arange(items * folds * columns), folds * columns)
    return selection((items * folds * columns, items * columns), i * columns + rest % columns)


def gather_order(items, folds, columns):
    f, rest = np.divmod(np.arange(items * folds * columns), items * columns)
    i, c = np.divmod(rest, columns)
    return selection((items * folds * columns,) * 2, (i * folds + f) * columns + c)


def lane_table(state):
    return jnp.asarray(np.repeat(np.eye(state, dtype=np.float32), LANES, axis=1), BF16)


def row_kernel(parts, items, columns, x_ref, gain_ref, wu_ref, wb_ref, wc_ref, rate_ref, skip_ref,
               order_ref, spread_ref, out_ref, normed, b_scr, c_scr, u_scr, y_scr, g_scr):
    block = items * columns
    steps = parts * columns
    rows = steps * items
    inner = u_scr.shape[1]
    folds = spread_ref.shape[0] // block
    gain = gain_ref[...]
    for part in range(parts):
        here = normalise(x_ref[part], gain)
        normed[part * block:(part + 1) * block, :] = dot(order_ref[...], here).astype(BF16)
    b_scr[...] = dot(normed[...], wb_ref[...]).astype(BF16).astype(F32)
    c_scr[...] = dot(normed[...], wc_ref[...]).astype(BF16).astype(F32)
    chunk = 128
    pieces = []
    at = 0
    for lag in range(steps):
        first = lag * items
        while first < rows:
            count = min(chunk, rows - first)
            pieces.append((lag, first, count, at))
            first += count
            at += count
    for lag, first, count, at in pieces:
        source = first - lag * items
        product = c_scr[first:first + count, :] * b_scr[source:source + count, :]
        g_scr[at:at + count, :] = product.astype(BF16)
    tile = 512

    def one_tile(tile_id, _):
        where = pl.ds(pl.multiple_of(tile_id * tile, tile), tile)
        u_scr[:, where] = dot(normed[...], wu_ref[:, where]).astype(BF16).astype(F32)
        rate = rate_ref[:, where]
        skip = skip_ref[:, where]
        done = -1
        table = None
        for lag, first, count, at in pieces:
            if lag != done:
                power = jnp.exp(rate * (-float(lag)))
                high = power.astype(BF16)
                low = (power - high.astype(F32)).astype(BF16)
                table = jnp.concatenate([high, low], axis=0)
                done = lag
            matrix = dot(g_scr[at:at + count, :], table)
            source = first - lag * items
            value = u_scr[source:source + count, where]
            if lag == 0:
                y_scr[first:first + count, where] = (matrix + skip) * value
            else:
                y_scr[first:first + count, where] += matrix * value
        return 0

    lax.fori_loop(0, inner // tile, one_tile, 0)
    width = inner // folds
    for part in range(parts):
        here = slice(part * block, (part + 1) * block)
        stacked = jnp.concatenate(
            [y_scr[here, f * width:(f + 1) * width].astype(BF16) for f in range(folds)], axis=0
        )
        out_ref[part] = dot(spread_ref[...], stacked).astype(BF16)


def row_scan(x, columns, folds, gain, w_u, w_bc, rate, skip):
    parts, block, width = x.shape
    items = block // columns
    inner = w_u.shape[1]
    state = rate.shape[0]
    rows = parts * block
    w_b, w_c = w_bc[:, :state], w_bc[:, state:2 * state]
    w_b = jnp.concatenate([w_b, w_b], axis=1)
    w_c = jnp.concatenate([w_c, w_c], axis=1)
    return pl.pallas_call(
        functools.partial(row_kernel, parts, items, columns),
        name="row_scan",
        out_shape=jax.ShapeDtypeStruct((parts, folds * block, inner // folds), BF16),
        in_specs=[VMEM] * 9,
        out_specs=VMEM,
        scratch_shapes=[
            pltpu.VMEM((rows, width), BF16),
            pltpu.VMEM((rows, 2 * state), F32),
            pltpu.VMEM((rows, 2 * state), F32),
            pltpu.VMEM((rows, inner), F32),
            pltpu.VMEM((rows, inner), F32),
            pltpu.VMEM((rows * (parts * columns + 1) // 2, 2 * state), BF16),
        ],
        compiler_params=params(),
        cost_estimate=pl.CostEstimate(
            flops=2 * rows * width * inner * 16, bytes_accessed=4 << 20, transcendentals=0
        ),
    )(x, gain[None, :], w_u, w_b, w_c, rate, skip[None, :], row_order(items, columns),
      spread_order(items, folds, columns))


def home_kernel(folds, columns, x_ref, gain_ref, wz_ref, wm_ref, repeat_ref, gate_ref, mix_ref):
    block = repeat_ref.shape[1]
    tall = repeat_ref.shape[0]
    width = wz_ref.shape[1] // folds
    fold_of = (lax.broadcasted_iota(jnp.int32, (tall, 1), 0) % (folds * columns)) // columns
    for start in range(x_ref.shape[0] // block):
        here = normalise(x_ref[start * block:(start + 1) * block, :], gain_ref[...])
        here = dot(repeat_ref[...], here).astype(BF16)
        there = slice(start * tall, (start + 1) * tall)
        project = dot(here, wz_ref[...])
        gate = project[:, :width]
        for fold in range(1, folds):
            gate = jnp.where(fold_of == fold, project[:, fold * width:(fold + 1) * width], gate)
        gate = gate.astype(BF16).astype(F32)
        gate_ref[there, :] = gate / (1.0 + jnp.exp(-gate))
        mix_ref[there, :] = dot(here, wm_ref[...]).astype(BF16)


def home(x, items, columns, folds, gain, w_z, w_m):
    rows = x.shape[0]
    return pl.pallas_call(
        functools.partial(home_kernel, folds, columns),
        name="home",
        out_shape=(
            jax.ShapeDtypeStruct((rows * folds, w_z.shape[1] // folds), F32),
            jax.ShapeDtypeStruct((rows * folds, w_m.shape[1]), BF16),
        ),
        in_specs=[VMEM] * 5,
        out_specs=(VMEM, VMEM),
        compiler_params=params(),
        cost_estimate=pl.CostEstimate(
            flops=4 * rows * x.shape[1] * w_z.shape[1], bytes_accessed=4 << 20, transcendentals=0
        ),
    )(x, gain[None, :], w_z, w_m, repeat_order(items, folds, columns))


def col_kernel(state, y_ref, mix_ref, rate_ref, table_ref, out_ref, end_ref, held, decay, b_scr, c_scr, v_scr):
    width = y_ref.shape[1]
    step_count = y_ref.shape[0] // 8

    @pl.when(pl.program_id(0) == 0)
    def _():
        held[...] = jnp.zeros_like(held)
        decay[...] = jnp.exp(-rate_ref[...])

    b_scr[...] = dot(mix_ref[:, :state], table_ref[...])
    c_scr[...] = dot(mix_ref[:, state:], table_ref[...])
    v_scr[...] = y_ref[...].astype(F32)
    tiles = 2
    for first in range(0, width // LANES, tiles):
        spans = [slice((first + k) * LANES, (first + k + 1) * LANES) for k in range(tiles)]

        def step(t, carry):
            at = pl.ds(pl.multiple_of(t * 8, 8), 8)
            value = [v_scr[at, span] for span in spans]
            total = list(value)
            new = []
            for n in range(state):
                b = b_scr[at, n * LANES:(n + 1) * LANES]
                c = c_scr[at, n * LANES:(n + 1) * LANES]
                for k, span in enumerate(spans):
                    h = decay[n, :, span] * carry[n * tiles + k] + b * value[k]
                    total[k] = total[k] + c * h
                    new.append(h)
            for k, span in enumerate(spans):
                out_ref[at, span] = total[k]
            return tuple(new)

        start = tuple(held[n, :, span] for n in range(state) for span in spans)
        end = lax.fori_loop(0, step_count, step, start, unroll=2)
        for n in range(state):
            for k, span in enumerate(spans):
                held[n, :, span] = end[n * tiles + k]

    @pl.when(pl.program_id(0) == pl.num_programs(0) - 1)
    def _():
        end_ref[...] = held[...].astype(BF16)


def col_scan(y, mix, rate, steps_at_once):
    rows, width = y.shape
    state = rate.shape[0]
    block = steps_at_once * 8
    return pl.pallas_call(
        functools.partial(col_kernel, state),
        name="col_scan",
        grid=(rows // block,),
        out_shape=(
            jax.ShapeDtypeStruct((rows, width), F32),
            jax.ShapeDtypeStruct(rate.shape, BF16),
        ),
        in_specs=[
            pl.BlockSpec((block, width), lambda i: (i, 0)),
            pl.BlockSpec((block, 2 * state), lambda i: (i, 0)),
            pl.BlockSpec(rate.shape, lambda i: (0, 0, 0)),
            pl.BlockSpec((state, state * LANES), lambda i: (0, 0)),
        ],
        out_specs=(
            pl.BlockSpec((block, width), lambda i: (i, 0)),
            pl.BlockSpec(rate.shape, lambda i: (0, 0, 0)),
        ),
        scratch_shapes=[
            pltpu.VMEM(rate.shape, F32),
            pltpu.VMEM(rate.shape, F32),
            pltpu.VMEM((block, state * LANES), F32),
            pltpu.VMEM((block, state * LANES), F32),
            pltpu.VMEM((block, width), F32),
        ],
        compiler_params=params(),
        cost_estimate=pl.CostEstimate(flops=rows * width * 16 * 100, bytes_accessed=8 << 20, transcendentals=0),
    )(y, mix, rate, lane_table(state))


def last_kernel(state, folds, y_ref, gate_ref, mix_ref, in_ref, rate_ref, table_ref, order_ref, w_ref,
                out_ref, held, decay, c_scr, g_scr):
    width = y_ref.shape[1]
    step_count = y_ref.shape[0] // 8

    @pl.when(pl.program_id(0) == 0)
    def _():
        held[...] = in_ref[...].astype(F32)
        decay[...] = jnp.exp(-rate_ref[...])

    c_scr[...] = dot(mix_ref[:, state:], table_ref[...])
    tiles = 2
    for first in range(0, width // LANES, tiles):
        spans = [slice((first + k) * LANES, (first + k + 1) * LANES) for k in range(tiles)]

        def step(t, carry):
            at = pl.ds(pl.multiple_of(t * 8, 8), 8)
            total = [y_ref[at, span] for span in spans]
            new = []
            for n in range(state):
                c = c_scr[at, n * LANES:(n + 1) * LANES]
                for k, span in enumerate(spans):
                    h = decay[n, :, span] * carry[n * tiles + k]
                    total[k] = total[k] + c * h
                    new.append(h)
            for k, span in enumerate(spans):
                g_scr[at, span] = total[k] * gate_ref[at, span]
            return tuple(new)

        start = tuple(held[n, :, span] for n in range(state) for span in spans)
        end = lax.fori_loop(0, step_count, step, start, unroll=2)
        for n in range(state):
            for k, span in enumerate(spans):
                held[n, :, span] = end[n * tiles + k]

    gated = dot(order_ref[...], g_scr[...].astype(BF16)).astype(BF16)
    rows = gated.shape[0] // folds
    total = dot(gated[:rows], w_ref[:width, :])
    for fold in range(1, folds):
        total = total + dot(gated[fold * rows:(fold + 1) * rows], w_ref[fold * width:(fold + 1) * width, :])
    out_ref[...] = total.astype(BF16)


def last(y, gate, mix, incoming, rate, w_out, folds, columns, steps_at_once):
    rows, width = y.shape
    state = rate.shape[0]
    block = steps_at_once * 8
    return pl.pallas_call(
        functools.partial(last_kernel, state, folds),
        name="last",
        grid=(rows // block,),
        out_shape=jax.ShapeDtypeStruct((rows // folds, w_out.shape[1]), BF16),
        in_specs=[
            pl.BlockSpec((block, width), lambda i: (i, 0)),
            pl.BlockSpec((block, width), lambda i: (i, 0)),
            pl.BlockSpec((block, 2 * state), lambda i: (i, 0)),
            pl.BlockSpec(rate.shape, lambda i: (0, 0, 0)),
            pl.BlockSpec(rate.shape, lambda i: (0, 0, 0)),
            pl.BlockSpec((state, state * LANES), lambda i: (0, 0)),
            pl.BlockSpec((block, block), lambda i: (0, 0)),
            pl.BlockSpec(w_out.shape, lambda i: (0, 0)),
        ],
        out_specs=pl.BlockSpec((block // folds, w_out.shape[1]), lambda i: (i, 0)),
        scratch_shapes=[
            pltpu.VMEM(rate.shape, F32),
            pltpu.VMEM(rate.shape, F32),
            pltpu.VMEM((block, state * LANES), F32),
            pltpu.VMEM((block, width), F32),
        ],
        compiler_params=params(),
        cost_estimate=pl.CostEstimate(flops=rows * width * 16 * 60, bytes_accessed=8 << 20, transcendentals=0),
    )(y, gate, mix, incoming, rate, lane_table(state), gather_order(steps_at_once, folds, columns), w_out)


def wide_row_scan(x, columns, folds, gain, w_u, w_bc, rate, skip):
    parts, block, width = x.shape
    items = block // columns
    inner = w_u.shape[1]
    state = rate.shape[0]
    normed = normalise(x.reshape(parts, items, columns, width), gain)
    normed = normed.transpose(0, 2, 1, 3).reshape(parts * columns, items, width)
    value = dot(normed, w_u).astype(BF16).astype(F32)
    mix = dot(normed, w_bc).astype(BF16).astype(F32)
    factor = jnp.exp(-rate)

    def advance(held, now):
        value_now, inject, readout = now
        held = factor * held + inject[:, :, None] * value_now[:, None, :]
        return held, jnp.sum(held * readout[:, :, None], axis=1) + skip * value_now

    start = jnp.zeros((items, state, inner), F32)
    _, out = lax.scan(advance, start, (value, mix[..., :state], mix[..., state:2 * state]))
    out = out.astype(BF16).reshape(parts, columns, items, folds, inner // folds)
    return out.transpose(0, 2, 3, 1, 4).reshape(parts, folds * block, inner // folds)


def per_device(tokens, norm_gain, w_in, w_bc, rate_row, rate_col, skip_gain, w_out):
    height, columns, features = tokens.shape
    inner = w_out.shape[0]
    state = rate_row.shape[0]
    parts = lax.axis_size("rows")
    items = height // parts
    folds = 8 // columns
    steps_at_once = 16
    tokens = tokens.reshape(height * columns, features)
    moved = lax.all_to_all(
        tokens.reshape(parts, items * columns, features), "rows", split_axis=0, concat_axis=0, tiled=True
    )
    gate, mix = home(tokens, steps_at_once, columns, folds, norm_gain, w_in[:, inner:], w_bc[:, 2 * state:])
    scan = row_scan if items % 8 == 0 and parts * columns <= 64 else wide_row_scan
    row_mixed = scan(
        moved, columns, folds, norm_gain, w_in[:, :inner], w_bc[:, :2 * state], rate_row, skip_gain
    )
    back = lax.all_to_all(row_mixed, "rows", split_axis=0, concat_axis=0, tiled=True)
    back = back.reshape(height * folds * columns, inner // folds)
    rate = jnp.repeat(rate_col.reshape(state, folds, inner // folds), columns, axis=1)
    col, end = col_scan(back, mix, rate, steps_at_once)
    size, here = lax.axis_size("cols"), lax.axis_index("cols")
    incoming = jnp.zeros_like(end)
    for k in range(size - 1):
        if k == 0:
            carried = end
        else:
            carried = (jnp.exp(-rate * height) * incoming.astype(F32) + end.astype(F32)).astype(BF16)
        arrived = lax.ppermute(carried, "cols", [(k, k + 1)])
        incoming = arrived if k == 0 else jnp.where(here == k + 1, arrived, incoming)
    out = last(col, gate, mix, incoming, rate, w_out, folds, columns, steps_at_once)
    return out.reshape(height, columns, features)


def solution(mesh):
    placed = (P(("slides", "cols"), "rows", None), P(), P(), P(), P(), P(), P(), P())
    return jax.shard_map(
        per_device,
        mesh=mesh,
        in_specs=placed,
        out_specs=P(("slides", "cols"), "rows", None),
        check_vma=False,
    )
```

time: 234 us -> 88.9 us (0.38)
  matrix products: 81.9 us -> 0 us
  other arithmetic: 51.2 us -> 0.01 us
  Pallas kernels: 0 us -> 34.6 us
  local copies, waits for them, and re-layouts: 27.4 us -> 7.63 us
  waiting for transfers between devices: 49.9 us -> 33.1 us
  blocking collectives: 3.85 us -> 0 us
  loops' own time: 3.01 us -> 0 us
  starting transfers between devices: 15.5 us -> 12.9 us
    dot_general x163 -> x0, matrix products: 81.9 us -> none  [the longest x160 75.8 us: one_block(): jnp.einsum('ine,in->ie', carried, read_now, precision=lax.Precision.HIGHEST)]
    pallas_call x0 -> x4, Pallas kernels: none -> 34.6 us  [the longest x1 12.2 us: col_scan(): pl.pallas_call(functools.partial(col_kernel, state), name='col_scan', gri...]
    all_to_all x3 -> x2, waiting for transfers between devices: 49.9 us -> 32.2 us  [the longest x1 20.8 us: per_device(): lax.all_to_all(row_mixed, 'rows', split_axis=0, concat_axis=0, tiled=True)]
    dynamic_update_slice x8 -> x0, other arithmetic: 13.9 us -> none  [correct(): return lax.dynamic_update_slice_in_dim(outputs, updated, first_row, 0)]
    convert_element_type x31 -> x0, other arithmetic: 11.3 us -> none  [the longest x10 9.74 us: one_block(): lax.dynamic_slice_in_dim(series, first_row, block_len, scan_axis)]
    dot_general x8 -> x0, other arithmetic: 10.4 us -> none  [correct(): jnp.einsum('lwn,lne,wne->lwe', read_part, powers, incoming, precision=lax...]
    add x10 -> x0, other arithmetic: 9.09 us -> none  [one_block(): decay_factor[None] * carried]
    dynamic_update_slice x10 -> x0, local copies, waits for them, and re-layouts: 7.58 us -> none  [one_block(): lax.dynamic_update_slice_in_dim(outputs, stacked, first_row, scan_axis)]
  transfers between devices with their start and end apart: 3 -> 3, of which waited for: 3 -> 3; matrix products, arithmetic and copies ran while one was open for 2% -> 4% of each run, Pallas kernels for 0% -> 3%
where the time goes in v1:
time: 88.9 us; the launch traced here: 88.5 us
  Pallas kernels  34.6 us (39%)
  waiting for transfers between devices  33.1 us (37%)
  starting transfers between devices  12.9 us (15%)
  local copies, waits for them, and re-layouts  7.63 us (9%)
    all_to_all x1, waiting for transfers between devices, per_device(): lax.all_to_all(row_mixed, 'rows', split_axis=0, concat_axis=0, tiled=True)  20.8 us
    pallas_call x1, Pallas kernels, col_scan(): pl.pallas_call(functools.partial(col_kernel, state), name='col_scan', gri...  12.2 us
    pallas_call x1, Pallas kernels, last(): pl.pallas_call(functools.partial(last_kernel, state, folds), name='last',...  11.4 us
    all_to_all x1, waiting for transfers between devices, per_device(): lax.all_to_all(tokens.reshape(parts, items * columns, features), 'rows',...  11.4 us
    pallas_call x1, Pallas kernels, row_scan(): pl.pallas_call(functools.partial(row_kernel, parts, items, columns), name...  7.86 us
    all_to_all x1, starting transfers between devices, per_device(): lax.all_to_all(tokens.reshape(parts, items * columns, features), 'rows',...  7.25 us
    all_to_all x1, starting transfers between devices, per_device(): lax.all_to_all(row_mixed, 'rows', split_axis=0, concat_axis=0, tiled=True)  4.38 us
    pallas_call x1, Pallas kernels, home(): pl.pallas_call(functools.partial(home_kernel, folds, columns), name='home...  3.08 us
  transfers between devices with their start and end apart: 3, of which 3 were waited for; matrix products, arithmetic and copies ran while one was open for 4% of the time, Pallas kernels for 3%

profile of v1, /device:TPU:0, one launch (start us, length us, event | category | flops | bytes accessed | tf_op | source)
XLA Modules:
  0.0 88.5 jit_solution(3937872297932531235)
XLA Ops:
  0.0 2.0 %reshape_reshape.3 = bf16[8,64,512]{2,1,0:T(8,128)(2,1)} reshape(bf16[128,4,512]{2,1,0:T(4,128)(2,1)} %param.14) | data formatting | bytes 1048576 | tf_op jit(solution)/shard_map/reshape;reshape | solution.py:374
  2.0 7.3 %all-to-all-start = ((bf16[8,64,512]{2,1,0:T(8,128)(2,1)}), bf16[8,64,512]{2,1,0:T(8,128)(2,1)S(1)}, u32[]{:S(2)}, u32[]{:S(2)}) async-start(bf16[8,64,512]{2,1,0:T(8,128)(2,1)} %reshape_reshape.3), calls=%async_computation | async-start | bytes 1048576 | tf_op jit(solution)/shard_map/all_to_all | solution.py:373
  9.2 0.0 copy-done.11
  9.3 0.1 copy.20.wb_ref
  9.4 0.1 copy.21.wc_ref
  9.5 0.0 copy-start.4
  9.6 0.0 copy-start.5
  9.6 0.0 copy-start.6
  9.6 0.0 copy-start.8
  9.6 0.0 copy-start.9
  9.6 2.7 %fusion = (bf16[512,1024]{1,0:T(8,128)(2,1)}, bf16[512,1024]{1,0:T(8,128)(2,1)S(1)}) fusion(bf16[512,2048]{1,0:T(8,128)(2,1)} %param.16), kind=kLoop, calls=%fused_computation.2 | loop fusion | bytes 4194304 | tf_op jit(solution)/shard_map/slice | solution.py:376
  12.3 11.4 %all-to-all-done.x_ref = bf16[8,64,512]{2,1,0:T(8,128)(2,1)S(1)} async-done(((bf16[8,64,512]{2,1,0:T(8,128)(2,1)}), bf16[8,64,512]{2,1,0:T(8,128)(2,1)S(1)}, u32[]{:S(2)}, u32[]{:S(2)}) %all-to-all-start) | async-done | bytes 524320 | tf_op jit(solution)/shard_map/all_to_all | solution.py:373
  23.7 0.0 copy-done.4
  23.7 0.0 copy-done.5
  23.7 0.0 copy-done.6
  23.8 7.9 %row_scan.1 = bf16[8,128,512]{2,1,0:T(8,128)(2,1)} custom-call(bf16[8,64,512]{2,1,0:T(8,128)(2,1)S(1)} %all-to-all-done.x_ref, f32[1,512]{1,0:T(1,128)S(1)} %bitcast.4, bf16[512,1024]{1,0:T(8,128)(2,1)S(1)} %get-tuple-element.14.wu_ref, bf16[512,32]{1,0:T(8,128)(2,1)S(1)} %copy.20.wb_ref, bf16[512,32]{1,0:T(8,128)(2,1)S(1)} %copy.21.wc_ref, ...), custom_call_target="tpu_custom_call" | custom-call | flops 8589934592 | bytes 4194304 | tf_op jit(solution)/shard_map/row_scan/pallas_call | solution.py:133
  31.6 4.4 %all-to-all-start.1 = ((bf16[8,128,512]{2,1,0:T(8,128)(2,1)}), bf16[8,128,512]{2,1,0:T(8,128)(2,1)}, u32[]{:S(2)}, u32[]{:S(2)}) async-start(bf16[8,128,512]{2,1,0:T(8,128)(2,1)} %row_scan.1), calls=%async_computation.1 | async-start | bytes 2097152 | tf_op jit(solution)/shard_map/all_to_all | solution.py:381
  36.0 0.1 reshape.16.x_ref
  36.2 0.1 reshape.17
  36.2 0.1 copy.23.wm_ref
  36.4 0.1 broadcast_in_dim.12
  36.5 0.1 reshape.18.rate_ref
  36.6 1.2 %copy-done.1 = bf16[512,1024]{1,0:T(8,128)(2,1)S(1)} copy-done((bf16[512,1024]{1,0:T(8,128)(2,1)S(1)}, bf16[512,1024]{1,0:T(8,128)(2,1)}, u32[]{:S(2)}) %copy-start.1) | copy-done | bytes 1048600
  37.8 3.1 %home.1 = (f32[1024,512]{1,0:T(8,128)S(1)}, bf16[1024,32]{1,0:T(8,128)(2,1)S(1)}) custom-call(bf16[512,512]{1,0:T(8,128)(2,1)S(1)} %reshape.16.x_ref, f32[1,512]{1,0:T(1,128)S(1)} %bitcast.5, bf16[512,1024]{1,0:T(8,128)(2,1)S(1)} %copy-done.1, bf16[512,32]{1,0:T(8,128)(2,1)S(1)} %copy.23.wm_ref, bf16[128,64]{1,0:T(8,128)(2,1)S(1)} %copy-done.7), custom_call_target="tpu_custom_call" | custom-call | flops 1073741824 | bytes 4194304 | tf_op jit(solution)/shard_map/home/pallas_call | solution.py:175
  40.9 0.0 copy-start.3
  40.9 20.8 %all-to-all-done.1 = bf16[8,128,512]{2,1,0:T(8,128)(2,1)} async-done(((bf16[8,128,512]{2,1,0:T(8,128)(2,1)}), bf16[8,128,512]{2,1,0:T(8,128)(2,1)}, u32[]{:S(2)}, u32[]{:S(2)}) %all-to-all-start.1) | async-done | bytes 1048608 | tf_op jit(solution)/shard_map/all_to_all | solution.py:381
  61.7 12.2 %col_scan.1 = (f32[1024,512]{1,0:T(8,128)S(1)}, bf16[16,8,512]{2,1,0:T(8,128)(2,1)S(1)}) custom-call(bf16[1024,512]{1,0:T(8,128)(2,1)} %bitcast.2.y_ref, bf16[1024,32]{1,0:T(8,128)(2,1)S(1)} %get-tuple-element.9.mix_ref, f32[16,8,512]{2,1,0:T(8,128)S(1)} %reshape.18.rate_ref, bf16[16,2048]{1,0:T(8,128)(2,1)S(1)} %copy-done.2), custom_call_target="tpu_custom_call" | custom-call | flops 838860800 | bytes 8388608 | tf_op jit(solution)/shard_map/col_scan/pallas_call | solution.py:238
  73.9 1.3 %collective-permute-start = (bf16[16,8,512]{2,1,0:T(8,128)(2,1)S(1)}, bf16[16,8,512]{2,1,0:T(8,128)(2,1)S(1)}, u32[]{:S(2)}, u32[]{:S(2)}) collective-permute-start(bf16[16,8,512]{2,1,0:T(8,128)(2,1)S(1)} %get-tuple-element.12), channel_id=1, source_target_pairs={{0,1},{2,3},{4,5},{6,7},{8,9},{10,11},{12,13},{14,15},{16,17},{18,... | collective-permute-start | bytes 393224 | tf_op jit(solution)/shard_map/ppermute | solution.py:392
  75.2 1.0 %collective-permute-done.in_ref = bf16[16,8,512]{2,1,0:T(8,128)(2,1)S(1)} collective-permute-done((bf16[16,8,512]{2,1,0:T(8,128)(2,1)S(1)}, bf16[16,8,512]{2,1,0:T(8,128)(2,1)S(1)}, u32[]{:S(2)}, u32[]{:S(2)}) %collective-permute-start) | collective-permute-done | bytes 131104 | tf_op jit(solution)/shard_map/ppermute | solution.py:392
  76.2 0.0 copy-done.3
  76.2 11.4 %last.1 = bf16[512,512]{1,0:T(8,128)(2,1)S(1)} custom-call(f32[1024,512]{1,0:T(8,128)S(1)} %get-tuple-element.10.y_ref, f32[1024,512]{1,0:T(8,128)S(1)} %get-tuple-element.11.gate_ref, bf16[1024,32]{1,0:T(8,128)(2,1)S(1)} %get-tuple-element.9.mix_ref, bf16[16,8,512]{2,1,0:T(8,128)(2,1)S(1)} %collective-permute-done.in_ref, ...), custom_call_target="tpu_custom_call" | custom-call | flops 503316480 | bytes 8388608 | tf_op jit(solution)/shard_map/last/pallas_call | solution.py:315
  87.6 0.9 %reshape.19 = bf16[128,4,512]{2,1,0:T(4,128)(2,1)} reshape(bf16[512,512]{1,0:T(8,128)(2,1)S(1)} %last.1) | data formatting | bytes 1048576 | tf_op jit(solution)/shard_map/reshape | solution.py:395
  (18 shorter events, 0.0 us)
Async XLA Ops:
  0.0 9.2 %copy-start.11 = (bf16[512,64]{0,1:T(8,128)(2,1)S(1)}, bf16[512,64]{0,1:T(8,128)(2,1)}, u32[]{:S(2)}) copy-start(bf16[512,64]{0,1:T(8,128)(2,1)} %param.17) | copy-start | bytes 196612
  2.0 21.7 %all-to-all-start = ((bf16[8,64,512]{2,1,0:T(8,128)(2,1)}), bf16[8,64,512]{2,1,0:T(8,128)(2,1)S(1)}, u32[]{:S(2)}, u32[]{:S(2)}) async-start(bf16[8,64,512]{2,1,0:T(8,128)(2,1)} %reshape_reshape.3), calls=%async_computation | async-start | bytes 1048576 | tf_op jit(solution)/shard_map/all_to_all | solution.py:373
  9.5 14.2 %copy-start.4 = (f32[16,1024]{1,0:T(8,128)S(1)}, f32[16,1024]{1,0:T(8,128)}, u32[]{:S(2)}) copy-start(f32[16,1024]{1,0:T(8,128)} %rate_ref.1) | copy-start | bytes 196612
  9.6 14.2 %copy-start.5 = (f32[1024]{0:T(1024)S(1)}, f32[1024]{0:T(1024)}, u32[]{:S(2)}) copy-start(f32[1024]{0:T(1024)} %param.20) | copy-start | bytes 12292
  9.6 14.2 %copy-start.6 = (f32[512]{0:T(512)S(1)}, f32[512]{0:T(512)}, u32[]{:S(2)}) copy-start(f32[512]{0:T(512)} %param.15) | copy-start | bytes 6148
  9.6 14.2 %copy-start.8 = (bf16[128,128]{1,0:T(8,128)(2,1)S(1)}, bf16[128,128]{1,0:T(8,128)(2,1)}, u32[]{:S(2)}) copy-start(bf16[128,128]{1,0:T(8,128)(2,1)} %constant.12.clone.spread_ref) | copy-start | bytes 98308
  9.6 14.2 %copy-start.9 = (bf16[64,64]{1,0:T(8,128)(2,1)S(1)}, bf16[64,64]{1,0:T(8,128)(2,1)}, u32[]{:S(2)}) copy-start(bf16[64,64]{1,0:T(8,128)(2,1)} %constant.11.clone.order_ref) | copy-start | bytes 24580
  31.6 4.4 %copy-start.10 = (bf16[128,4,512]{2,1,0:T(4,128)(2,1)S(1)}, bf16[128,4,512]{2,1,0:T(4,128)(2,1)}, u32[]{:S(2)}) copy-start(bf16[128,4,512]{2,1,0:T(4,128)(2,1)} %param.14) | copy-start | bytes 1572868
  31.6 4.5 %copy-start.12 = (f32[16,1024]{1,0:T(8,128)S(1)}, f32[16,1024]{1,0:T(8,128)}, u32[]{:S(2)}) copy-start(f32[16,1024]{1,0:T(8,128)} %param.19) | copy-start | bytes 196612
  31.6 4.6 %slice-start = ((bf16[512,64]{0,1:T(8,128)(2,1)}), bf16[512,32]{0,1:T(8,128)(2,1)S(1)}, s32[]{:S(2)}) async-start(bf16[512,64]{0,1:T(8,128)(2,1)} %param.17), calls=%async_computation.2 | async-start | bytes 65536 | tf_op jit(solution)/shard_map/slice | solution.py:376
  31.6 4.9 %copy-start.7 = (bf16[128,64]{1,0:T(8,128)(2,1)S(1)}, bf16[128,64]{1,0:T(8,128)(2,1)}, u32[]{:S(2)}) copy-start(bf16[128,64]{1,0:T(8,128)(2,1)} %constant.10.clone.repeat_ref) | copy-start | bytes 49156
  31.6 30.0 %all-to-all-start.1 = ((bf16[8,128,512]{2,1,0:T(8,128)(2,1)}), bf16[8,128,512]{2,1,0:T(8,128)(2,1)}, u32[]{:S(2)}, u32[]{:S(2)}) async-start(bf16[8,128,512]{2,1,0:T(8,128)(2,1)} %row_scan.1), calls=%async_computation.1 | async-start | bytes 2097152 | tf_op jit(solution)/shard_map/all_to_all | solution.py:381
  36.6 1.2 %copy-start.1 = (bf16[512,1024]{1,0:T(8,128)(2,1)S(1)}, bf16[512,1024]{1,0:T(8,128)(2,1)}, u32[]{:S(2)}) copy-start(bf16[512,1024]{1,0:T(8,128)(2,1)} %get-tuple-element.13.wz_ref) | copy-start | bytes 3145732
  37.8 23.9 %copy-start.2 = (bf16[16,2048]{1,0:T(8,128)(2,1)S(1)}, bf16[16,2048]{1,0:T(8,128)(2,1)}, u32[]{:S(2)}) copy-start(bf16[16,2048]{1,0:T(8,128)(2,1)} %constant.13.clone.table_ref) | copy-start | bytes 196612
  40.9 35.3 %copy-start.3 = (bf16[128,128]{1,0:T(8,128)(2,1)S(1)}, bf16[128,128]{1,0:T(8,128)(2,1)}, u32[]{:S(2)}) copy-start(bf16[128,128]{1,0:T(8,128)(2,1)} %constant.14.clone.order_ref) | copy-start | bytes 98308
  61.7 14.5 %copy-start = (bf16[1024,512]{1,0:T(8,128)(2,1)S(1)}, bf16[1024,512]{1,0:T(8,128)(2,1)}, u32[]{:S(2)}) copy-start(bf16[1024,512]{1,0:T(8,128)(2,1)} %w_ref.1) | copy-start | bytes 3145732
  73.9 2.3 %collective-permute-start = (bf16[16,8,512]{2,1,0:T(8,128)(2,1)S(1)}, bf16[16,8,512]{2,1,0:T(8,128)(2,1)S(1)}, u32[]{:S(2)}, u32[]{:S(2)}) collective-permute-start(bf16[16,8,512]{2,1,0:T(8,128)(2,1)S(1)} %get-tuple-element.12), channel_id=1, source_target_pairs={{0,1},{2,3},{4,5},{6,7},{8,9},{10,11},{12,13},{14,15},{16,17},{18,... | collective-permute-start | bytes 393224 | tf_op jit(solution)/shard_map/ppermute | solution.py:392

commit v2 on v1

v2 whole, which is shorter than its diff:
```python
import functools

import jax
import jax.numpy as jnp
import numpy as np
from jax import lax
from jax.experimental import pallas as pl
from jax.experimental.pallas import tpu as pltpu
from jax.sharding import PartitionSpec as P

F32 = jnp.float32
BF16 = jnp.bfloat16
VMEM = pl.BlockSpec(memory_space=pltpu.VMEM)
LANES = 128


def normalise(tokens, gain):
    as_float = tokens.astype(F32)
    scale_now = lax.rsqrt(jnp.mean(as_float * as_float, axis=-1, keepdims=True) + 1e-05)
    return (as_float * scale_now * gain).astype(BF16)


def dot(a, b):
    return jnp.dot(a, b, preferred_element_type=F32)


def params():
    return pltpu.CompilerParams(vmem_limit_bytes=40 << 20)


def selection(shape, sources):
    matrix = np.zeros(shape, np.float32)
    matrix[np.arange(shape[0]), sources] = 1.0
    return jnp.asarray(matrix, BF16)


def row_order(items, columns):
    c, i = np.divmod(np.arange(items * columns), items)
    return selection((items * columns,) * 2, i * columns + c)


def spread_order(items, folds, columns):
    i, rest = np.divmod(np.arange(items * folds * columns), folds * columns)
    return selection((items * folds * columns,) * 2, rest * items + i)


def repeat_order(items, folds, columns):
    i, rest = np.divmod(np.arange(items * folds * columns), folds * columns)
    return selection((items * folds * columns, items * columns), i * columns + rest % columns)


def gather_order(items, folds, columns):
    f, rest = np.divmod(np.arange(items * folds * columns), items * columns)
    i, c = np.divmod(rest, columns)
    return selection((items * folds * columns,) * 2, (i * folds + f) * columns + c)


def lane_table(state):
    return jnp.asarray(np.repeat(np.eye(state, dtype=np.float32), LANES, axis=1), BF16)


def row_kernel(parts, items, columns, x_ref, gain_ref, wu_ref, wb_ref, wc_ref, rate_ref, skip_ref,
               order_ref, spread_ref, out_ref, normed, b_scr, c_scr, u_scr, y_scr, g_scr):
    block = items * columns
    steps = parts * columns
    rows = steps * items
    inner = u_scr.shape[1]
    folds = spread_ref.shape[0] // block
    gain = gain_ref[...]
    for part in range(parts):
        here = normalise(x_ref[part], gain)
        normed[part * block:(part + 1) * block, :] = dot(order_ref[...], here).astype(BF16)
    b_scr[...] = dot(normed[...], wb_ref[...]).astype(BF16).astype(F32)
    c_scr[...] = dot(normed[...], wc_ref[...]).astype(BF16).astype(F32)
    chunk = 128
    pieces = []
    at = 0
    for lag in range(steps):
        first = lag * items
        while first < rows:
            count = min(chunk, rows - first)
            pieces.append((lag, first, count, at))
            first += count
            at += count
    for lag, first, count, at in pieces:
        source = first - lag * items
        product = c_scr[first:first + count, :] * b_scr[source:source + count, :]
        g_scr[at:at + count, :] = product.astype(BF16)
    tile = 512

    def one_tile(tile_id, _):
        where = pl.ds(pl.multiple_of(tile_id * tile, tile), tile)
        u_scr[:, where] = dot(normed[...], wu_ref[:, where]).astype(BF16).astype(F32)
        rate = rate_ref[:, where]
        skip = skip_ref[:, where]
        done = -1
        table = None
        for lag, first, count, at in pieces:
            if lag != done:
                power = jnp.exp(rate * (-float(lag)))
                high = power.astype(BF16)
                low = (power - high.astype(F32)).astype(BF16)
                table = jnp.concatenate([high, low], axis=0)
                done = lag
            matrix = dot(g_scr[at:at + count, :], table)
            source = first - lag * items
            value = u_scr[source:source + count, where]
            if lag == 0:
                y_scr[first:first + count, where] = (matrix + skip) * value
            else:
                y_scr[first:first + count, where] += matrix * value
        return 0

    lax.fori_loop(0, inner // tile, one_tile, 0)
    width = out_ref.shape[2]
    halves = out_ref.shape[0] // parts
    for part in range(parts):
        here = slice(part * block, (part + 1) * block)
        for half in range(halves):
            first = half * folds * width
            stacked = jnp.concatenate(
                [y_scr[here, first + f * width:first + (f + 1) * width].astype(BF16) for f in range(folds)], axis=0
            )
            out_ref[part * halves + half] = dot(spread_ref[...], stacked).astype(BF16)


def row_scan(x, columns, folds, halves, gain, w_u, w_bc, rate, skip):
    parts, block, width = x.shape
    items = block // columns
    inner = w_u.shape[1]
    state = rate.shape[0]
    rows = parts * block
    w_b, w_c = w_bc[:, :state], w_bc[:, state:2 * state]
    w_b = jnp.concatenate([w_b, w_b], axis=1)
    w_c = jnp.concatenate([w_c, w_c], axis=1)
    return pl.pallas_call(
        functools.partial(row_kernel, parts, items, columns),
        name="row_scan",
        out_shape=jax.ShapeDtypeStruct((parts * halves, folds * block, inner // (halves * folds)), BF16),
        in_specs=[VMEM] * 9,
        out_specs=VMEM,
        scratch_shapes=[
            pltpu.VMEM((rows, width), BF16),
            pltpu.VMEM((rows, 2 * state), F32),
            pltpu.VMEM((rows, 2 * state), F32),
            pltpu.VMEM((rows, inner), F32),
            pltpu.VMEM((rows, inner), F32),
            pltpu.VMEM((rows * (parts * columns + 1) // 2, 2 * state), BF16),
        ],
        compiler_params=params(),
        cost_estimate=pl.CostEstimate(
            flops=2 * rows * width * inner * 16, bytes_accessed=4 << 20, transcendentals=0
        ),
    )(x, gain[None, :], w_u, w_b, w_c, rate, skip[None, :], row_order(items, columns),
      spread_order(items, folds, columns))


def home_kernel(folds, columns, x_ref, gain_ref, wz_ref, wm_ref, repeat_ref, gate_ref, mix_ref):
    block = repeat_ref.shape[1]
    tall = repeat_ref.shape[0]
    width = wz_ref.shape[1] // folds
    fold_of = (lax.broadcasted_iota(jnp.int32, (tall, 1), 0) % (folds * columns)) // columns
    for start in range(x_ref.shape[0] // block):
        here = normalise(x_ref[start * block:(start + 1) * block, :], gain_ref[...])
        here = dot(repeat_ref[...], here).astype(BF16)
        there = slice(start * tall, (start + 1) * tall)
        project = dot(here, wz_ref[...])
        gate = project[:, :width]
        for fold in range(1, folds):
            gate = jnp.where(fold_of == fold, project[:, fold * width:(fold + 1) * width], gate)
        gate = gate.astype(BF16).astype(F32)
        gate_ref[there, :] = gate / (1.0 + jnp.exp(-gate))
        mix_ref[there, :] = dot(here, wm_ref[...]).astype(BF16)


def home(x, items, columns, folds, gain, w_z, w_m):
    rows = x.shape[0]
    return pl.pallas_call(
        functools.partial(home_kernel, folds, columns),
        name="home",
        out_shape=(
            jax.ShapeDtypeStruct((rows * folds, w_z.shape[1] // folds), F32),
            jax.ShapeDtypeStruct((rows * folds, w_m.shape[1]), BF16),
        ),
        in_specs=[VMEM] * 5,
        out_specs=(VMEM, VMEM),
        compiler_params=params(),
        cost_estimate=pl.CostEstimate(
            flops=4 * rows * x.shape[1] * w_z.shape[1], bytes_accessed=4 << 20, transcendentals=0
        ),
    )(x, gain[None, :], w_z, w_m, repeat_order(items, folds, columns))


def col_kernel(state, halves, core_ref, y_ref, gate_ref, mix_ref, next_ref, rate_ref, table_ref, *rest):
    outs, (held, decay, b0, c0, b1, c1, v_scr, g_scr) = rest[:halves], rest[halves:]
    block = b0.shape[0]
    steps = block // 8
    width = held.shape[2]
    tiles = width // LANES
    spans = [slice(k * LANES, (k + 1) * LANES) for k in range(tiles)]
    per_tile = 2 * LANES
    pieces = [(w, p) for p in range(state * LANES // per_tile) for w in range(2)]

    def spread(rows, which, piece, targets):
        there = slice(piece * per_tile, (piece + 1) * per_tile)
        targets[which][:, there] = dot(rows[:, which * state:(which + 1) * state], table_ref[:, there])

    @pl.when(pl.program_id(0) == 0)
    def _():
        held[...] = jnp.zeros_like(held)
        decay[...] = jnp.exp(-rate_ref[...])
        for which, piece in pieces:
            spread(mix_ref[0, :block, :], which, piece, (b0, c0))

    source_rows = y_ref.shape[2]
    for k in range(y_ref.shape[0]):
        v_scr[k * source_rows:(k + 1) * source_rows, :] = y_ref[k, 0].astype(F32)

    def scan(offset, b_scr, c_scr, ahead, targets):
        carry = [held[n, :, span] for n in range(state) for span in spans]
        done = 0
        for t in range(steps):
            while done < len(pieces) * (t + 1) // steps:
                spread(ahead, *pieces[done], targets)
                done += 1
            here = slice(t * 8, t * 8 + 8)
            rows = slice(offset + t * 8, offset + t * 8 + 8)
            value = [v_scr[rows, span] for span in spans]
            total = list(value)
            for n in range(state):
                b = b_scr[here, n * LANES:(n + 1) * LANES]
                c = c_scr[here, n * LANES:(n + 1) * LANES]
                for k, span in enumerate(spans):
                    h = decay[n, :, span] * carry[n * tiles + k] + b * value[k]
                    total[k] = total[k] + c * h
                    carry[n * tiles + k] = h
            for k, span in enumerate(spans):
                g_scr[rows, span] = total[k] * gate_ref[0, rows, span]
        for n in range(state):
            for k, span in enumerate(spans):
                held[n, :, span] = carry[n * tiles + k]

    scan(0, b0, c0, mix_ref[0, block:, :], (b1, c1))
    scan(block, b1, c1, next_ref[0, :block, :], (b0, c0))
    per_half = pl.num_programs(0) // halves
    slot = lax.rem(pl.program_id(0) // per_half + halves - core_ref[0], halves)
    for s in range(halves):
        @pl.when(slot == s)
        def _(s=s):
            outs[s][...] = g_scr[...].astype(BF16)


def col_scan(core, y, gate, mix, rate):
    sources, halves, source_rows, width = y.shape
    state = rate.shape[0]
    take = max(1, min(sources, 256 // source_rows))
    block = take * source_rows
    per_half = sources // take
    last_step = halves * per_half - 1

    def slot(i, core):
        return lax.rem(i // per_half + halves - core[0], halves)

    def out_map(s):
        def place(i, core):
            first = lax.rem(core[0] + s, halves) * per_half
            return (jnp.clip(i - first, 0, per_half - 1), 0)
        return place

    half_block = block // 2
    return pl.pallas_call(
        functools.partial(col_kernel, state, halves),
        name="col_scan",
        grid_spec=pltpu.PrefetchScalarGridSpec(
            num_scalar_prefetch=1,
            grid=(halves * per_half,),
            in_specs=[
                pl.BlockSpec((take, 1, source_rows, width), lambda i, core: (i % per_half, i // per_half, 0, 0)),
                pl.BlockSpec((1, block, width), lambda i, core: (slot(i, core), i % per_half, 0)),
                pl.BlockSpec((1, block, 2 * state), lambda i, core: (slot(i, core), i % per_half, 0)),
                pl.BlockSpec((1, block, 2 * state), lambda i, core: (
                    slot(jnp.minimum(i + 1, last_step), core), jnp.minimum(i + 1, last_step) % per_half, 0)),
                pl.BlockSpec(rate.shape, lambda i, core: (0, 0, 0)),
                pl.BlockSpec((state, state * LANES), lambda i, core: (0, 0)),
            ],
            out_specs=[pl.BlockSpec((block, width), out_map(s)) for s in range(halves)],
            scratch_shapes=[
                pltpu.VMEM(rate.shape, F32),
                pltpu.VMEM(rate.shape, F32),
                pltpu.VMEM((half_block, state * LANES), F32),
                pltpu.VMEM((half_block, state * LANES), F32),
                pltpu.VMEM((half_block, state * LANES), F32),
                pltpu.VMEM((half_block, state * LANES), F32),
                pltpu.VMEM((block, width), F32),
                pltpu.VMEM((block, width), F32),
            ],
        ),
        out_shape=[jax.ShapeDtypeStruct((per_half * block, width), BF16)] * halves,
        compiler_params=params(),
        cost_estimate=pl.CostEstimate(flops=5 * halves * per_half * block * width * state, bytes_accessed=8 << 20,
                                      transcendentals=0),
    )(core, y, gate, mix, mix, rate, lane_table(state))


def last_kernel(folds, halves, *refs):
    parts, (order_ref, w_ref, out_ref) = refs[:halves], refs[halves:]
    block = order_ref.shape[0]
    rows = block // folds
    width = parts[0].shape[1]
    for at in range(parts[0].shape[0] // block):
        here = slice(at * block, (at + 1) * block)
        gated = jnp.concatenate([part[here, :] for part in parts], axis=1)
        gated = dot(order_ref[...], gated).astype(BF16)
        total = dot(gated[:rows], w_ref[0])
        for fold in range(1, folds):
            total = total + dot(gated[fold * rows:(fold + 1) * rows], w_ref[fold])
        out_ref[at * rows:(at + 1) * rows, :] = total.astype(BF16)


def last(parts, w_out, items, folds, columns):
    rows = parts[0].shape[0] // folds
    features = w_out.shape[2]
    return pl.pallas_call(
        functools.partial(last_kernel, folds, len(parts)),
        name="last",
        out_shape=jax.ShapeDtypeStruct((rows, features), BF16),
        in_specs=[VMEM] * (len(parts) + 2),
        out_specs=VMEM,
        compiler_params=params(),
        cost_estimate=pl.CostEstimate(flops=2 * rows * w_out.size // folds, bytes_accessed=2 << 20, transcendentals=0),
    )(*parts, gather_order(items, folds, columns), w_out)


def wide_row_scan(x, columns, folds, halves, gain, w_u, w_bc, rate, skip):
    parts, block, width = x.shape
    items = block // columns
    inner = w_u.shape[1]
    state = rate.shape[0]
    normed = normalise(x.reshape(parts, items, columns, width), gain)
    normed = normed.transpose(0, 2, 1, 3).reshape(parts * columns, items, width)
    value = dot(normed, w_u).astype(BF16).astype(F32)
    mix = dot(normed, w_bc).astype(BF16).astype(F32)
    factor = jnp.exp(-rate)

    def advance(held, now):
        value_now, inject, readout = now
        held = factor * held + inject[:, :, None] * value_now[:, None, :]
        return held, jnp.sum(held * readout[:, :, None], axis=1) + skip * value_now

    start = jnp.zeros((items, state, inner), F32)
    _, out = lax.scan(advance, start, (value, mix[..., :state], mix[..., state:2 * state]))
    narrow = inner // (halves * folds)
    out = out.astype(BF16).reshape(parts, columns, items, halves, folds, narrow)
    return out.transpose(0, 3, 2, 4, 1, 5).reshape(parts * halves, folds * block, narrow)


def per_device(tokens, norm_gain, w_in, w_bc, rate_row, rate_col, skip_gain, w_out):
    height, columns, features = tokens.shape
    inner = w_out.shape[0]
    state = rate_row.shape[0]
    parts, halves = lax.axis_size("rows"), lax.axis_size("cols")
    core = lax.axis_index("cols")
    both = ("rows", "cols")
    sources = parts * halves
    items = height // sources
    folds = 8 // columns
    group = inner // halves
    width = group // folds
    tokens = tokens.reshape(height * columns, features)
    moved = lax.all_to_all(
        tokens.reshape(sources, items * columns, features), both, split_axis=0, concat_axis=0, tiled=True
    )
    scan = row_scan if items * halves % 8 == 0 and parts * columns <= 64 else wide_row_scan
    row_mixed = scan(
        moved.reshape(parts, halves * items * columns, features), columns, folds, halves, norm_gain,
        w_in[:, :inner], w_bc[:, :2 * state], rate_row, skip_gain
    )
    back = lax.all_to_all(row_mixed, both, split_axis=0, concat_axis=0, tiled=True)

    whole = [tokens] + [
        lax.ppermute(tokens, "cols", [(k, (k - s) % halves) for k in range(halves)]) for s in range(1, halves)
    ]
    own = core * group
    w_gate = lax.dynamic_slice_in_dim(w_in, inner + own, group, 1)
    pieces = [home(t, 16, columns, folds, norm_gain, w_gate, w_bc[:, 2 * state:]) for t in whole]
    gate = jnp.stack([piece[0] for piece in pieces])
    mix = jnp.stack([piece[1] for piece in pieces])
    rate = lax.dynamic_slice_in_dim(rate_col, own, group, 1)
    rate = jnp.repeat(rate.reshape(state, folds, width), columns, axis=1)
    back = back.reshape(sources, halves, items * folds * columns, width)
    if items * folds * columns % 16 != 0:
        blocks = max(1, height * folds * columns // 256)
        back = back.reshape(blocks, sources // blocks, halves, -1, width).transpose(0, 2, 1, 3, 4)
        back = back.reshape(blocks, halves, -1, width)
    gated = col_scan(core.reshape(1), back, gate, mix, rate)
    groups = [gated[0]] + [
        lax.ppermute(gated[s], "cols", [(k, (k + s) % halves) for k in range(halves)]) for s in range(1, halves)
    ]
    w_out = w_out.reshape(halves, folds, width, features)
    w_last = jnp.stack([w_out[(core - s) % halves] for s in range(halves)], axis=1)
    w_last = w_last.reshape(folds, halves * width, features)
    return last(groups, w_last, 16, folds, columns).reshape(height, columns, features)


def solution(mesh):
    placed = (P(("slides", "cols"), "rows", None), P(), P(), P(), P(), P(), P(), P())
    return jax.shard_map(
        per_device,
        mesh=mesh,
        in_specs=placed,
        out_specs=P(("slides", "cols"), "rows", None),
        check_vma=False,
    )
```

time: 88.9 us -> 77 us (0.87)
  the two profiles are of different devices: /device:TPU:0 before, /device:TPU:17 now
where the time goes in v2:
time: 77 us; the launch traced here: 76.6 us
  waiting for transfers between devices  30.1 us (39%)
  Pallas kernels  25.3 us (33%)
  starting transfers between devices  13.4 us (17%)
  local copies, waits for them, and re-layouts  7.27 us (9%)
    all_to_all x1, waiting for transfers between devices, per_device(): lax.all_to_all(row_mixed, both, split_axis=0, concat_axis=0, tiled=True)  18.1 us
    all_to_all x1, waiting for transfers between devices, per_device(): lax.all_to_all(tokens.reshape(sources, items * columns, features), both,...  11.6 us
    pallas_call x1, Pallas kernels, col_scan(): pl.pallas_call(functools.partial(col_kernel, state, halves), name='col_sc...  10.5 us
    pallas_call x1, Pallas kernels, row_scan(): pl.pallas_call(functools.partial(row_kernel, parts, items, columns), name...  7.84 us
    all_to_all x1, starting transfers between devices, per_device(): lax.all_to_all(tokens.reshape(sources, items * columns, features), both,...  6.47 us
    all_to_all x1, starting transfers between devices, per_device(): lax.all_to_all(row_mixed, both, split_axis=0, concat_axis=0, tiled=True)  5.63 us
    pallas_call x2, Pallas kernels, home(): pl.pallas_call(functools.partial(home_kernel, folds, columns), name='home...  4.41 us
    pallas_call x1, Pallas kernels, last(): pl.pallas_call(functools.partial(last_kernel, folds, len(parts)), name='l...  2.55 us
  transfers between devices with their start and end apart: 4, of which 3 were waited for; matrix products, arithmetic and copies ran while one was open for 6% of the time, Pallas kernels for 6%

profile of v2, /device:TPU:17, one launch (start us, length us, event | category | flops | bytes accessed | tf_op | source)
XLA Modules:
  0.0 76.6 jit_solution(13603169363895148130)
XLA Ops:
  0.0 0.0 copy-start
  0.0 0.0 copy-start.10
  0.0 0.0 copy-start.5
  0.1 2.0 %reshape_reshape.3 = bf16[16,32,512]{2,1,0:T(8,128)(2,1)} reshape(bf16[128,4,512]{2,1,0:T(4,128)(2,1)} %param.14) | data formatting | bytes 1048576 | tf_op jit(solution)/shard_map/reshape;reshape | solution.py:371
  2.1 6.5 %all-to-all-start = ((bf16[16,32,512]{2,1,0:T(8,128)(2,1)}), bf16[16,32,512]{2,1,0:T(8,128)(2,1)S(1)}, u32[]{:S(2)}, u32[]{:S(2)}) async-start(bf16[16,32,512]{2,1,0:T(8,128)(2,1)} %reshape_reshape.3), calls=%async_computation | async-start | bytes 1048576 | tf_op jit(solution)/shard_map/all_to_all | solution.py:370
  8.6 0.0 copy-done.10
  8.6 0.1 copy.27.wb_ref
  8.7 0.1 copy.28.wc_ref
  8.9 1.3 %slice.16.wu_ref = bf16[512,1024]{1,0:T(8,128)(2,1)S(1)} slice(bf16[512,2048]{1,0:T(8,128)(2,1)} %param.16), slice={[0:512], [0:1024]} | slice | bytes 2097152 | tf_op jit(solution)/shard_map/slice | solution.py:376
  10.2 11.6 %all-to-all-done = bf16[16,32,512]{2,1,0:T(8,128)(2,1)S(1)} async-done(((bf16[16,32,512]{2,1,0:T(8,128)(2,1)}), bf16[16,32,512]{2,1,0:T(8,128)(2,1)S(1)}, u32[]{:S(2)}, u32[]{:S(2)}) %all-to-all-start) | async-done | bytes 524320 | tf_op jit(solution)/shard_map/all_to_all | solution.py:370
  21.8 7.8 %row_scan.1 = bf16[16,128,256]{2,1,0:T(8,128)(2,1)} custom-call(bf16[8,64,512]{2,1,0:T(8,128)(2,1)S(1)} %bitcast.18, f32[1,512]{1,0:T(1,128)S(1)} %bitcast.22, bf16[512,1024]{1,0:T(8,128)(2,1)S(1)} %slice.16.wu_ref, bf16[512,32]{1,0:T(8,128)(2,1)S(1)} %copy.27.wb_ref, bf16[512,32]{1,0:T(8,128)(2,1)S(1)} %copy.28.wc_ref, f32[16,1024]{1,0:T(8,128)S(1)} %copy-done.3, ...), custom_call_target="tpu_custom_call" | custom-call | flops 8589934592 | bytes 4194304 | tf_op jit(solution)/shard_map/row_scan/pallas_call | solution.py:136
  29.6 5.6 %all-to-all-start.1 = ((bf16[16,128,256]{2,1,0:T(8,128)(2,1)}), bf16[16,128,256]{2,1,0:T(8,128)(2,1)}, u32[]{:S(2)}, u32[]{:S(2)}) async-start(bf16[16,128,256]{2,1,0:T(8,128)(2,1)} %row_scan.1), calls=%async_computation.1 | async-start | bytes 2097152 | tf_op jit(solution)/shard_map/all_to_all | solution.py:378
  35.3 0.1 reshape.30.x_ref
  35.4 0.4 collective-permute-start
  35.8 0.1 copy.30.wm_ref
  35.9 0.0 copy-done
  36.1 1.1 %constant_dynamic-slice_fusion.1.wz_ref = bf16[512,512]{1,0:T(8,128)(2,1)S(1)} fusion(bf16[512,2048]{1,0:T(8,128)(2,1)} %param.16, s32[]{:T(128)S(6)} %select_n.23), kind=kLoop, calls=%fused_computation.8 | loop fusion | bytes 1048580 | tf_op jit(solution)/shard_map/dynamic_slice | solution.py:384
  37.2 0.0 copy-done.6
  37.2 2.2 %home.2 = (f32[1024,256]{1,0:T(8,128)S(1)}, bf16[1024,32]{1,0:T(8,128)(2,1)S(1)}) custom-call(bf16[512,512]{1,0:T(8,128)(2,1)S(1)} %reshape.30.x_ref, f32[1,512]{1,0:T(1,128)S(1)} %bitcast.23, bf16[512,512]{1,0:T(8,128)(2,1)S(1)} %constant_dynamic-slice_fusion.1.wz_ref, bf16[512,32]{1,0:T(8,128)(2,1)S(1)} %copy.30.wm_ref, bf16[128,64]{1,0:T(8,128)(2,1)S(1)} %copy-done.6), custom_call_target="tpu_custom_call" | custom-call | flops 536870912 | bytes 4194304 | tf_op jit(solution)/shard_map/home/pallas_call | solution.py:178
  39.4 0.0 collective-permute-done.x_ref
  39.4 2.2 %home.3 = (f32[1024,256]{1,0:T(8,128)S(1)}, bf16[1024,32]{1,0:T(8,128)(2,1)S(1)}) custom-call(bf16[512,512]{1,0:T(8,128)(2,1)S(1)} %collective-permute-done.x_ref, f32[1,512]{1,0:T(1,128)S(1)} %bitcast.24, bf16[512,512]{1,0:T(8,128)(2,1)S(1)} %constant_dynamic-slice_fusion.1.wz_ref, bf16[512,32]{1,0:T(8,128)(2,1)S(1)} %copy.30.wm_ref, ...), custom_call_target="tpu_custom_call" | custom-call | flops 536870912 | bytes 4194304 | tf_op jit(solution)/shard_map/home/pallas_call | solution.py:178
  41.6 0.1 pad_maximum_fusion.2.mix_ref.next_ref
  41.7 0.0 copy-start.1
  41.8 0.1 pad_maximum_fusion.gate_ref
  41.9 18.1 %all-to-all-done.1 = bf16[16,128,256]{2,1,0:T(8,128)(2,1)} async-done(((bf16[16,128,256]{2,1,0:T(8,128)(2,1)}), bf16[16,128,256]{2,1,0:T(8,128)(2,1)}, u32[]{:S(2)}, u32[]{:S(2)}) %all-to-all-start.1) | async-done | bytes 1048608 | tf_op jit(solution)/shard_map/all_to_all | solution.py:378
  60.0 10.5 %col_scan.1 = (bf16[1024,256]{1,0:T(8,128)(2,1)S(1)}, bf16[1024,256]{1,0:T(8,128)(2,1)}) custom-call(s32[1]{0:T(128)} %bitcast.core_ref, bf16[16,2,64,256]{3,2,1,0:T(8,128)(2,1)} %bitcast.4.y_ref, f32[2,1024,256]{2,1,0:T(8,128)S(1)} %pad_maximum_fusion.gate_ref, bf16[2,1024,32]{2,1,0:T(8,128)(2,1)S(1)} %pad_maximum_fusion.2.mix_ref.next_ref, ...), custom_call_target="tpu_custom_call" | custom-call | flops 41943040 | bytes 8388608 | tf_op jit(solution)/shard_map/col_scan/pallas_call | solution.py:271
  70.5 0.9 %collective-permute-start.1 = (bf16[1024,256]{1,0:T(8,128)(2,1)}, bf16[1024,256]{1,0:T(8,128)(2,1)S(1)}, u32[]{:S(2)}, u32[]{:S(2)}) collective-permute-start(bf16[1024,256]{1,0:T(8,128)(2,1)} %get-tuple-element.16), channel_id=1, source_target_pairs={{0,1},{1,0},{2,3},{3,2},{4,5},{5,4},{6,7},{7,6},{8,9},{9,8},{10,11... | collective-permute-start | bytes 1572872 | tf_op jit(solution)/shard_map/ppermute | solution.py:397
  71.4 1.3 %dynamic-slice_bitcast_fusion.1 = (bf16[2,1,256,512]{3,2,1,0:T(8,128)(2,1)S(1)}, bf16[2,1,256,512]{3,2,1,0:T(8,128)(2,1)S(1)}) fusion(bf16[2,2,256,512]{3,2,1,0:T(8,128)(2,1)} %bitcast.25, s32[]{:T(128)S(6)} %select_n.26, s32[]{:T(128)S(6)} %select_n.28), kind=kLoop, calls=%fused_computation.4 | loop fusion | bytes 2097160 | tf_op jit(solution)/shard_map/stack;squeeze | solution.py:400
  72.6 0.1 pad_maximum_fusion.1
  72.7 0.4 collective-permute-done.1.refs_1_
  73.1 2.5 %last.1 = bf16[512,512]{1,0:T(8,128)(2,1)S(1)} custom-call(bf16[1024,256]{1,0:T(8,128)(2,1)S(1)} %get-tuple-element.15.refs_0_, bf16[1024,256]{1,0:T(8,128)(2,1)S(1)} %collective-permute-done.1.refs_1_, bf16[128,128]{1,0:T(8,128)(2,1)S(1)} %copy-done.2, bf16[2,512,512]{2,1,0:T(8,128)(2,1)S(1)} %bitcast.15), custom_call_target="tpu_custom_call" | custom-call | flops 268435456 | bytes 2097152 | tf_op jit(solution)/shard_map/last/pallas_call | solution.py:323
  75.7 0.9 %reshape.35 = bf16[128,4,512]{2,1,0:T(4,128)(2,1)} reshape(bf16[512,512]{1,0:T(8,128)(2,1)S(1)} %last.1) | data formatting | bytes 1048576 | tf_op jit(solution)/shard_map/reshape | solution.py:402
  (23 shorter events, 0.2 us)
Async XLA Ops:
  0.0 35.9 %copy-start = (f32[16,1024]{1,0:T(8,128)S(1)}, f32[16,1024]{1,0:T(8,128)}, u32[]{:S(2)}) copy-start(f32[16,1024]{1,0:T(8,128)} %param.19) | copy-start | bytes 196612
  0.0 21.8 %copy-start.7 = (bf16[128,128]{1,0:T(8,128)(2,1)S(1)}, bf16[128,128]{1,0:T(8,128)(2,1)}, u32[]{:S(2)}) copy-start(bf16[128,128]{1,0:T(8,128)(2,1)} %constant.43.clone.spread_ref) | copy-start | bytes 98308
  0.0 21.8 %copy-start.8 = (bf16[64,64]{1,0:T(8,128)(2,1)S(1)}, bf16[64,64]{1,0:T(8,128)(2,1)}, u32[]{:S(2)}) copy-start(bf16[64,64]{1,0:T(8,128)(2,1)} %constant.42.clone.order_ref) | copy-start | bytes 24580
  0.0 8.6 %copy-start.10 = (bf16[512,64]{0,1:T(8,128)(2,1)S(1)}, bf16[512,64]{0,1:T(8,128)(2,1)}, u32[]{:S(2)}) copy-start(bf16[512,64]{0,1:T(8,128)(2,1)} %param.17) | copy-start | bytes 196612
  0.0 21.7 %copy-start.5 = (f32[512]{0:T(512)S(1)}, f32[512]{0:T(512)}, u32[]{:S(2)}) copy-start(f32[512]{0:T(512)} %param.15) | copy-start | bytes 6148
  0.0 21.7 %copy-start.4 = (f32[1024]{0:T(1024)S(1)}, f32[1024]{0:T(1024)}, u32[]{:S(2)}) copy-start(f32[1024]{0:T(1024)} %param.20) | copy-start | bytes 12292
  0.0 21.7 %copy-start.3 = (f32[16,1024]{1,0:T(8,128)S(1)}, f32[16,1024]{1,0:T(8,128)}, u32[]{:S(2)}) copy-start(f32[16,1024]{1,0:T(8,128)} %rate_ref.1) | copy-start | bytes 196612
  2.1 19.7 %all-to-all-start = ((bf16[16,32,512]{2,1,0:T(8,128)(2,1)}), bf16[16,32,512]{2,1,0:T(8,128)(2,1)S(1)}, u32[]{:S(2)}, u32[]{:S(2)}) async-start(bf16[16,32,512]{2,1,0:T(8,128)(2,1)} %reshape_reshape.3), calls=%async_computation | async-start | bytes 1048576 | tf_op jit(solution)/shard_map/all_to_all | solution.py:370
  29.6 5.6 %copy-start.9 = (bf16[128,4,512]{2,1,0:T(4,128)(2,1)S(1)}, bf16[128,4,512]{2,1,0:T(4,128)(2,1)}, u32[]{:S(2)}) copy-start(bf16[128,4,512]{2,1,0:T(4,128)(2,1)} %param.14) | copy-start | bytes 1572868
  29.6 6.2 %slice-start = ((bf16[512,64]{0,1:T(8,128)(2,1)}), bf16[512,32]{0,1:T(8,128)(2,1)S(1)}, s32[]{:S(2)}) async-start(bf16[512,64]{0,1:T(8,128)(2,1)} %param.17), calls=%async_computation.2 | async-start | bytes 65536 | tf_op jit(solution)/shard_map/slice | solution.py:385
  29.6 7.6 %copy-start.6 = (bf16[128,64]{1,0:T(8,128)(2,1)S(1)}, bf16[128,64]{1,0:T(8,128)(2,1)}, u32[]{:S(2)}) copy-start(bf16[128,64]{1,0:T(8,128)(2,1)} %constant.44.clone.repeat_ref) | copy-start | bytes 49156
  29.6 30.4 %all-to-all-start.1 = ((bf16[16,128,256]{2,1,0:T(8,128)(2,1)}), bf16[16,128,256]{2,1,0:T(8,128)(2,1)}, u32[]{:S(2)}, u32[]{:S(2)}) async-start(bf16[16,128,256]{2,1,0:T(8,128)(2,1)} %row_scan.1), calls=%async_computation.1 | async-start | bytes 2097152 | tf_op jit(solution)/shard_map/all_to_all | solution.py:378
  35.4 4.0 %collective-permute-start = (bf16[512,512]{1,0:T(8,128)(2,1)S(1)}, bf16[512,512]{1,0:T(8,128)(2,1)S(1)}, u32[]{:S(2)}, u32[]{:S(2)}) collective-permute-start(bf16[512,512]{1,0:T(8,128)(2,1)S(1)} %reshape.30.x_ref), channel_id=1, source_target_pairs={{0,1},{1,0},{2,3},{3,2},{4,5},{5,4},{6,7},{7,6},{8,9},{9,8},{10,11... | collective-permute-start | bytes 1572872 | tf_op jit(solution)/shard_map/ppermute | solution.py:381
  41.7 18.3 %copy-start.1 = (bf16[16,2048]{1,0:T(8,128)(2,1)S(1)}, bf16[16,2048]{1,0:T(8,128)(2,1)}, u32[]{:S(2)}) copy-start(bf16[16,2048]{1,0:T(8,128)(2,1)} %constant.45.clone.table_ref) | copy-start | bytes 196612
  70.5 2.6 %collective-permute-start.1 = (bf16[1024,256]{1,0:T(8,128)(2,1)}, bf16[1024,256]{1,0:T(8,128)(2,1)S(1)}, u32[]{:S(2)}, u32[]{:S(2)}) collective-permute-start(bf16[1024,256]{1,0:T(8,128)(2,1)} %get-tuple-element.16), channel_id=1, source_target_pairs={{0,1},{1,0},{2,3},{3,2},{4,5},{5,4},{6,7},{7,6},{8,9},{9,8},{10,11... | collective-permute-start | bytes 1572872 | tf_op jit(solution)/shard_map/ppermute | solution.py:397
  71.4 1.8 %copy-start.2 = (bf16[128,128]{1,0:T(8,128)(2,1)S(1)}, bf16[128,128]{1,0:T(8,128)(2,1)}, u32[]{:S(2)}) copy-start(bf16[128,128]{1,0:T(8,128)(2,1)} %constant.46.clone.refs_2_) | copy-start | bytes 98308

commit v3 on v2

v3 whole, which is shorter than its diff:
```python
import functools

import jax
import jax.numpy as jnp
import numpy as np
from jax import lax
from jax.experimental import pallas as pl
from jax.experimental.pallas import tpu as pltpu
from jax.sharding import PartitionSpec as P

F32 = jnp.float32
BF16 = jnp.bfloat16
VMEM = pl.BlockSpec(memory_space=pltpu.VMEM)
LANES = 128
AHEAD = 3


def normalise(tokens, gain):
    as_float = tokens.astype(F32)
    scale_now = lax.rsqrt(jnp.mean(as_float * as_float, axis=-1, keepdims=True) + 1e-05)
    return (as_float * scale_now * gain).astype(BF16)


def dot(a, b):
    return jnp.dot(a, b, preferred_element_type=F32)


def params(mebibytes):
    return pltpu.CompilerParams(vmem_limit_bytes=mebibytes << 20)


def selection(shape, sources):
    matrix = np.zeros(shape, np.float32)
    matrix[np.arange(shape[0]), sources] = 1.0
    return jnp.asarray(matrix, BF16)


def row_order(items, columns):
    c, i = np.divmod(np.arange(items * columns), items)
    return selection((items * columns,) * 2, i * columns + c)


def lane_order(columns):
    part, rest = np.divmod(np.arange(columns * LANES), LANES)
    column, channel = np.divmod(rest, LANES // columns)
    return selection((columns * LANES,) * 2, column * LANES + part * (LANES // columns) + channel).T


def lane_table(columns, count):
    lane = np.arange(count * LANES)
    matrix = np.zeros((columns, count, count * LANES), np.float32)
    matrix[lane % LANES // (LANES // columns), lane // LANES, lane] = 1.0
    return jnp.asarray(matrix, BF16)


def row_kernel(parts, items, columns, x_ref, gain_ref, wu_ref, wb_ref, wc_ref, rate_ref, skip_ref,
               order_ref, lane_ref, out_ref, normed, b_scr, c_scr, u_scr, y_scr, g_scr, l_scr):
    block = items * columns
    steps = parts * columns
    rows = steps * items
    inner = u_scr.shape[1]
    gain = gain_ref[...]
    for part in range(parts):
        here = normalise(x_ref[part], gain)
        normed[part * block:(part + 1) * block, :] = dot(order_ref[...], here).astype(BF16)
    b_scr[...] = dot(normed[...], wb_ref[...]).astype(BF16).astype(F32)
    c_scr[...] = dot(normed[...], wc_ref[...]).astype(BF16).astype(F32)
    chunk = 128
    pieces = []
    at = 0
    for lag in range(steps):
        first = lag * items
        while first < rows:
            count = min(chunk, rows - first)
            pieces.append((lag, first, count, at))
            first += count
            at += count
    for lag, first, count, at in pieces:
        source = first - lag * items
        product = c_scr[first:first + count, :] * b_scr[source:source + count, :]
        g_scr[at:at + count, :] = product.astype(BF16)
    tile = 512

    def one_tile(tile_id, _):
        where = pl.ds(pl.multiple_of(tile_id * tile, tile), tile)
        u_scr[:, where] = dot(normed[...], wu_ref[:, where]).astype(BF16).astype(F32)
        rate = rate_ref[:, where]
        skip = skip_ref[:, where]
        done = -1
        table = None
        for lag, first, count, at in pieces:
            if lag != done:
                power = jnp.exp(rate * (-float(lag)))
                high = power.astype(BF16)
                low = (power - high.astype(F32)).astype(BF16)
                table = jnp.concatenate([high, low], axis=0)
                done = lag
            matrix = dot(g_scr[at:at + count, :], table)
            source = first - lag * items
            value = u_scr[source:source + count, where]
            if lag == 0:
                y_scr[first:first + count, where] = (matrix + skip) * value
            else:
                y_scr[first:first + count, where] += matrix * value
        return 0

    lax.fori_loop(0, inner // tile, one_tile, 0)
    for part in range(parts):
        for column in range(columns):
            here = slice((part * columns + column) * items, (part * columns + column + 1) * items)
            for at in range(inner // LANES):
                there = slice((at * columns + column) * LANES, (at * columns + column + 1) * LANES)
                l_scr[part * items:(part + 1) * items, there] = y_scr[here, at * LANES:(at + 1) * LANES].astype(BF16)
    halves = out_ref.shape[0] // parts
    few = items // halves
    groups = out_ref.shape[2] // few
    for at in range(inner // LANES):
        span = columns * LANES
        turned = dot(l_scr[:, at * span:(at + 1) * span], lane_ref[...])
        half, first = divmod(at * columns, groups)
        for part in range(parts):
            for own in range(halves):
                rows_at = part * items + own * few
                for k in range(0, columns, 2):
                    pair = jnp.concatenate(
                        [turned[rows_at:rows_at + few, (k + j) * LANES:(k + j + 1) * LANES] for j in range(2)], axis=0
                    )
                    out_ref[part * halves + half, own, (first + k) * few:(first + k + 2) * few, :] = pair.astype(BF16)


def row_scan(x, columns, halves, gain, w_u, w_bc, rate, skip):
    parts, block, width = x.shape
    items = block // columns
    inner = w_u.shape[1]
    state = rate.shape[0]
    rows = parts * block
    w_b, w_c = w_bc[:, :state], w_bc[:, state:2 * state]
    w_b = jnp.concatenate([w_b, w_b], axis=1)
    w_c = jnp.concatenate([w_c, w_c], axis=1)
    return pl.pallas_call(
        functools.partial(row_kernel, parts, items, columns),
        name="row_scan",
        out_shape=jax.ShapeDtypeStruct(
            (parts * halves, halves, inner * columns // (halves * LANES) * (items // halves), LANES), BF16
        ),
        in_specs=[VMEM] * 9,
        out_specs=VMEM,
        scratch_shapes=[
            pltpu.VMEM((rows, width), BF16),
            pltpu.VMEM((rows, 2 * state), F32),
            pltpu.VMEM((rows, 2 * state), F32),
            pltpu.VMEM((rows, inner), F32),
            pltpu.VMEM((rows, inner), F32),
            pltpu.VMEM((rows * (parts * columns + 1) // 2, 2 * state), BF16),
            pltpu.VMEM((parts * items, columns * inner), BF16),
        ],
        compiler_params=params(20),
        cost_estimate=pl.CostEstimate(
            flops=2 * rows * width * inner * 16, bytes_accessed=4 << 20, transcendentals=0
        ),
    )(x, gain[None, :], w_u, w_b, w_c, rate, skip[None, :], row_order(items, columns),
      lane_order(columns))


def home_kernel(columns, halves, gain_ref, wz_ref, wm_ref, order_ref, lane_ref, table_ref, *refs):
    x_refs, (gate_ref, mix_ref, n_scr) = refs[:halves], refs[halves:]
    block = order_ref.shape[0]
    items = block // columns
    steps = x_refs[0].shape[0] // columns
    groups = gate_ref.shape[1] // steps
    for half, x_ref in enumerate(x_refs):
        for start in range(x_ref.shape[0] // block):
            here = normalise(x_ref[start * block:(start + 1) * block, :], gain_ref[...])
            here = dot(order_ref[...], here).astype(BF16)
            for column in range(columns):
                first = column * steps + start * items
                n_scr[first:first + items, :] = here[column * items:(column + 1) * items]
        mix = None
        project = []
        for column in range(columns):
            here = n_scr[column * steps:(column + 1) * steps, :]
            project.append(dot(here, wz_ref[...]).astype(BF16))
            part = dot(dot(here, wm_ref[...]).astype(BF16), table_ref[column])
            mix = part if mix is None else mix + part
        for n in range(mix_ref.shape[2]):
            for at in range(steps // items):
                mix_ref[half, at, n] = mix[at * items:(at + 1) * items, n * LANES:(n + 1) * LANES]
        for at in range(wz_ref.shape[1] // LANES):
            joined = jnp.concatenate([part[:, at * LANES:(at + 1) * LANES] for part in project], axis=1)
            gate = dot(joined, lane_ref[...])
            gate = gate / (1.0 + jnp.exp(-gate))
            for k in range(columns):
                gate_ref[half, pl.ds(at * columns + k, steps, stride=groups), :] = gate[:, k * LANES:(k + 1) * LANES]


def home(tokens, items, columns, gain, w_z, w_m):
    halves = len(tokens)
    rows, width = tokens[0].shape
    steps = rows // columns
    groups = w_z.shape[1] * columns // LANES
    count = w_m.shape[1]
    gate, mix = pl.pallas_call(
        functools.partial(home_kernel, columns, halves),
        name="home",
        out_shape=(
            jax.ShapeDtypeStruct((halves, steps * groups, LANES), F32),
            jax.ShapeDtypeStruct((halves, steps // items, count, items, LANES), F32),
        ),
        in_specs=[VMEM] * (6 + halves),
        out_specs=(VMEM, VMEM),
        scratch_shapes=[pltpu.VMEM((rows, width), BF16)],
        compiler_params=params(20),
        cost_estimate=pl.CostEstimate(
            flops=4 * halves * rows * width * w_z.shape[1], bytes_accessed=8 << 20, transcendentals=0
        ),
    )(gain[None, :], w_z, w_m, row_order(items, columns), lane_order(columns), lane_table(columns, count), *tokens)
    return gate.reshape(halves, steps, groups, LANES), mix


def col_kernel(state, halves, core_ref, y_hbm, gate_hbm, mix_hbm, rate_hbm, *rest):
    outs = rest[:halves]
    y_ref, gate_ref, mix_ref, out_ref, held, decay, v_scr, g_scr, sems = rest[halves:]
    per_half, _, span_steps, _ = mix_hbm.shape[1:]
    count = halves * per_half
    groups = gate_hbm.shape[2]
    take = y_hbm.shape[0] // per_half
    items = span_steps // take
    tiles = groups // 8
    spans = [slice(f * 8, f * 8 + 8) for f in range(tiles)]

    def slot_of(at):
        return lax.rem(at // per_half + halves - core_ref[0], halves)

    def copies(at):
        half, place, slot = at // per_half, at % per_half, slot_of(at)
        first = pl.multiple_of(place * span_steps, span_steps)
        return (
            pltpu.make_async_copy(y_hbm.at[pl.ds(place * take, take), half], y_ref.at[at], sems.at[at, 0]),
            pltpu.make_async_copy(mix_hbm.at[slot, place], mix_ref.at[at], sems.at[at, 1]),
            pltpu.make_async_copy(gate_hbm.at[slot, pl.ds(first, span_steps)], gate_ref.at[at], sems.at[at, 2]),
        )

    def result(at, s):
        return pltpu.make_async_copy(out_ref.at[at], outs[s].at[at % per_half], sems.at[at, 3])

    def launch(at, _):
        for copy in copies(at):
            copy.start()
        return 0

    first_copy = pltpu.make_async_copy(rate_hbm, decay, sems.at[count, 0])
    first_copy.start()
    lax.fori_loop(0, min(AHEAD, count), launch, 0)
    held[...] = jnp.zeros_like(held)
    first_copy.wait()
    decay[...] = jnp.exp(-decay[...])

    def one_span(at, _):
        for copy in copies(at):
            copy.wait()

        @pl.when(at + AHEAD < count)
        def _():
            launch(at + AHEAD, 0)

        for k in range(take):
            v_scr[k * groups * items:(k + 1) * groups * items, :] = y_ref[at, k].astype(F32)
        carry = [held[n, span, :] for n in range(state) for span in spans]
        for t in range(span_steps):
            k, i = divmod(t, items)
            value = [v_scr[pl.ds((k * groups + f * 8) * items + i, 8, stride=items), :] for f in range(tiles)]
            total = list(value)
            for n in range(state):
                b = jnp.broadcast_to(mix_ref[at, n, t:t + 1, :], (8, LANES))
                c = jnp.broadcast_to(mix_ref[at, state + n, t:t + 1, :], (8, LANES))
                for f, span in enumerate(spans):
                    h = decay[n, span, :] * carry[n * tiles + f] + b * value[f]
                    total[f] = total[f] + c * h
                    carry[n * tiles + f] = h
            for f, span in enumerate(spans):
                g_scr[pl.ds(f * 8 * span_steps + t, 8, stride=span_steps), :] = total[f] * gate_ref[at, t, span, :]
        for n in range(state):
            for f, span in enumerate(spans):
                held[n, span, :] = carry[n * tiles + f]
        out_ref[at] = g_scr[...].astype(BF16)
        for s in range(halves):
            @pl.when(slot_of(at) == s)
            def _(s=s):
                result(at, s).start()
        return 0

    lax.fori_loop(0, count, one_span, 0)

    def finish(at, _):
        for s in range(halves):
            @pl.when(slot_of(at) == s)
            def _(s=s):
                result(at, s).wait()
        return 0

    lax.fori_loop(0, count, finish, 0)


def col_scan(core, y, gate, mix, rate):
    sources, halves, rows, _ = y.shape
    state, groups, _ = rate.shape
    per_half, _, span_steps, _ = mix.shape[1:]
    count = halves * per_half
    far = pl.BlockSpec(memory_space=pltpu.HBM)
    return pl.pallas_call(
        functools.partial(col_kernel, state, halves),
        name="col_scan",
        in_specs=[pl.BlockSpec(memory_space=pltpu.SMEM)] + [far] * 4,
        out_specs=[far] * halves,
        scratch_shapes=[
            pltpu.VMEM((count, sources // per_half, rows, LANES), BF16),
            pltpu.VMEM((count, span_steps, groups, LANES), F32),
            pltpu.VMEM((count, 2 * state, span_steps, LANES), F32),
            pltpu.VMEM((count, groups * span_steps, LANES), BF16),
            pltpu.VMEM(rate.shape, F32),
            pltpu.VMEM(rate.shape, F32),
            pltpu.VMEM((span_steps * groups, LANES), F32),
            pltpu.VMEM((span_steps * groups, LANES), F32),
            pltpu.SemaphoreType.DMA((count + 1, 4)),
        ],
        out_shape=[jax.ShapeDtypeStruct((per_half, groups * span_steps, LANES), BF16)] * halves,
        compiler_params=params(62),
        cost_estimate=pl.CostEstimate(flops=5 * count * span_steps * groups * LANES * state,
                                      bytes_accessed=8 << 20, transcendentals=0),
    )(core, y, gate, mix, rate)


def last_kernel(columns, halves, group_ref, part_ref, w_ref, lane_ref, *refs):
    out_ref, l_scr = refs[-2:]
    spans, rows, _ = part_ref.shape
    width = w_ref.shape[0] // halves
    groups = width * columns // LANES
    span = rows // groups
    steps = spans * span
    for at in range(width // LANES):
        joined = jnp.concatenate([
            jnp.concatenate([
                part_ref[p, (at * columns + k) * span:(at * columns + k + 1) * span, :] for p in range(spans)
            ], axis=0) for k in range(columns)
        ], axis=1)
        turned = dot(joined, lane_ref[...])
        for column in range(columns):
            l_scr[at, pl.ds(column, steps, stride=columns), :] = turned[:, column * LANES:(column + 1) * LANES]
    first = pl.multiple_of(group_ref[0] * width, width)
    gated = jnp.concatenate([l_scr[at].astype(BF16) for at in range(width // LANES)], axis=1)
    total = dot(gated, w_ref[pl.ds(first, width), :])
    if len(refs) > 2:
        total = total + refs[0][...]
    out_ref[...] = total.reshape(out_ref.shape).astype(out_ref.dtype)


def last(group, part, w_out, columns, halves, before, out_type):
    inner, features = w_out.shape
    groups = inner * columns // (halves * LANES)
    steps = part.shape[0] * part.shape[1] // groups
    rows = steps * columns
    others = () if before is None else (before,)
    return pl.pallas_call(
        functools.partial(last_kernel, columns, halves),
        name="last",
        out_shape=jax.ShapeDtypeStruct((steps, columns, features) if out_type == BF16 else (rows, features), out_type),
        in_specs=[pl.BlockSpec(memory_space=pltpu.SMEM)] + [VMEM] * (3 + len(others)),
        out_specs=VMEM,
        scratch_shapes=[pltpu.VMEM((groups // columns, rows, LANES), F32)],
        compiler_params=params(8),
        cost_estimate=pl.CostEstimate(
            flops=2 * rows * features * groups * LANES // columns, bytes_accessed=2 << 20, transcendentals=0
        ),
    )(group.reshape(1), part, w_out, lane_order(columns).T, *others)


def wide_row_scan(x, columns, halves, gain, w_u, w_bc, rate, skip):
    parts, block, width = x.shape
    items = block // columns
    inner = w_u.shape[1]
    state = rate.shape[0]
    normed = normalise(x.reshape(parts, items, columns, width), gain)
    normed = normed.transpose(0, 2, 1, 3).reshape(parts * columns, items, width)
    value = dot(normed, w_u).astype(BF16).astype(F32)
    mix = dot(normed, w_bc).astype(BF16).astype(F32)
    factor = jnp.exp(-rate)

    def advance(held, now):
        value_now, inject, readout = now
        held = factor * held + inject[:, :, None] * value_now[:, None, :]
        return held, jnp.sum(held * readout[:, :, None], axis=1) + skip * value_now

    start = jnp.zeros((items, state, inner), F32)
    _, out = lax.scan(advance, start, (value, mix[..., :state], mix[..., state:2 * state]))
    lanes = LANES // columns
    out = out.astype(BF16).reshape(parts, columns, halves, items // halves, halves, inner // (halves * lanes), lanes)
    return out.transpose(0, 4, 2, 5, 3, 1, 6).reshape(parts * halves, halves, -1, LANES)


def per_device(tokens, norm_gain, w_in, w_bc, rate_row, rate_col, skip_gain, w_out):
    height, columns, features = tokens.shape
    inner = w_out.shape[0]
    state = rate_row.shape[0]
    parts, halves = lax.axis_size("rows"), lax.axis_size("cols")
    core = lax.axis_index("cols")
    both = ("rows", "cols")
    sources = parts * halves
    items = height // sources
    group = inner // halves
    lanes = LANES // columns
    moved = lax.all_to_all(
        tokens.reshape(sources, items, columns, features), both, split_axis=0, concat_axis=0, tiled=True
    )
    scan = row_scan if items * halves % 8 == 0 and parts * columns <= 64 else wide_row_scan
    row_mixed = scan(
        moved.reshape(parts, halves * items * columns, features), columns, halves, norm_gain,
        w_in[:, :inner], w_bc[:, :2 * state], rate_row, skip_gain
    )
    back = lax.all_to_all(row_mixed, both, split_axis=0, concat_axis=0, tiled=True)

    tokens = tokens.reshape(height * columns, features)
    whole = [tokens] + [
        lax.ppermute(tokens, "cols", [(k, (k - s) % halves) for k in range(halves)]) for s in range(1, halves)
    ]
    own = core * group
    w_gate = lax.dynamic_slice_in_dim(w_in, inner + own, group, 1)
    gate, mix = home(whole, 16, columns, norm_gain, w_gate, w_bc[:, 2 * state:])
    rate = lax.dynamic_slice_in_dim(rate_col, own, group, 1)
    rate = jnp.tile(rate.reshape(state, group // lanes, lanes), (1, 1, columns))
    if items % 8 != 0:
        blocks = max(1, height // 16)
        back = back.reshape(blocks, sources // blocks, halves, group // lanes, items, LANES)
        back = back.transpose(0, 2, 3, 1, 4, 5).reshape(blocks, halves, -1, LANES)
    gated = col_scan(core.reshape(1), back, gate, mix, rate)
    out = last(core, gated[0], w_out, columns, halves, None, BF16 if halves == 1 else F32)
    for s in range(1, halves):
        arrived = lax.ppermute(gated[s], "cols", [(k, (k + s) % halves) for k in range(halves)])
        out = last((core - s) % halves, arrived, w_out, columns, halves, out, BF16 if s == halves - 1 else F32)
    return out


def solution(mesh):
    placed = (P(("slides", "cols"), "rows", None), P(), P(), P(), P(), P(), P(), P())
    return jax.shard_map(
        per_device,
        mesh=mesh,
        in_specs=placed,
        out_specs=P(("slides", "cols"), "rows", None),
        check_vma=False,
    )
```

time: 77 us -> 72.2 us (0.938)
  waiting for transfers between devices: 30.1 us -> 23.3 us
  local copies, waits for them, and re-layouts: 7.27 us -> 9.71 us
    all_to_all x1, waiting for transfers between devices: 18.1 us -> 11.7 us  [per_device(): lax.all_to_all(row_mixed, both, split_axis=0, concat_axis=0, tiled=True)]
    unnamed x23 -> x27, local copies, waits for them, and re-layouts: 0.17 us -> 5.7 us
    another operation x2 -> x3, local copies, waits for them, and re-layouts: 3.32 us -> 1.13 us  [per_device(): rate = jnp.tile(rate.reshape(state, group // lanes, lanes), (1, 1, columns))]
    pallas_call x1, Pallas kernels: 10.5 us -> 8.71 us  [col_scan(): pl.pallas_call(functools.partial(col_kernel, state, halves), name='col_sc...]
    pallas_call x3, Pallas kernels: 6.95 us -> 7.83 us  [the longest x1 5.55 us: home(): pl.pallas_call(functools.partial(home_kernel, columns, halves), name='hom...]
    reshape x3 -> x1, local copies, waits for them, and re-layouts: 0.99 us -> 0.12 us  [per_device(): moved.reshape(parts, halves * items * columns, features)]
  transfers between devices with their start and end apart: 4 -> 4, of which waited for: 3 -> 2; matrix products, arithmetic and copies ran while one was open for 6% -> 6% of each run, Pallas kernels for 6% -> 9%
where the time goes in v3:
time: 72.2 us; the launch traced here: 71.7 us
  Pallas kernels  24.8 us (34%)
  waiting for transfers between devices  23.3 us (32%)
  starting transfers between devices  13.6 us (19%)
  local copies, waits for them, and re-layouts  9.71 us (13%)
    all_to_all x1, waiting for transfers between devices, per_device(): lax.all_to_all(row_mixed, both, split_axis=0, concat_axis=0, tiled=True)  11.7 us
    all_to_all x1, waiting for transfers between devices, per_device(): lax.all_to_all(tokens.reshape(sources, items, columns, features), both, s...  11.6 us
    pallas_call x1, Pallas kernels, col_scan(): pl.pallas_call(functools.partial(col_kernel, state, halves), name='col_sc...  8.71 us
    pallas_call x1, Pallas kernels, row_scan(): pl.pallas_call(functools.partial(row_kernel, parts, items, columns), name...  8.23 us
    all_to_all x1, starting transfers between devices, per_device(): lax.all_to_all(tokens.reshape(sources, items, columns, features), both, s...  6.61 us
    unnamed x27, local copies, waits for them, and re-layouts  5.7 us
    all_to_all x1, starting transfers between devices, per_device(): lax.all_to_all(row_mixed, both, split_axis=0, concat_axis=0, tiled=True)  5.63 us
    pallas_call x1, Pallas kernels, home(): pl.pallas_call(functools.partial(home_kernel, columns, halves), name='hom...  5.55 us
  transfers between devices with their start and end apart: 4, of which 2 were waited for; matrix products, arithmetic and copies ran while one was open for 6% of the time, Pallas kernels for 9%

profile of v3, /device:TPU:17, one launch (start us, length us, event | category | flops | bytes accessed | tf_op | source)
XLA Modules:
  0.0 71.7 jit_solution(14572434105067338535)
XLA Ops:
  0.0 0.0 copy-start.6
  0.0 0.0 copy-start.7
  0.0 0.0 copy-start.8
  0.0 0.0 copy-start.10
  0.1 6.6 %all-to-all-start = ((bf16[16,8,4,512]{3,2,1,0:T(4,128)(2,1)}), bf16[16,8,4,512]{3,2,1,0:T(4,128)(2,1)S(1)}, u32[]{:S(2)}, u32[]{:S(2)}) async-start(bf16[16,8,4,512]{3,2,1,0:T(4,128)(2,1)} %bitcast.10), calls=%async_computation | async-start | bytes 1048576 | tf_op jit(solution)/shard_map/all_to_all | solution.py:411
  6.7 1.3 %slice.15.wu_ref = bf16[512,1024]{1,0:T(8,128)(2,1)S(1)} slice(bf16[512,2048]{1,0:T(8,128)(2,1)} %param.17), slice={[0:512], [0:1024]} | slice | bytes 2097152 | tf_op jit(solution)/shard_map/slice | solution.py:417
  8.0 0.1 copy.21.wb_ref
  8.1 0.1 copy.22.wc_ref
  8.3 11.6 %all-to-all-done = bf16[16,8,4,512]{3,2,1,0:T(4,128)(2,1)S(1)} async-done(((bf16[16,8,4,512]{3,2,1,0:T(4,128)(2,1)}), bf16[16,8,4,512]{3,2,1,0:T(4,128)(2,1)S(1)}, u32[]{:S(2)}, u32[]{:S(2)}) %all-to-all-start) | async-done | bytes 524320 | tf_op jit(solution)/shard_map/all_to_all | solution.py:411
  19.9 0.1 reshape.26.x_ref
  20.0 8.2 %row_scan.1 = bf16[16,2,128,128]{3,2,1,0:T(8,128)(2,1)} custom-call(bf16[8,64,512]{2,1,0:T(8,128)(2,1)S(1)} %reshape.26.x_ref, f32[1,512]{1,0:T(1,128)S(1)} %bitcast.8, bf16[512,1024]{1,0:T(8,128)(2,1)S(1)} %slice.15.wu_ref, bf16[512,32]{1,0:T(8,128)(2,1)S(1)} %copy.21.wb_ref, bf16[512,32]{1,0:T(8,128)(2,1)S(1)} %copy.22.wc_ref, f32[16,1024]{1,0:T(8,128)S(1)} %copy-done.6, ...), custom_call_target="tpu_custom_call" | custom-call | flops 8589934592 | bytes 4194304 | tf_op jit(solution)/shard_map/row_scan/pallas_call | solution.py:140
  28.3 5.6 %all-to-all-start.1 = ((bf16[16,2,128,128]{3,2,1,0:T(8,128)(2,1)}), bf16[16,2,128,128]{3,2,1,0:T(8,128)(2,1)}, u32[]{:S(2)}, u32[]{:S(2)}) async-start(bf16[16,2,128,128]{3,2,1,0:T(8,128)(2,1)} %row_scan.1), calls=%async_computation.1 | async-start | bytes 2097152 | tf_op jit(solution)/shard_map/all_to_all | solution.py:419
  33.9 0.1 reshape.27.refs_0_
  34.0 0.4 collective-permute-start
  34.5 0.1 copy.24.wm_ref
  34.6 0.1 tile.10
  34.7 0.1 tile.11
  34.9 0.9 %tile.12.rate_hbm = f32[16,16,128]{2,1,0:T(8,128)} reshape(f32[16,16,4,32]{3,2,1,0:T(4,128)S(1)} %tile.11) | data formatting | bytes 262144 | tf_op jit(solution)/shard_map/tile | solution.py:429
  35.8 1.1 %constant_dynamic-slice_fusion.1.wz_ref = bf16[512,512]{1,0:T(8,128)(2,1)S(1)} fusion(bf16[512,2048]{1,0:T(8,128)(2,1)} %param.17, s32[]{:T(128)S(6)} %select_n.14), kind=kLoop, calls=%fused_computation.3 | loop fusion | bytes 1048580 | tf_op jit(solution)/shard_map/dynamic_slice | solution.py:426
  36.8 0.0 collective-permute-done.refs_1_
  36.9 0.0 copy-start.9
  36.9 1.2 %copy-done.9 = bf16[4,32,4096]{2,1,0:T(8,128)(2,1)S(1)} copy-done((bf16[4,32,4096]{2,1,0:T(8,128)(2,1)S(1)}, bf16[4,32,4096]{2,1,0:T(8,128)(2,1)}, u32[]{:S(2)}) %copy-start.9) | copy-done | bytes 1048600
  38.1 5.5 %home.1 = (f32[2,2048,128]{2,1,0:T(8,128)S(1)}, f32[2,8,32,16,128]{4,3,2,1,0:T(8,128)S(1)}) custom-call(f32[1,512]{1,0:T(1,128)S(1)} %bitcast.9, bf16[512,512]{1,0:T(8,128)(2,1)S(1)} %constant_dynamic-slice_fusion.1.wz_ref, bf16[512,32]{1,0:T(8,128)(2,1)S(1)} %copy.24.wm_ref, bf16[64,64]{1,0:T(8,128)(2,1)S(1)} %copy-done.10, bf16[512,512]{1,0:T(8,128)(2,1)S(1)} %copy-done.4, ...), custom_call_target="tpu_custom_call" | custom-call | flops 1073741824 | bytes 8388608 | tf_op jit(solution)/shard_map/home/pallas_call | solution.py:202
  43.7 1.9 %copy-done.1 = f32[2,8,32,16,128]{4,3,2,1,0:T(8,128)} copy-done((f32[2,8,32,16,128]{4,3,2,1,0:T(8,128)}, f32[2,8,32,16,128]{4,3,2,1,0:T(8,128)S(1)}, u32[]{:S(2)}) %copy-start.1) | copy-done | bytes 4194328
  45.6 1.3 %copy-done.3 = f32[2,2048,128]{2,1,0:T(8,128)} copy-done((f32[2,2048,128]{2,1,0:T(8,128)}, f32[2,2048,128]{2,1,0:T(8,128)S(1)}, u32[]{:S(2)}) %copy-start.3) | copy-done | bytes 2097176
  46.9 11.7 %all-to-all-done.1.y_hbm = bf16[16,2,128,128]{3,2,1,0:T(8,128)(2,1)} async-done(((bf16[16,2,128,128]{3,2,1,0:T(8,128)(2,1)}), bf16[16,2,128,128]{3,2,1,0:T(8,128)(2,1)}, u32[]{:S(2)}, u32[]{:S(2)}) %all-to-all-start.1) | async-done | bytes 1048608 | tf_op jit(solution)/shard_map/all_to_all | solution.py:419
  58.7 8.7 %col_scan.1 = (bf16[8,256,128]{2,1,0:T(8,128)(2,1)}, bf16[8,256,128]{2,1,0:T(8,128)(2,1)}) custom-call(s32[1]{0:T(128)} %bitcast.1.core_ref.group_ref, bf16[16,2,128,128]{3,2,1,0:T(8,128)(2,1)} %all-to-all-done.1.y_hbm, f32[2,128,16,128]{3,2,1,0:T(8,128)} %bitcast.6, f32[2,8,32,16,128]{4,3,2,1,0:T(8,128)} %copy-done.1, f32[16,16,128]{2,1,0:T(8,128)} %tile.12.rate_hbm), custom_call_target="tpu_custom_call" | custom-call | flops 41943040 | bytes 8388608 | tf_op jit(solution)/shard_map/col_scan/pallas_call | solution.py:310
  67.4 0.9 %collective-permute-start.1 = (bf16[8,256,128]{2,1,0:T(8,128)(2,1)}, bf16[8,256,128]{2,1,0:T(8,128)(2,1)S(1)}, u32[]{:S(2)}, u32[]{:S(2)}) collective-permute-start(bf16[8,256,128]{2,1,0:T(8,128)(2,1)} %get-tuple-element.11), channel_id=1, source_target_pairs={{0,1},{1,0},{2,3},{3,2},{4,5},{5,4},{6,7},{7,6},{8,9},{9,8},{10,11... | collective-permute-start | bytes 1572872 | tf_op jit(solution)/shard_map/ppermute | solution.py:437
  68.3 1.0 %copy-done.5 = bf16[8,256,128]{2,1,0:T(8,128)(2,1)S(1)} copy-done((bf16[8,256,128]{2,1,0:T(8,128)(2,1)S(1)}, bf16[8,256,128]{2,1,0:T(8,128)(2,1)}, u32[]{:S(2)}) %copy-start.5) | copy-done | bytes 524312
  69.4 0.7 last.2.refs_0_
  70.1 0.0 collective-permute-done.1.part_ref
  70.1 1.6 %last.3 = bf16[128,4,512]{2,1,0:T(4,128)(2,1)} custom-call(s32[1]{0:T(128)} %bitcast.group_ref, bf16[8,256,128]{2,1,0:T(8,128)(2,1)S(1)} %collective-permute-done.1.part_ref, bf16[1024,512]{1,0:T(8,128)(2,1)S(1)} %copy-done.2, bf16[512,512]{1,0:T(8,128)(2,1)S(1)} %copy-done.4, f32[512,512]{1,0:T(8,128)S(1)} %last.2.refs_0_), custom_call_target="tpu_custom_call" | custom-call | flops 268435456 | bytes 2097152 | tf_op jit(solution)/shard_map/last/pallas_call | solution.py:363
  (22 shorter events, 0.1 us)
Async XLA Ops:
  0.0 34.6 %copy-start = (f32[16,1024]{1,0:T(8,128)S(1)}, f32[16,1024]{1,0:T(8,128)}, u32[]{:S(2)}) copy-start(f32[16,1024]{1,0:T(8,128)} %param.20) | copy-start | bytes 196612
  0.0 8.0 %copy-start.12 = (bf16[512,64]{0,1:T(8,128)(2,1)S(1)}, bf16[512,64]{0,1:T(8,128)(2,1)}, u32[]{:S(2)}) copy-start(bf16[512,64]{0,1:T(8,128)(2,1)} %param.18) | copy-start | bytes 196612
  0.0 20.0 %copy-start.4 = (bf16[512,512]{1,0:T(8,128)(2,1)S(1)}, bf16[512,512]{1,0:T(8,128)(2,1)}, u32[]{:S(2)}) copy-start(bf16[512,512]{1,0:T(8,128)(2,1)} %constant.35.clone.lane_ref) | copy-start | bytes 1572868
  0.0 20.0 %copy-start.6 = (f32[16,1024]{1,0:T(8,128)S(1)}, f32[16,1024]{1,0:T(8,128)}, u32[]{:S(2)}) copy-start(f32[16,1024]{1,0:T(8,128)} %rate_ref.1) | copy-start | bytes 196612
  0.0 20.0 %copy-start.7 = (f32[1024]{0:T(1024)S(1)}, f32[1024]{0:T(1024)}, u32[]{:S(2)}) copy-start(f32[1024]{0:T(1024)} %param.21) | copy-start | bytes 12292
  0.0 20.0 %copy-start.8 = (f32[512]{0:T(512)S(1)}, f32[512]{0:T(512)}, u32[]{:S(2)}) copy-start(f32[512]{0:T(512)} %param.16) | copy-start | bytes 6148
  0.0 20.0 %copy-start.10 = (bf16[64,64]{1,0:T(8,128)(2,1)S(1)}, bf16[64,64]{1,0:T(8,128)(2,1)}, u32[]{:S(2)}) copy-start(bf16[64,64]{1,0:T(8,128)(2,1)} %constant.34.clone.order_ref) | copy-start | bytes 24580
  0.1 19.8 %all-to-all-start = ((bf16[16,8,4,512]{3,2,1,0:T(4,128)(2,1)}), bf16[16,8,4,512]{3,2,1,0:T(4,128)(2,1)S(1)}, u32[]{:S(2)}, u32[]{:S(2)}) async-start(bf16[16,8,4,512]{3,2,1,0:T(4,128)(2,1)} %bitcast.10), calls=%async_computation | async-start | bytes 1048576 | tf_op jit(solution)/shard_map/all_to_all | solution.py:411
  28.3 5.6 %copy-start.11 = (bf16[128,4,512]{2,1,0:T(4,128)(2,1)S(1)}, bf16[128,4,512]{2,1,0:T(4,128)(2,1)}, u32[]{:S(2)}) copy-start(bf16[128,4,512]{2,1,0:T(4,128)(2,1)} %param.15) | copy-start | bytes 1572868
  28.3 6.2 %slice-start = ((bf16[512,64]{0,1:T(8,128)(2,1)}), bf16[512,32]{0,1:T(8,128)(2,1)S(1)}, s32[]{:S(2)}) async-start(bf16[512,64]{0,1:T(8,128)(2,1)} %param.18), calls=%async_computation.2 | async-start | bytes 65536 | tf_op jit(solution)/shard_map/slice | solution.py:427
  28.3 30.4 %all-to-all-start.1 = ((bf16[16,2,128,128]{3,2,1,0:T(8,128)(2,1)}), bf16[16,2,128,128]{3,2,1,0:T(8,128)(2,1)}, u32[]{:S(2)}, u32[]{:S(2)}) async-start(bf16[16,2,128,128]{3,2,1,0:T(8,128)(2,1)} %row_scan.1), calls=%async_computation.1 | async-start | bytes 2097152 | tf_op jit(solution)/shard_map/all_to_all | solution.py:419
  34.0 2.8 %collective-permute-start = (bf16[512,512]{1,0:T(8,128)(2,1)S(1)}, bf16[512,512]{1,0:T(8,128)(2,1)S(1)}, u32[]{:S(2)}, u32[]{:S(2)}) collective-permute-start(bf16[512,512]{1,0:T(8,128)(2,1)S(1)} %reshape.27.refs_0_), channel_id=1, source_target_pairs={{0,1},{1,0},{2,3},{3,2},{4,5},{5,4},{6,7},{7,6},{8,9},{9,8},{10,11... | collective-permute-start | bytes 1572872 | tf_op jit(solution)/shard_map/ppermute | solution.py:423
  36.9 1.2 %copy-start.9 = (bf16[4,32,4096]{2,1,0:T(8,128)(2,1)S(1)}, bf16[4,32,4096]{2,1,0:T(8,128)(2,1)}, u32[]{:S(2)}) copy-start(bf16[4,32,4096]{2,1,0:T(8,128)(2,1)} %constant.36.clone.table_ref) | copy-start | bytes 3145732
  43.6 1.9 %copy-start.1 = (f32[2,8,32,16,128]{4,3,2,1,0:T(8,128)}, f32[2,8,32,16,128]{4,3,2,1,0:T(8,128)S(1)}, u32[]{:S(2)}) copy-start(f32[2,8,32,16,128]{4,3,2,1,0:T(8,128)S(1)} %get-tuple-element.10.mix_hbm) | copy-start | bytes 12582916
  45.6 1.3 %copy-start.3 = (f32[2,2048,128]{2,1,0:T(8,128)}, f32[2,2048,128]{2,1,0:T(8,128)S(1)}, u32[]{:S(2)}) copy-start(f32[2,2048,128]{2,1,0:T(8,128)S(1)} %get-tuple-element.9) | copy-start | bytes 6291460
  58.7 9.7 %copy-start.2 = (bf16[1024,512]{1,0:T(8,128)(2,1)S(1)}, bf16[1024,512]{1,0:T(8,128)(2,1)}, u32[]{:S(2)}) copy-start(bf16[1024,512]{1,0:T(8,128)(2,1)} %w_ref.3) | copy-start | bytes 3145732
  67.4 2.7 %collective-permute-start.1 = (bf16[8,256,128]{2,1,0:T(8,128)(2,1)}, bf16[8,256,128]{2,1,0:T(8,128)(2,1)S(1)}, u32[]{:S(2)}, u32[]{:S(2)}) collective-permute-start(bf16[8,256,128]{2,1,0:T(8,128)(2,1)} %get-tuple-element.11), channel_id=1, source_target_pairs={{0,1},{1,0},{2,3},{3,2},{4,5},{5,4},{6,7},{7,6},{8,9},{9,8},{10,11... | collective-permute-start | bytes 1572872 | tf_op jit(solution)/shard_map/ppermute | solution.py:437
  68.3 1.0 %copy-start.5 = (bf16[8,256,128]{2,1,0:T(8,128)(2,1)S(1)}, bf16[8,256,128]{2,1,0:T(8,128)(2,1)}, u32[]{:S(2)}) copy-start(bf16[8,256,128]{2,1,0:T(8,128)(2,1)} %get-tuple-element.12.part_ref) | copy-start | bytes 1572868

commit v4 on v3

--- a/solution.py
+++ b/solution.py
@@ -53,18 +53,27 @@
     return jnp.asarray(matrix, BF16)
 
 
-def row_kernel(parts, items, columns, x_ref, gain_ref, wu_ref, wb_ref, wc_ref, rate_ref, skip_ref,
-               order_ref, lane_ref, out_ref, normed, b_scr, c_scr, u_scr, y_scr, g_scr, l_scr):
+def row_kernel(parts, items, columns, halves, x_ref, gain_ref, wu_ref, wbc_ref, rate_ref, skip_ref,
+               lane_ref, out_hbm, normed, b_scr, c_scr, u_all, y_all, g_scr, l_all, out_scr, p_scr, sems):
     block = items * columns
     steps = parts * columns
     rows = steps * items
-    inner = u_scr.shape[1]
+    tile = u_all.shape[2]
+    state = rate_ref.shape[0]
     gain = gain_ref[...]
     for part in range(parts):
-        here = normalise(x_ref[part], gain)
-        normed[part * block:(part + 1) * block, :] = dot(order_ref[...], here).astype(BF16)
-    b_scr[...] = dot(normed[...], wb_ref[...]).astype(BF16).astype(F32)
-    c_scr[...] = dot(normed[...], wc_ref[...]).astype(BF16).astype(F32)
+        here = normalise(x_ref[part], gain).astype(F32)
+        for at in range(p_scr.shape[0]):
+            there = slice(at * LANES, (at + 1) * LANES)
+            p_scr[at, part * block:(part + 1) * block, :] = here[:, there]
+            for column in range(columns):
+                first = (part * columns + column) * items
+                normed[first:first + items, there] = (
+                    p_scr[at, pl.ds(part * block + column, items, stride=columns), :].astype(BF16)
+                )
+    mix = dot(normed[...], wbc_ref[...]).astype(BF16).astype(F32)
+    b_scr[...] = mix[:, :2 * state]
+    c_scr[...] = mix[:, LANES:LANES + 2 * state]
     chunk = 128
     pieces = []
     at = 0
@@ -79,14 +88,25 @@
         source = first - lag * items
         product = c_scr[first:first + count, :] * b_scr[source:source + count, :]
         g_scr[at:at + count, :] = product.astype(BF16)
-    tile = 512
-
-    def one_tile(tile_id, _):
-        where = pl.ds(pl.multiple_of(tile_id * tile, tile), tile)
-        u_scr[:, where] = dot(normed[...], wu_ref[:, where]).astype(BF16).astype(F32)
+    few = items // halves
+    pieces_out = out_scr.shape[1]
+    tiles_each = tile // LANES // pieces_out
+    rows_each = out_scr.shape[4]
+
+    def send(tile_id, piece):
+        return pltpu.make_async_copy(
+            out_scr.at[tile_id, piece],
+            out_hbm.at[:, tile_id, :, pl.ds(piece * rows_each, rows_each), :],
+            sems.at[tile_id, piece],
+        )
+
+    def one_tile(tile_id, u_scr, y_scr, l_scr):
+        where = slice(tile_id * tile, (tile_id + 1) * tile)
+        u_scr[...] = dot(normed[...], wu_ref[:, where]).astype(BF16).astype(F32)
         rate = rate_ref[:, where]
         skip = skip_ref[:, where]
-        done = -1
+        ones = jnp.concatenate([jnp.ones((state, LANES), BF16), jnp.zeros((state, LANES), BF16)], axis=0)
+        done = 0
         table = None
         for lag, first, count, at in pieces:
             if lag != done:
@@ -95,37 +115,41 @@
                 low = (power - high.astype(F32)).astype(BF16)
                 table = jnp.concatenate([high, low], axis=0)
                 done = lag
-            matrix = dot(g_scr[at:at + count, :], table)
             source = first - lag * items
-            value = u_scr[source:source + count, where]
+            value = u_scr[source:source + count, :]
             if lag == 0:
-                y_scr[first:first + count, where] = (matrix + skip) * value
+                matrix = jnp.concatenate([dot(g_scr[at:at + count, :], ones)] * (tile // LANES), axis=1)
+                y_scr[first:first + count, :] = (matrix + skip) * value
             else:
-                y_scr[first:first + count, where] += matrix * value
-        return 0
-
-    lax.fori_loop(0, inner // tile, one_tile, 0)
-    for part in range(parts):
-        for column in range(columns):
-            here = slice((part * columns + column) * items, (part * columns + column + 1) * items)
-            for at in range(inner // LANES):
-                there = slice((at * columns + column) * LANES, (at * columns + column + 1) * LANES)
-                l_scr[part * items:(part + 1) * items, there] = y_scr[here, at * LANES:(at + 1) * LANES].astype(BF16)
-    halves = out_ref.shape[0] // parts
-    few = items // halves
-    groups = out_ref.shape[2] // few
-    for at in range(inner // LANES):
-        span = columns * LANES
-        turned = dot(l_scr[:, at * span:(at + 1) * span], lane_ref[...])
-        half, first = divmod(at * columns, groups)
+                y_scr[first:first + count, :] += dot(g_scr[at:at + count, :], table) * value
+        tall = parts * items
         for part in range(parts):
-            for own in range(halves):
-                rows_at = part * items + own * few
-                for k in range(0, columns, 2):
-                    pair = jnp.concatenate(
-                        [turned[rows_at:rows_at + few, (k + j) * LANES:(k + j + 1) * LANES] for j in range(2)], axis=0
-                    )
-                    out_ref[part * halves + half, own, (first + k) * few:(first + k + 2) * few, :] = pair.astype(BF16)
+            for column in range(columns):
+                here = slice((part * columns + column) * items, (part * columns + column + 1) * items)
+                there = slice(column * LANES, (column + 1) * LANES)
+                for at in range(tile // LANES):
+                    begin = at * tall + part * items
+                    l_scr[begin:begin + items, there] = y_scr[here, at * LANES:(at + 1) * LANES].astype(BF16)
+        for k in range(0, columns, 2):
+            turned = dot(l_scr[...], lane_ref[:, k * LANES:(k + 2) * LANES])
+            for at in range(tile // LANES):
+                piece, first = divmod(at, tiles_each)
+                begin = (first * columns + k) * few
+                for part in range(parts):
+                    for own in range(halves):
+                        rows_at = at * tall + part * items + own * few
+                        pair = jnp.concatenate(
+                            [turned[rows_at:rows_at + few, j * LANES:(j + 1) * LANES] for j in range(2)], axis=0
+                        )
+                        out_scr[tile_id, piece, part, own, begin:begin + 2 * few, :] = pair.astype(BF16)
+        for piece in range(pieces_out):
+            send(tile_id, piece).start()
+
+    for tile_id in range(halves):
+        one_tile(tile_id, u_all.at[tile_id], y_all.at[tile_id], l_all.at[tile_id])
+    for half in range(halves):
+        for piece in range(pieces_out):
+            send(half, piece).wait()
 
 
 def row_scan(x, columns, halves, gain, w_u, w_bc, rate, skip):
@@ -135,31 +159,35 @@
     state = rate.shape[0]
     rows = parts * block
     w_b, w_c = w_bc[:, :state], w_bc[:, state:2 * state]
-    w_b = jnp.concatenate([w_b, w_b], axis=1)
-    w_c = jnp.concatenate([w_c, w_c], axis=1)
-    return pl.pallas_call(
-        functools.partial(row_kernel, parts, items, columns),
+    blank = jnp.zeros((width, LANES - 2 * state), BF16)
+    w_mix = jnp.concatenate([w_b, w_b, blank, w_c, w_c, blank], axis=1)
+    tile = inner // halves
+    out_rows = tile * columns // LANES * (items // halves)
+    pieces_out = 2
+    out = pl.pallas_call(
+        functools.partial(row_kernel, parts, items, columns, halves),
         name="row_scan",
-        out_shape=jax.ShapeDtypeStruct(
-            (parts * halves, halves, inner * columns // (halves * LANES) * (items // halves), LANES), BF16
-        ),
-        in_specs=[VMEM] * 9,
-        out_specs=VMEM,
+        out_shape=jax.ShapeDtypeStruct((parts, halves, halves, out_rows, LANES), BF16),
+        in_specs=[VMEM] * 7,
+        out_specs=pl.BlockSpec(memory_space=pltpu.HBM),
         scratch_shapes=[
             pltpu.VMEM((rows, width), BF16),
             pltpu.VMEM((rows, 2 * state), F32),
             pltpu.VMEM((rows, 2 * state), F32),
-            pltpu.VMEM((rows, inner), F32),
-            pltpu.VMEM((rows, inner), F32),
+            pltpu.VMEM((halves, rows, tile), F32),
+            pltpu.VMEM((halves, rows, tile), F32),
             pltpu.VMEM((rows * (parts * columns + 1) // 2, 2 * state), BF16),
-            pltpu.VMEM((parts * items, columns * inner), BF16),
+            pltpu.VMEM((halves, parts * items * tile // LANES, columns * LANES), BF16),
+            pltpu.VMEM((halves, pieces_out, parts, halves, out_rows // pieces_out, LANES), BF16),
+            pltpu.VMEM((width // LANES, rows, LANES), F32),
+            pltpu.SemaphoreType.DMA((halves, pieces_out)),
         ],
         compiler_params=params(20),
         cost_estimate=pl.CostEstimate(
             flops=2 * rows * width * inner * 16, bytes_accessed=4 << 20, transcendentals=0
         ),
-    )(x, gain[None, :], w_u, w_b, w_c, rate, skip[None, :], row_order(items, columns),
-      lane_order(columns))
+    )(x, gain[None, :], w_u, w_mix, rate, skip[None, :], lane_order(columns))
+    return out.reshape(parts * halves, halves, out_rows, LANES)
 
 
 def home_kernel(columns, halves, gain_ref, wz_ref, wm_ref, order_ref, lane_ref, table_ref, *refs):

time: 72.2 us -> 71.6 us (level)
  no operation moved by 1% of the time
where the time goes in v4:
time: 71.6 us; the launch traced here: 71.1 us
  Pallas kernels  24.2 us (34%)
  waiting for transfers between devices  22.9 us (32%)
  starting transfers between devices  13.6 us (19%)
  local copies, waits for them, and re-layouts  10.1 us (14%)
    all_to_all x1, waiting for transfers between devices, per_device(): lax.all_to_all(row_mixed, both, split_axis=0, concat_axis=0, tiled=True)  11.7 us
    all_to_all x1, waiting for transfers between devices, per_device(): lax.all_to_all(tokens.reshape(sources, items, columns, features), both, s...  11.2 us
    pallas_call x1, Pallas kernels, col_scan(): pl.pallas_call(functools.partial(col_kernel, state, halves), name='col_sc...  8.71 us
    pallas_call x1, Pallas kernels, row_scan(): pl.pallas_call(functools.partial(row_kernel, parts, items, columns, halve...  7.68 us
    all_to_all x1, starting transfers between devices, per_device(): lax.all_to_all(tokens.reshape(sources, items, columns, features), both, s...  6.6 us
    unnamed x27, local copies, waits for them, and re-layouts  5.7 us
    all_to_all x1, starting transfers between devices, per_device(): lax.all_to_all(row_mixed, both, split_axis=0, concat_axis=0, tiled=True)  5.63 us
    pallas_call x1, Pallas kernels, home(): pl.pallas_call(functools.partial(home_kernel, columns, halves), name='hom...  5.57 us
  transfers between devices with their start and end apart: 4, of which 2 were waited for; matrix products, arithmetic and copies ran while one was open for 6% of the time, Pallas kernels for 9%

profile of v4, /device:TPU:17, one launch (start us, length us, event | category | flops | bytes accessed | tf_op | source)
XLA Modules:
  0.0 71.1 jit_solution(13970878373727126078)
XLA Ops:
  0.0 6.6 %all-to-all-start = ((bf16[16,8,4,512]{3,2,1,0:T(4,128)(2,1)}), bf16[16,8,4,512]{3,2,1,0:T(4,128)(2,1)S(1)}, u32[]{:S(2)}, u32[]{:S(2)}) async-start(bf16[16,8,4,512]{3,2,1,0:T(4,128)(2,1)} %bitcast.11), calls=%async_computation | async-start | bytes 1048576 | tf_op jit(solution)/shard_map/all_to_all | solution.py:439
  6.6 0.0 copy-start.6
  6.6 0.0 copy-start.7
  6.6 0.0 copy-start.8
  6.7 1.3 %slice.15.wu_ref = bf16[512,1024]{1,0:T(8,128)(2,1)S(1)} slice(bf16[512,2048]{1,0:T(8,128)(2,1)} %param.16), slice={[0:512], [0:1024]} | slice | bytes 2097152 | tf_op jit(solution)/shard_map/slice | solution.py:445
  8.0 0.1 copy.15
  8.2 0.1 copy.17
  8.3 0.3 concatenate.3.wbc_ref
  8.6 11.2 %all-to-all-done = bf16[16,8,4,512]{3,2,1,0:T(4,128)(2,1)S(1)} async-done(((bf16[16,8,4,512]{3,2,1,0:T(4,128)(2,1)}), bf16[16,8,4,512]{3,2,1,0:T(4,128)(2,1)S(1)}, u32[]{:S(2)}, u32[]{:S(2)}) %all-to-all-start) | async-done | bytes 524320 | tf_op jit(solution)/shard_map/all_to_all | solution.py:439
  19.8 0.1 reshape.29.x_ref
  20.0 7.7 %row_scan.1 = bf16[8,2,2,128,128]{4,3,2,1,0:T(8,128)(2,1)} custom-call(bf16[8,64,512]{2,1,0:T(8,128)(2,1)S(1)} %reshape.29.x_ref, f32[1,512]{1,0:T(1,128)S(1)} %bitcast.9, bf16[512,1024]{1,0:T(8,128)(2,1)S(1)} %slice.15.wu_ref, bf16[512,256]{1,0:T(8,128)(2,1)S(1)} %concatenate.3.wbc_ref, f32[16,1024]{1,0:T(8,128)S(1)} %copy-done.6, f32[1,1024]{1,0:T(1,128)S(1)} %bitcast.8, ...), custom_call_target="tpu_custom_call" | custom-call | flops 8589934592 | bytes 4194304 | tf_op jit(solution)/shard_map/row_scan/pallas_call | solution.py:167
  27.7 0.0 slice-start
  27.7 5.6 %all-to-all-start.1 = ((bf16[16,2,128,128]{3,2,1,0:T(8,128)(2,1)}), bf16[16,2,128,128]{3,2,1,0:T(8,128)(2,1)}, u32[]{:S(2)}, u32[]{:S(2)}) async-start(bf16[16,2,128,128]{3,2,1,0:T(8,128)(2,1)} %bitcast.5), calls=%async_computation.1 | async-start | bytes 2097152 | tf_op jit(solution)/shard_map/all_to_all | solution.py:447
  33.3 0.0 copy-start.10
  33.3 0.1 reshape.31.refs_0_
  33.5 0.4 collective-permute-start
  33.9 0.1 copy.20.wm_ref
  34.1 0.1 tile.10
  34.1 0.1 tile.11
  34.3 0.9 %tile.12.rate_hbm = f32[16,16,128]{2,1,0:T(8,128)} reshape(f32[16,16,4,32]{3,2,1,0:T(4,128)S(1)} %tile.11) | data formatting | bytes 262144 | tf_op jit(solution)/shard_map/tile | solution.py:457
  35.2 1.1 %constant_dynamic-slice_fusion.1.wz_ref = bf16[512,512]{1,0:T(8,128)(2,1)S(1)} fusion(bf16[512,2048]{1,0:T(8,128)(2,1)} %param.16, s32[]{:T(128)S(6)} %select_n.14), kind=kLoop, calls=%fused_computation.1 | loop fusion | bytes 1048580 | tf_op jit(solution)/shard_map/dynamic_slice | solution.py:454
  36.3 0.0 copy-start.9
  36.3 1.2 %copy-done.9 = bf16[4,32,4096]{2,1,0:T(8,128)(2,1)S(1)} copy-done((bf16[4,32,4096]{2,1,0:T(8,128)(2,1)S(1)}, bf16[4,32,4096]{2,1,0:T(8,128)(2,1)}, u32[]{:S(2)}) %copy-start.9) | copy-done | bytes 1048600
  37.5 5.6 %home.1 = (f32[2,2048,128]{2,1,0:T(8,128)S(1)}, f32[2,8,32,16,128]{4,3,2,1,0:T(8,128)S(1)}) custom-call(f32[1,512]{1,0:T(1,128)S(1)} %bitcast.10, bf16[512,512]{1,0:T(8,128)(2,1)S(1)} %constant_dynamic-slice_fusion.1.wz_ref, bf16[512,32]{1,0:T(8,128)(2,1)S(1)} %copy.20.wm_ref, bf16[64,64]{1,0:T(8,128)(2,1)S(1)} %copy-done.10, ...), custom_call_target="tpu_custom_call" | custom-call | flops 1073741824 | bytes 8388608 | tf_op jit(solution)/shard_map/home/pallas_call | solution.py:230
  43.1 1.9 %copy-done.1 = f32[2,8,32,16,128]{4,3,2,1,0:T(8,128)} copy-done((f32[2,8,32,16,128]{4,3,2,1,0:T(8,128)}, f32[2,8,32,16,128]{4,3,2,1,0:T(8,128)S(1)}, u32[]{:S(2)}) %copy-start.1) | copy-done | bytes 4194328
  45.0 1.3 %copy-done.3 = f32[2,2048,128]{2,1,0:T(8,128)} copy-done((f32[2,2048,128]{2,1,0:T(8,128)}, f32[2,2048,128]{2,1,0:T(8,128)S(1)}, u32[]{:S(2)}) %copy-start.3) | copy-done | bytes 2097176
  46.4 11.7 %all-to-all-done.1.y_hbm = bf16[16,2,128,128]{3,2,1,0:T(8,128)(2,1)} async-done(((bf16[16,2,128,128]{3,2,1,0:T(8,128)(2,1)}), bf16[16,2,128,128]{3,2,1,0:T(8,128)(2,1)}, u32[]{:S(2)}, u32[]{:S(2)}) %all-to-all-start.1) | async-done | bytes 1048608 | tf_op jit(solution)/shard_map/all_to_all | solution.py:447
  58.1 8.7 %col_scan.1 = (bf16[8,256,128]{2,1,0:T(8,128)(2,1)}, bf16[8,256,128]{2,1,0:T(8,128)(2,1)}) custom-call(s32[1]{0:T(128)} %bitcast.1.core_ref.group_ref, bf16[16,2,128,128]{3,2,1,0:T(8,128)(2,1)} %all-to-all-done.1.y_hbm, f32[2,128,16,128]{3,2,1,0:T(8,128)} %bitcast.7, f32[2,8,32,16,128]{4,3,2,1,0:T(8,128)} %copy-done.1, f32[16,16,128]{2,1,0:T(8,128)} %tile.12.rate_hbm), custom_call_target="tpu_custom_call" | custom-call | flops 41943040 | bytes 8388608 | tf_op jit(solution)/shard_map/col_scan/pallas_call | solution.py:338
  66.8 0.9 %collective-permute-start.1 = (bf16[8,256,128]{2,1,0:T(8,128)(2,1)}, bf16[8,256,128]{2,1,0:T(8,128)(2,1)S(1)}, u32[]{:S(2)}, u32[]{:S(2)}) collective-permute-start(bf16[8,256,128]{2,1,0:T(8,128)(2,1)} %get-tuple-element.11), channel_id=1, source_target_pairs={{0,1},{1,0},{2,3},{3,2},{4,5},{5,4},{6,7},{7,6},{8,9},{9,8},{10,11... | collective-permute-start | bytes 1572872 | tf_op jit(solution)/shard_map/ppermute | solution.py:465
  67.7 1.0 %copy-done.5 = bf16[8,256,128]{2,1,0:T(8,128)(2,1)S(1)} copy-done((bf16[8,256,128]{2,1,0:T(8,128)(2,1)S(1)}, bf16[8,256,128]{2,1,0:T(8,128)(2,1)}, u32[]{:S(2)}) %copy-start.5) | copy-done | bytes 524312
  68.8 0.7 %last.2.refs_0_ = f32[512,512]{1,0:T(8,128)S(1)} custom-call(s32[1]{0:T(128)} %bitcast.1.core_ref.group_ref, bf16[8,256,128]{2,1,0:T(8,128)(2,1)S(1)} %copy-done.5, bf16[1024,512]{1,0:T(8,128)(2,1)S(1)} %copy-done.2, bf16[512,512]{1,0:T(8,128)(2,1)S(1)} %copy-done.4), custom_call_target="tpu_custom_call" | custom-call | flops 268435456 | bytes 2097152 | tf_op jit(solution)/shard_map/last/pallas_call | solution.py:391
  69.5 1.6 %last.3 = bf16[128,4,512]{2,1,0:T(4,128)(2,1)} custom-call(s32[1]{0:T(128)} %bitcast.group_ref, bf16[8,256,128]{2,1,0:T(8,128)(2,1)S(1)} %collective-permute-done.1.part_ref, bf16[1024,512]{1,0:T(8,128)(2,1)S(1)} %copy-done.2, bf16[512,512]{1,0:T(8,128)(2,1)S(1)} %copy-done.4, f32[512,512]{1,0:T(8,128)S(1)} %last.2.refs_0_), custom_call_target="tpu_custom_call" | custom-call | flops 268435456 | bytes 2097152 | tf_op jit(solution)/shard_map/last/pallas_call | solution.py:391
  (23 shorter events, 0.1 us)
Async XLA Ops:
  0.0 34.0 %copy-start = (f32[16,1024]{1,0:T(8,128)S(1)}, f32[16,1024]{1,0:T(8,128)}, u32[]{:S(2)}) copy-start(f32[16,1024]{1,0:T(8,128)} %param.19) | copy-start | bytes 196612
  0.0 8.0 %copy-start.12 = (bf16[512,64]{0,1:T(8,128)(2,1)S(1)}, bf16[512,64]{0,1:T(8,128)(2,1)}, u32[]{:S(2)}) copy-start(bf16[512,64]{0,1:T(8,128)(2,1)} %param.17) | copy-start | bytes 196612
  0.0 19.8 %all-to-all-start = ((bf16[16,8,4,512]{3,2,1,0:T(4,128)(2,1)}), bf16[16,8,4,512]{3,2,1,0:T(4,128)(2,1)S(1)}, u32[]{:S(2)}, u32[]{:S(2)}) async-start(bf16[16,8,4,512]{3,2,1,0:T(4,128)(2,1)} %bitcast.11), calls=%async_computation | async-start | bytes 1048576 | tf_op jit(solution)/shard_map/all_to_all | solution.py:439
  6.6 13.3 %copy-start.4 = (bf16[512,512]{1,0:T(8,128)(2,1)S(1)}, bf16[512,512]{1,0:T(8,128)(2,1)}, u32[]{:S(2)}) copy-start(bf16[512,512]{1,0:T(8,128)(2,1)} %constant.36.clone.lane_ref) | copy-start | bytes 1572868
  6.6 13.3 %copy-start.6 = (f32[16,1024]{1,0:T(8,128)S(1)}, f32[16,1024]{1,0:T(8,128)}, u32[]{:S(2)}) copy-start(f32[16,1024]{1,0:T(8,128)} %rate_ref.1) | copy-start | bytes 196612
  6.6 13.3 %copy-start.7 = (f32[1024]{0:T(1024)S(1)}, f32[1024]{0:T(1024)}, u32[]{:S(2)}) copy-start(f32[1024]{0:T(1024)} %param.20) | copy-start | bytes 12292
  6.6 13.3 %copy-start.8 = (f32[512]{0:T(512)S(1)}, f32[512]{0:T(512)}, u32[]{:S(2)}) copy-start(f32[512]{0:T(512)} %param.15) | copy-start | bytes 6148
  27.7 5.7 %copy-start.11 = (bf16[128,4,512]{2,1,0:T(4,128)(2,1)S(1)}, bf16[128,4,512]{2,1,0:T(4,128)(2,1)}, u32[]{:S(2)}) copy-start(bf16[128,4,512]{2,1,0:T(4,128)(2,1)} %param.14) | copy-start | bytes 1572868
  27.7 6.2 %slice-start = ((bf16[512,64]{0,1:T(8,128)(2,1)}), bf16[512,32]{0,1:T(8,128)(2,1)S(1)}, s32[]{:S(2)}) async-start(bf16[512,64]{0,1:T(8,128)(2,1)} %param.17), calls=%async_computation.2 | async-start | bytes 65536 | tf_op jit(solution)/shard_map/slice | solution.py:455
  27.7 30.4 %all-to-all-start.1 = ((bf16[16,2,128,128]{3,2,1,0:T(8,128)(2,1)}), bf16[16,2,128,128]{3,2,1,0:T(8,128)(2,1)}, u32[]{:S(2)}, u32[]{:S(2)}) async-start(bf16[16,2,128,128]{3,2,1,0:T(8,128)(2,1)} %bitcast.5), calls=%async_computation.1 | async-start | bytes 2097152 | tf_op jit(solution)/shard_map/all_to_all | solution.py:447
  33.3 3.0 %copy-start.10 = (bf16[64,64]{1,0:T(8,128)(2,1)S(1)}, bf16[64,64]{1,0:T(8,128)(2,1)}, u32[]{:S(2)}) copy-start(bf16[64,64]{1,0:T(8,128)(2,1)} %constant.37.clone.order_ref) | copy-start | bytes 24580
  33.5 2.8 %collective-permute-start = (bf16[512,512]{1,0:T(8,128)(2,1)S(1)}, bf16[512,512]{1,0:T(8,128)(2,1)S(1)}, u32[]{:S(2)}, u32[]{:S(2)}) collective-permute-start(bf16[512,512]{1,0:T(8,128)(2,1)S(1)} %reshape.31.refs_0_), channel_id=1, source_target_pairs={{0,1},{1,0},{2,3},{3,2},{4,5},{5,4},{6,7},{7,6},{8,9},{9,8},{10,11... | collective-permute-start | bytes 1572872 | tf_op jit(solution)/shard_map/ppermute | solution.py:451
  36.3 1.2 %copy-start.9 = (bf16[4,32,4096]{2,1,0:T(8,128)(2,1)S(1)}, bf16[4,32,4096]{2,1,0:T(8,128)(2,1)}, u32[]{:S(2)}) copy-start(bf16[4,32,4096]{2,1,0:T(8,128)(2,1)} %constant.38.clone.table_ref) | copy-start | bytes 3145732
  43.1 1.9 %copy-start.1 = (f32[2,8,32,16,128]{4,3,2,1,0:T(8,128)}, f32[2,8,32,16,128]{4,3,2,1,0:T(8,128)S(1)}, u32[]{:S(2)}) copy-start(f32[2,8,32,16,128]{4,3,2,1,0:T(8,128)S(1)} %get-tuple-element.10.mix_hbm) | copy-start | bytes 12582916
  45.0 1.3 %copy-start.3 = (f32[2,2048,128]{2,1,0:T(8,128)}, f32[2,2048,128]{2,1,0:T(8,128)S(1)}, u32[]{:S(2)}) copy-start(f32[2,2048,128]{2,1,0:T(8,128)S(1)} %get-tuple-element.9) | copy-start | bytes 6291460
  58.1 9.6 %copy-start.2 = (bf16[1024,512]{1,0:T(8,128)(2,1)S(1)}, bf16[1024,512]{1,0:T(8,128)(2,1)}, u32[]{:S(2)}) copy-start(bf16[1024,512]{1,0:T(8,128)(2,1)} %w_ref.3) | copy-start | bytes 3145732
  66.8 2.7 %collective-permute-start.1 = (bf16[8,256,128]{2,1,0:T(8,128)(2,1)}, bf16[8,256,128]{2,1,0:T(8,128)(2,1)S(1)}, u32[]{:S(2)}, u32[]{:S(2)}) collective-permute-start(bf16[8,256,128]{2,1,0:T(8,128)(2,1)} %get-tuple-element.11), channel_id=1, source_target_pairs={{0,1},{1,0},{2,3},{3,2},{4,5},{5,4},{6,7},{7,6},{8,9},{9,8},{10,11... | collective-permute-start | bytes 1572872 | tf_op jit(solution)/shard_map/ppermute | solution.py:465
  67.7 1.0 %copy-start.5 = (bf16[8,256,128]{2,1,0:T(8,128)(2,1)S(1)}, bf16[8,256,128]{2,1,0:T(8,128)(2,1)}, u32[]{:S(2)}) copy-start(bf16[8,256,128]{2,1,0:T(8,128)(2,1)} %get-tuple-element.12.part_ref) | copy-start | bytes 1572868

commit v5 on v4

--- a/solution.py
+++ b/solution.py
@@ -12,7 +12,8 @@
 BF16 = jnp.bfloat16
 VMEM = pl.BlockSpec(memory_space=pltpu.VMEM)
 LANES = 128
-AHEAD = 3
+AHEAD = 8
+SPAN = 16
 
 
 def normalise(tokens, gain):
@@ -88,15 +89,14 @@
         source = first - lag * items
         product = c_scr[first:first + count, :] * b_scr[source:source + count, :]
         g_scr[at:at + count, :] = product.astype(BF16)
-    few = items // halves
     pieces_out = out_scr.shape[1]
     tiles_each = tile // LANES // pieces_out
-    rows_each = out_scr.shape[4]
+    rows_each = out_scr.shape[3]
 
     def send(tile_id, piece):
         return pltpu.make_async_copy(
             out_scr.at[tile_id, piece],
-            out_hbm.at[:, tile_id, :, pl.ds(piece * rows_each, rows_each), :],
+            out_hbm.at[:, tile_id, pl.ds(piece * rows_each, rows_each), :],
             sems.at[tile_id, piece],
         )
 
@@ -134,14 +134,13 @@
             turned = dot(l_scr[...], lane_ref[:, k * LANES:(k + 2) * LANES])
             for at in range(tile // LANES):
                 piece, first = divmod(at, tiles_each)
-                begin = (first * columns + k) * few
+                begin = (first * columns + k) * items
                 for part in range(parts):
-                    for own in range(halves):
-                        rows_at = at * tall + part * items + own * few
-                        pair = jnp.concatenate(
-                            [turned[rows_at:rows_at + few, j * LANES:(j + 1) * LANES] for j in range(2)], axis=0
+                    rows_at = at * tall + part * items
+                    for j in range(2):
+                        out_scr[tile_id, piece, part, begin + j * items:begin + (j + 1) * items, :] = (
+                            turned[rows_at:rows_at + items, j * LANES:(j + 1) * LANES].astype(BF16)
                         )
-                        out_scr[tile_id, piece, part, own, begin:begin + 2 * few, :] = pair.astype(BF16)
         for piece in range(pieces_out):
             send(tile_id, piece).start()
 
@@ -162,12 +161,12 @@
     blank = jnp.zeros((width, LANES - 2 * state), BF16)
     w_mix = jnp.concatenate([w_b, w_b, blank, w_c, w_c, blank], axis=1)
     tile = inner // halves
-    out_rows = tile * columns // LANES * (items // halves)
+    out_rows = tile * columns // LANES * items
     pieces_out = 2
     out = pl.pallas_call(
         functools.partial(row_kernel, parts, items, columns, halves),
         name="row_scan",
-        out_shape=jax.ShapeDtypeStruct((parts, halves, halves, out_rows, LANES), BF16),
+        out_shape=jax.ShapeDtypeStruct((parts, halves, out_rows, LANES), BF16),
         in_specs=[VMEM] * 7,
         out_specs=pl.BlockSpec(memory_space=pltpu.HBM),
         scratch_shapes=[
@@ -178,7 +177,7 @@
             pltpu.VMEM((halves, rows, tile), F32),
             pltpu.VMEM((rows * (parts * columns + 1) // 2, 2 * state), BF16),
             pltpu.VMEM((halves, parts * items * tile // LANES, columns * LANES), BF16),
-            pltpu.VMEM((halves, pieces_out, parts, halves, out_rows // pieces_out, LANES), BF16),
+            pltpu.VMEM((halves, pieces_out, parts, out_rows // pieces_out, LANES), BF16),
             pltpu.VMEM((width // LANES, rows, LANES), F32),
             pltpu.SemaphoreType.DMA((halves, pieces_out)),
         ],
@@ -187,7 +186,7 @@
             flops=2 * rows * width * inner * 16, bytes_accessed=4 << 20, transcendentals=0
         ),
     )(x, gain[None, :], w_u, w_mix, rate, skip[None, :], lane_order(columns))
-    return out.reshape(parts * halves, halves, out_rows, LANES)
+    return out.reshape(parts * halves, out_rows, LANES)
 
 
 def home_kernel(columns, halves, gain_ref, wz_ref, wm_ref, order_ref, lane_ref, table_ref, *refs):
@@ -251,8 +250,6 @@
     per_half, _, span_steps, _ = mix_hbm.shape[1:]
     count = halves * per_half
     groups = gate_hbm.shape[2]
-    take = y_hbm.shape[0] // per_half
-    items = span_steps // take
     tiles = groups // 8
     spans = [slice(f * 8, f * 8 + 8) for f in range(tiles)]
 
@@ -263,7 +260,7 @@
         half, place, slot = at // per_half, at % per_half, slot_of(at)
         first = pl.multiple_of(place * span_steps, span_steps)
         return (
-            pltpu.make_async_copy(y_hbm.at[pl.ds(place * take, take), half], y_ref.at[at], sems.at[at, 0]),
+            pltpu.make_async_copy(y_hbm.at[place * halves + half], y_ref.at[at], sems.at[at, 0]),
             pltpu.make_async_copy(mix_hbm.at[slot, place], mix_ref.at[at], sems.at[at, 1]),
             pltpu.make_async_copy(gate_hbm.at[slot, pl.ds(first, span_steps)], gate_ref.at[at], sems.at[at, 2]),
         )
@@ -291,12 +288,10 @@
         def _():
             launch(at + AHEAD, 0)
 
-        for k in range(take):
-            v_scr[k * groups * items:(k + 1) * groups * items, :] = y_ref[at, k].astype(F32)
+        v_scr[...] = y_ref[at].astype(F32)
         carry = [held[n, span, :] for n in range(state) for span in spans]
         for t in range(span_steps):
-            k, i = divmod(t, items)
-            value = [v_scr[pl.ds((k * groups + f * 8) * items + i, 8, stride=items), :] for f in range(tiles)]
+            value = [v_scr[pl.ds(f * 8 * span_steps + t, 8, stride=span_steps), :] for f in range(tiles)]
             total = list(value)
             for n in range(state):
                 b = jnp.broadcast_to(mix_ref[at, n, t:t + 1, :], (8, LANES))
@@ -330,9 +325,8 @@
 
 
 def col_scan(core, y, gate, mix, rate):
-    sources, halves, rows, _ = y.shape
     state, groups, _ = rate.shape
-    per_half, _, span_steps, _ = mix.shape[1:]
+    halves, per_half, _, span_steps, _ = mix.shape
     count = halves * per_half
     far = pl.BlockSpec(memory_space=pltpu.HBM)
     return pl.pallas_call(
@@ -341,7 +335,7 @@
         in_specs=[pl.BlockSpec(memory_space=pltpu.SMEM)] + [far] * 4,
         out_specs=[far] * halves,
         scratch_shapes=[
-            pltpu.VMEM((count, sources // per_half, rows, LANES), BF16),
+            pltpu.VMEM((count, groups * span_steps, LANES), BF16),
             pltpu.VMEM((count, span_steps, groups, LANES), F32),
             pltpu.VMEM((count, 2 * state, span_steps, LANES), F32),
             pltpu.VMEM((count, groups * span_steps, LANES), BF16),
@@ -421,8 +415,8 @@
     start = jnp.zeros((items, state, inner), F32)
     _, out = lax.scan(advance, start, (value, mix[..., :state], mix[..., state:2 * state]))
     lanes = LANES // columns
-    out = out.astype(BF16).reshape(parts, columns, halves, items // halves, halves, inner // (halves * lanes), lanes)
-    return out.transpose(0, 4, 2, 5, 3, 1, 6).reshape(parts * halves, halves, -1, LANES)
+    out = out.astype(BF16).reshape(parts, columns, items, halves, inner // (halves * lanes), lanes)
+    return out.transpose(0, 3, 4, 2, 1, 5).reshape(parts * halves, -1, LANES)
 
 
 def per_device(tokens, norm_gain, w_in, w_bc, rate_row, rate_col, skip_gain, w_out):
@@ -432,16 +426,15 @@
     parts, halves = lax.axis_size("rows"), lax.axis_size("cols")
     core = lax.axis_index("cols")
     both = ("rows", "cols")
-    sources = parts * halves
-    items = height // sources
+    items = height // parts
     group = inner // halves
     lanes = LANES // columns
     moved = lax.all_to_all(
-        tokens.reshape(sources, items, columns, features), both, split_axis=0, concat_axis=0, tiled=True
+        tokens.reshape(parts, items, columns, features), "rows", split_axis=0, concat_axis=0, tiled=True
     )
-    scan = row_scan if items * halves % 8 == 0 and parts * columns <= 64 else wide_row_scan
+    scan = row_scan if items == SPAN and parts * columns <= 64 else wide_row_scan
     row_mixed = scan(
-        moved.reshape(parts, halves * items * columns, features), columns, halves, norm_gain,
+        moved.reshape(parts, items * columns, features), columns, halves, norm_gain,
         w_in[:, :inner], w_bc[:, :2 * state], rate_row, skip_gain
     )
     back = lax.all_to_all(row_mixed, both, split_axis=0, concat_axis=0, tiled=True)
@@ -452,13 +445,13 @@
     ]
     own = core * group
     w_gate = lax.dynamic_slice_in_dim(w_in, inner + own, group, 1)
-    gate, mix = home(whole, 16, columns, norm_gain, w_gate, w_bc[:, 2 * state:])
+    gate, mix = home(whole, SPAN, columns, norm_gain, w_gate, w_bc[:, 2 * state:])
     rate = lax.dynamic_slice_in_dim(rate_col, own, group, 1)
     rate = jnp.tile(rate.reshape(state, group // lanes, lanes), (1, 1, columns))
-    if items % 8 != 0:
-        blocks = max(1, height // 16)
-        back = back.reshape(blocks, sources // blocks, halves, group // lanes, items, LANES)
-        back = back.transpose(0, 2, 3, 1, 4, 5).reshape(blocks, halves, -1, LANES)
+    if items != SPAN:
+        spans = height // SPAN
+        back = back.reshape(spans, parts // spans, halves, group // lanes, items, LANES)
+        back = back.transpose(0, 2, 3, 1, 4, 5).reshape(spans * halves, -1, LANES)
     gated = col_scan(core.reshape(1), back, gate, mix, rate)
     out = last(core, gated[0], w_out, columns, halves, None, BF16 if halves == 1 else F32)
     for s in range(1, halves):

time: 71.6 us -> 71.4 us (level)
  waiting for transfers between devices: 22.9 us -> 22.1 us
    all_to_all x1, starting transfers between devices: 5.63 us -> 7.26 us  [per_device(): lax.all_to_all(row_mixed, both, split_axis=0, concat_axis=0, tiled=True)]
    all_to_all x1, starting transfers between devices: 6.6 us -> 5.71 us  [per_device(): lax.all_to_all(tokens.reshape(parts, items, columns, features), 'rows', s...]
    all_to_all x1, waiting for transfers between devices: 11.2 us -> 10.4 us  [per_device(): lax.all_to_all(tokens.reshape(parts, items, columns, features), 'rows', s...]
where the time goes in v5:
time: 71.4 us; the launch traced here: 70.9 us
  Pallas kernels  24.1 us (34%)
  waiting for transfers between devices  22.1 us (31%)
  starting transfers between devices  14.3 us (20%)
  local copies, waits for them, and re-layouts  10 us (14%)
    all_to_all x1, waiting for transfers between devices, per_device(): lax.all_to_all(row_mixed, both, split_axis=0, concat_axis=0, tiled=True)  11.7 us
    all_to_all x1, waiting for transfers between devices, per_device(): lax.all_to_all(tokens.reshape(parts, items, columns, features), 'rows', s...  10.4 us
    pallas_call x1, Pallas kernels, col_scan(): pl.pallas_call(functools.partial(col_kernel, state, halves), name='col_sc...  8.91 us
    pallas_call x1, Pallas kernels, row_scan(): pl.pallas_call(functools.partial(row_kernel, parts, items, columns, halve...  7.4 us
    all_to_all x1, starting transfers between devices, per_device(): lax.all_to_all(row_mixed, both, split_axis=0, concat_axis=0, tiled=True)  7.26 us
    all_to_all x1, starting transfers between devices, per_device(): lax.all_to_all(tokens.reshape(parts, items, columns, features), 'rows', s...  5.71 us
    unnamed x27, local copies, waits for them, and re-layouts  5.69 us
    pallas_call x1, Pallas kernels, home(): pl.pallas_call(functools.partial(home_kernel, columns, halves), name='hom...  5.55 us
  transfers between devices with their start and end apart: 4, of which 2 were waited for; matrix products, arithmetic and copies ran while one was open for 6% of the time, Pallas kernels for 9%

profile of v5, /device:TPU:17, one launch (start us, length us, event | category | flops | bytes accessed | tf_op | source)
XLA Modules:
  0.0 70.9 jit_solution(7232836946397339716)
XLA Ops:
  0.0 5.7 %all-to-all-start = ((bf16[8,16,4,512]{3,2,1,0:T(4,128)(2,1)}), bf16[8,16,4,512]{3,2,1,0:T(4,128)(2,1)S(1)}, u32[]{:S(2)}, u32[]{:S(2)}) async-start(bf16[8,16,4,512]{3,2,1,0:T(4,128)(2,1)} %bitcast.11), calls=%async_computation | async-start | bytes 1048576 | tf_op jit(solution)/shard_map/all_to_all | solution.py:432
  5.7 0.0 copy-start.8
  5.7 1.4 %slice.15.wu_ref = bf16[512,1024]{1,0:T(8,128)(2,1)S(1)} slice(bf16[512,2048]{1,0:T(8,128)(2,1)} %param.16), slice={[0:512], [0:1024]} | slice | bytes 2097152 | tf_op jit(solution)/shard_map/slice | solution.py:438
  7.1 0.1 copy.15
  7.2 0.1 copy.17
  7.4 0.3 concatenate.3.wbc_ref
  7.7 10.4 %all-to-all-done = bf16[8,16,4,512]{3,2,1,0:T(4,128)(2,1)S(1)} async-done(((bf16[8,16,4,512]{3,2,1,0:T(4,128)(2,1)}), bf16[8,16,4,512]{3,2,1,0:T(4,128)(2,1)S(1)}, u32[]{:S(2)}, u32[]{:S(2)}) %all-to-all-start) | async-done | bytes 524320 | tf_op jit(solution)/shard_map/all_to_all | solution.py:432
  18.1 0.1 reshape.29.x_ref
  18.2 7.4 %row_scan.1 = bf16[8,2,256,128]{3,2,1,0:T(8,128)(2,1)} custom-call(bf16[8,64,512]{2,1,0:T(8,128)(2,1)S(1)} %reshape.29.x_ref, f32[1,512]{1,0:T(1,128)S(1)} %bitcast.9, bf16[512,1024]{1,0:T(8,128)(2,1)S(1)} %slice.15.wu_ref, bf16[512,256]{1,0:T(8,128)(2,1)S(1)} %concatenate.3.wbc_ref, f32[16,1024]{1,0:T(8,128)S(1)} %copy-done.6, f32[1,1024]{1,0:T(1,128)S(1)} %bitcast.8, ...), custom_call_target="tpu_custom_call" | custom-call | flops 8589934592 | bytes 4194304 | tf_op jit(solution)/shard_map/row_scan/pallas_call | solution.py:166
  25.7 0.0 copy-start.11
  25.7 0.0 slice-start
  25.7 7.3 %all-to-all-start.1 = ((bf16[16,256,128]{2,1,0:T(8,128)(2,1)}), bf16[16,256,128]{2,1,0:T(8,128)(2,1)}, u32[]{:S(2)}, u32[]{:S(2)}) async-start(bf16[16,256,128]{2,1,0:T(8,128)(2,1)} %bitcast.5), calls=%async_computation.1 | async-start | bytes 2097152 | tf_op jit(solution)/shard_map/all_to_all | solution.py:440
  32.9 0.0 copy-start.10
  33.0 0.1 reshape.31.refs_0_
  33.1 0.4 collective-permute-start
  33.5 0.1 copy.20.wm_ref
  33.7 0.1 tile.10
  33.8 0.1 tile.11
  33.9 0.9 %tile.12.rate_hbm = f32[16,16,128]{2,1,0:T(8,128)} reshape(f32[16,16,4,32]{3,2,1,0:T(4,128)S(1)} %tile.11) | data formatting | bytes 262144 | tf_op jit(solution)/shard_map/tile | solution.py:450
  34.8 1.1 %constant_dynamic-slice_fusion.1.wz_ref = bf16[512,512]{1,0:T(8,128)(2,1)S(1)} fusion(bf16[512,2048]{1,0:T(8,128)(2,1)} %param.16, s32[]{:T(128)S(6)} %select_n.14), kind=kLoop, calls=%fused_computation.1 | loop fusion | bytes 1048580 | tf_op jit(solution)/shard_map/dynamic_slice | solution.py:447
  35.9 0.0 collective-permute-done.refs_1_
  35.9 0.0 copy-start.9
  35.9 1.2 %copy-done.9 = bf16[4,32,4096]{2,1,0:T(8,128)(2,1)S(1)} copy-done((bf16[4,32,4096]{2,1,0:T(8,128)(2,1)S(1)}, bf16[4,32,4096]{2,1,0:T(8,128)(2,1)}, u32[]{:S(2)}) %copy-start.9) | copy-done | bytes 1048600
  37.1 5.5 %home.1 = (f32[2,2048,128]{2,1,0:T(8,128)S(1)}, f32[2,8,32,16,128]{4,3,2,1,0:T(8,128)S(1)}) custom-call(f32[1,512]{1,0:T(1,128)S(1)} %bitcast.10, bf16[512,512]{1,0:T(8,128)(2,1)S(1)} %constant_dynamic-slice_fusion.1.wz_ref, bf16[512,32]{1,0:T(8,128)(2,1)S(1)} %copy.20.wm_ref, bf16[64,64]{1,0:T(8,128)(2,1)S(1)} %copy-done.10, ...), custom_call_target="tpu_custom_call" | custom-call | flops 1073741824 | bytes 8388608 | tf_op jit(solution)/shard_map/home/pallas_call | solution.py:229
  42.7 1.9 %copy-done.1 = f32[2,8,32,16,128]{4,3,2,1,0:T(8,128)} copy-done((f32[2,8,32,16,128]{4,3,2,1,0:T(8,128)}, f32[2,8,32,16,128]{4,3,2,1,0:T(8,128)S(1)}, u32[]{:S(2)}) %copy-start.1) | copy-done | bytes 4194328
  44.6 1.3 %copy-done.3 = f32[2,2048,128]{2,1,0:T(8,128)} copy-done((f32[2,2048,128]{2,1,0:T(8,128)}, f32[2,2048,128]{2,1,0:T(8,128)S(1)}, u32[]{:S(2)}) %copy-start.3) | copy-done | bytes 2097176
  46.0 11.7 %all-to-all-done.1.y_hbm = bf16[16,256,128]{2,1,0:T(8,128)(2,1)} async-done(((bf16[16,256,128]{2,1,0:T(8,128)(2,1)}), bf16[16,256,128]{2,1,0:T(8,128)(2,1)}, u32[]{:S(2)}, u32[]{:S(2)}) %all-to-all-start.1) | async-done | bytes 1048608 | tf_op jit(solution)/shard_map/all_to_all | solution.py:440
  57.7 8.9 %col_scan.1 = (bf16[8,256,128]{2,1,0:T(8,128)(2,1)}, bf16[8,256,128]{2,1,0:T(8,128)(2,1)}) custom-call(s32[1]{0:T(128)} %bitcast.1.core_ref.group_ref, bf16[16,256,128]{2,1,0:T(8,128)(2,1)} %all-to-all-done.1.y_hbm, f32[2,128,16,128]{3,2,1,0:T(8,128)} %bitcast.7, f32[2,8,32,16,128]{4,3,2,1,0:T(8,128)} %copy-done.1, f32[16,16,128]{2,1,0:T(8,128)} %tile.12.rate_hbm), custom_call_target="tpu_custom_call" | custom-call | flops 41943040 | bytes 8388608 | tf_op jit(solution)/shard_map/col_scan/pallas_call | solution.py:332
  66.6 0.9 %collective-permute-start.1 = (bf16[8,256,128]{2,1,0:T(8,128)(2,1)}, bf16[8,256,128]{2,1,0:T(8,128)(2,1)S(1)}, u32[]{:S(2)}, u32[]{:S(2)}) collective-permute-start(bf16[8,256,128]{2,1,0:T(8,128)(2,1)} %get-tuple-element.11), channel_id=1, source_target_pairs={{0,1},{1,0},{2,3},{3,2},{4,5},{5,4},{6,7},{7,6},{8,9},{9,8},{10,11... | collective-permute-start | bytes 1572872 | tf_op jit(solution)/shard_map/ppermute | solution.py:458
  67.6 1.0 %copy-done.5 = bf16[8,256,128]{2,1,0:T(8,128)(2,1)S(1)} copy-done((bf16[8,256,128]{2,1,0:T(8,128)(2,1)S(1)}, bf16[8,256,128]{2,1,0:T(8,128)(2,1)}, u32[]{:S(2)}) %copy-start.5) | copy-done | bytes 524312
  68.6 0.7 %last.2.refs_0_ = f32[512,512]{1,0:T(8,128)S(1)} custom-call(s32[1]{0:T(128)} %bitcast.1.core_ref.group_ref, bf16[8,256,128]{2,1,0:T(8,128)(2,1)S(1)} %copy-done.5, bf16[1024,512]{1,0:T(8,128)(2,1)S(1)} %copy-done.2, bf16[512,512]{1,0:T(8,128)(2,1)S(1)} %copy-done.4), custom_call_target="tpu_custom_call" | custom-call | flops 268435456 | bytes 2097152 | tf_op jit(solution)/shard_map/last/pallas_call | solution.py:385
  69.3 1.6 %last.3 = bf16[128,4,512]{2,1,0:T(4,128)(2,1)} custom-call(s32[1]{0:T(128)} %bitcast.group_ref, bf16[8,256,128]{2,1,0:T(8,128)(2,1)S(1)} %collective-permute-done.1.part_ref, bf16[1024,512]{1,0:T(8,128)(2,1)S(1)} %copy-done.2, bf16[512,512]{1,0:T(8,128)(2,1)S(1)} %copy-done.4, f32[512,512]{1,0:T(8,128)S(1)} %last.2.refs_0_), custom_call_target="tpu_custom_call" | custom-call | flops 268435456 | bytes 2097152 | tf_op jit(solution)/shard_map/last/pallas_call | solution.py:385
  (23 shorter events, 0.1 us)
Async XLA Ops:
  0.0 33.7 %copy-start = (f32[16,1024]{1,0:T(8,128)S(1)}, f32[16,1024]{1,0:T(8,128)}, u32[]{:S(2)}) copy-start(f32[16,1024]{1,0:T(8,128)} %param.19) | copy-start | bytes 196612
  0.0 7.1 %copy-start.12 = (bf16[512,64]{0,1:T(8,128)(2,1)S(1)}, bf16[512,64]{0,1:T(8,128)(2,1)}, u32[]{:S(2)}) copy-start(bf16[512,64]{0,1:T(8,128)(2,1)} %param.17) | copy-start | bytes 196612
  0.0 18.1 %all-to-all-start = ((bf16[8,16,4,512]{3,2,1,0:T(4,128)(2,1)}), bf16[8,16,4,512]{3,2,1,0:T(4,128)(2,1)S(1)}, u32[]{:S(2)}, u32[]{:S(2)}) async-start(bf16[8,16,4,512]{3,2,1,0:T(4,128)(2,1)} %bitcast.11), calls=%async_computation | async-start | bytes 1048576 | tf_op jit(solution)/shard_map/all_to_all | solution.py:432
  5.7 12.5 %copy-start.4 = (bf16[512,512]{1,0:T(8,128)(2,1)S(1)}, bf16[512,512]{1,0:T(8,128)(2,1)}, u32[]{:S(2)}) copy-start(bf16[512,512]{1,0:T(8,128)(2,1)} %constant.36.clone.lane_ref) | copy-start | bytes 1572868
  5.7 12.5 %copy-start.6 = (f32[16,1024]{1,0:T(8,128)S(1)}, f32[16,1024]{1,0:T(8,128)}, u32[]{:S(2)}) copy-start(f32[16,1024]{1,0:T(8,128)} %rate_ref.1) | copy-start | bytes 196612
  5.7 12.5 %copy-start.7 = (f32[1024]{0:T(1024)S(1)}, f32[1024]{0:T(1024)}, u32[]{:S(2)}) copy-start(f32[1024]{0:T(1024)} %param.20) | copy-start | bytes 12292
  5.7 12.5 %copy-start.8 = (f32[512]{0:T(512)S(1)}, f32[512]{0:T(512)}, u32[]{:S(2)}) copy-start(f32[512]{0:T(512)} %param.15) | copy-start | bytes 6148
  25.7 7.3 %copy-start.11 = (bf16[128,4,512]{2,1,0:T(4,128)(2,1)S(1)}, bf16[128,4,512]{2,1,0:T(4,128)(2,1)}, u32[]{:S(2)}) copy-start(bf16[128,4,512]{2,1,0:T(4,128)(2,1)} %param.14) | copy-start | bytes 1572868
  25.7 7.8 %slice-start = ((bf16[512,64]{0,1:T(8,128)(2,1)}), bf16[512,32]{0,1:T(8,128)(2,1)S(1)}, s32[]{:S(2)}) async-start(bf16[512,64]{0,1:T(8,128)(2,1)} %param.17), calls=%async_computation.2 | async-start | bytes 65536 | tf_op jit(solution)/shard_map/slice | solution.py:448
  25.7 32.0 %all-to-all-start.1 = ((bf16[16,256,128]{2,1,0:T(8,128)(2,1)}), bf16[16,256,128]{2,1,0:T(8,128)(2,1)}, u32[]{:S(2)}, u32[]{:S(2)}) async-start(bf16[16,256,128]{2,1,0:T(8,128)(2,1)} %bitcast.5), calls=%async_computation.1 | async-start | bytes 2097152 | tf_op jit(solution)/shard_map/all_to_all | solution.py:440
  32.9 3.0 %copy-start.10 = (bf16[64,64]{1,0:T(8,128)(2,1)S(1)}, bf16[64,64]{1,0:T(8,128)(2,1)}, u32[]{:S(2)}) copy-start(bf16[64,64]{1,0:T(8,128)(2,1)} %constant.37.clone.order_ref) | copy-start | bytes 24580
  33.1 2.8 %collective-permute-start = (bf16[512,512]{1,0:T(8,128)(2,1)S(1)}, bf16[512,512]{1,0:T(8,128)(2,1)S(1)}, u32[]{:S(2)}, u32[]{:S(2)}) collective-permute-start(bf16[512,512]{1,0:T(8,128)(2,1)S(1)} %reshape.31.refs_0_), channel_id=1, source_target_pairs={{0,1},{1,0},{2,3},{3,2},{4,5},{5,4},{6,7},{7,6},{8,9},{9,8},{10,11... | collective-permute-start | bytes 1572872 | tf_op jit(solution)/shard_map/ppermute | solution.py:444
  35.9 1.2 %copy-start.9 = (bf16[4,32,4096]{2,1,0:T(8,128)(2,1)S(1)}, bf16[4,32,4096]{2,1,0:T(8,128)(2,1)}, u32[]{:S(2)}) copy-start(bf16[4,32,4096]{2,1,0:T(8,128)(2,1)} %constant.38.clone.table_ref) | copy-start | bytes 3145732
  42.7 1.9 %copy-start.1 = (f32[2,8,32,16,128]{4,3,2,1,0:T(8,128)}, f32[2,8,32,16,128]{4,3,2,1,0:T(8,128)S(1)}, u32[]{:S(2)}) copy-start(f32[2,8,32,16,128]{4,3,2,1,0:T(8,128)S(1)} %get-tuple-element.10.mix_hbm) | copy-start | bytes 12582916
  44.6 1.3 %copy-start.3 = (f32[2,2048,128]{2,1,0:T(8,128)}, f32[2,2048,128]{2,1,0:T(8,128)S(1)}, u32[]{:S(2)}) copy-start(f32[2,2048,128]{2,1,0:T(8,128)S(1)} %get-tuple-element.9) | copy-start | bytes 6291460
  57.7 9.8 %copy-start.2 = (bf16[1024,512]{1,0:T(8,128)(2,1)S(1)}, bf16[1024,512]{1,0:T(8,128)(2,1)}, u32[]{:S(2)}) copy-start(bf16[1024,512]{1,0:T(8,128)(2,1)} %w_ref.3) | copy-start | bytes 3145732
  66.6 2.7 %collective-permute-start.1 = (bf16[8,256,128]{2,1,0:T(8,128)(2,1)}, bf16[8,256,128]{2,1,0:T(8,128)(2,1)S(1)}, u32[]{:S(2)}, u32[]{:S(2)}) collective-permute-start(bf16[8,256,128]{2,1,0:T(8,128)(2,1)} %get-tuple-element.11), channel_id=1, source_target_pairs={{0,1},{1,0},{2,3},{3,2},{4,5},{5,4},{6,7},{7,6},{8,9},{9,8},{10,11... | collective-permute-start | bytes 1572872 | tf_op jit(solution)/shard_map/ppermute | solution.py:458
  67.5 1.0 %copy-start.5 = (bf16[8,256,128]{2,1,0:T(8,128)(2,1)S(1)}, bf16[8,256,128]{2,1,0:T(8,128)(2,1)}, u32[]{:S(2)}) copy-start(bf16[8,256,128]{2,1,0:T(8,128)(2,1)} %get-tuple-element.12.part_ref) | copy-start | bytes 1572868

commit v6 on v5

--- a/solution.py
+++ b/solution.py
@@ -12,7 +12,6 @@
 BF16 = jnp.bfloat16
 VMEM = pl.BlockSpec(memory_space=pltpu.VMEM)
 LANES = 128
-AHEAD = 8
 SPAN = 16
 
 
@@ -253,11 +252,11 @@
     tiles = groups // 8
     spans = [slice(f * 8, f * 8 + 8) for f in range(tiles)]
 
-    def slot_of(at):
-        return lax.rem(at // per_half + halves - core_ref[0], halves)
-
-    def copies(at):
-        half, place, slot = at // per_half, at % per_half, slot_of(at)
+    def slot_of(half):
+        return lax.rem(half + halves - core_ref[0], halves)
+
+    def copies(half, slot, place):
+        at = half * per_half + place
         first = pl.multiple_of(place * span_steps, span_steps)
         return (
             pltpu.make_async_copy(y_hbm.at[place * halves + half], y_ref.at[at], sems.at[at, 0]),
@@ -265,28 +264,35 @@
             pltpu.make_async_copy(gate_hbm.at[slot, pl.ds(first, span_steps)], gate_ref.at[at], sems.at[at, 2]),
         )
 
-    def result(at, s):
-        return pltpu.make_async_copy(out_ref.at[at], outs[s].at[at % per_half], sems.at[at, 3])
-
-    def launch(at, _):
-        for copy in copies(at):
+    def result(half, place, s):
+        at = half * per_half + place
+        return pltpu.make_async_copy(out_ref.at[at], outs[s].at[place], sems.at[at, 3])
+
+    def launch(half, slot, place):
+        for copy in copies(half, slot, place):
             copy.start()
-        return 0
 
     first_copy = pltpu.make_async_copy(rate_hbm, decay, sems.at[count, 0])
     first_copy.start()
-    lax.fori_loop(0, min(AHEAD, count), launch, 0)
+    first_slot = slot_of(0)
+
+    def launch_first(place, _):
+        launch(0, first_slot, place)
+        return 0
+
+    lax.fori_loop(0, per_half, launch_first, 0)
     held[...] = jnp.zeros_like(held)
     first_copy.wait()
     decay[...] = jnp.exp(-decay[...])
 
-    def one_span(at, _):
-        for copy in copies(at):
+    def one_span(half, slot, next_slot, place):
+        at = half * per_half + place
+        for copy in copies(half, slot, place):
             copy.wait()
 
-        @pl.when(at + AHEAD < count)
+        @pl.when(half + 1 < halves)
         def _():
-            launch(at + AHEAD, 0)
+            launch(half + 1, next_slot, place)
 
         v_scr[...] = y_ref[at].astype(F32)
         carry = [held[n, span, :] for n in range(state) for span in spans]
@@ -307,21 +313,30 @@
                 held[n, span, :] = carry[n * tiles + f]
         out_ref[at] = g_scr[...].astype(BF16)
         for s in range(halves):
-            @pl.when(slot_of(at) == s)
+            @pl.when(slot == s)
             def _(s=s):
-                result(at, s).start()
+                result(half, place, s).start()
+
+    def one_half(half, _):
+        slot, next_slot = slot_of(half), slot_of(half + 1)
+
+        def step(place, _):
+            one_span(half, slot, next_slot, place)
+            return 0
+
+        return lax.fori_loop(0, per_half, step, 0)
+
+    lax.fori_loop(0, halves, one_half, 0)
+
+    def finish(half, _):
+        for s in range(halves):
+            @pl.when(slot_of(half) == s)
+            def _(s=s):
+                for place in range(per_half):
+                    result(half, place, s).wait()
         return 0
 
-    lax.fori_loop(0, count, one_span, 0)
-
-    def finish(at, _):
-        for s in range(halves):
-            @pl.when(slot_of(at) == s)
-            def _(s=s):
-                result(at, s).wait()
-        return 0
-
-    lax.fori_loop(0, count, finish, 0)
+    lax.fori_loop(0, halves, finish, 0)
 
 
 def col_scan(core, y, gate, mix, rate):

time: 71.4 us -> 71.2 us (level)
  no operation moved by 1% of the time
where the time goes in v6:
time: 71.2 us; the launch traced here: 70.7 us
  Pallas kernels  24 us (34%)
  waiting for transfers between devices  22.1 us (31%)
  starting transfers between devices  14.3 us (20%)
  local copies, waits for them, and re-layouts  10 us (14%)
    all_to_all x1, waiting for transfers between devices, per_device(): lax.all_to_all(row_mixed, both, split_axis=0, concat_axis=0, tiled=True)  11.7 us
    all_to_all x1, waiting for transfers between devices, per_device(): lax.all_to_all(tokens.reshape(parts, items, columns, features), 'rows', s...  10.4 us
    pallas_call x1, Pallas kernels, col_scan(): pl.pallas_call(functools.partial(col_kernel, state, halves), name='col_sc...  8.76 us
    pallas_call x1, Pallas kernels, row_scan(): pl.pallas_call(functools.partial(row_kernel, parts, items, columns, halve...  7.4 us
    all_to_all x1, starting transfers between devices, per_device(): lax.all_to_all(row_mixed, both, split_axis=0, concat_axis=0, tiled=True)  7.26 us
    all_to_all x1, starting transfers between devices, per_device(): lax.all_to_all(tokens.reshape(parts, items, columns, features), 'rows', s...  5.71 us
    unnamed x27, local copies, waits for them, and re-layouts  5.69 us
    pallas_call x1, Pallas kernels, home(): pl.pallas_call(functools.partial(home_kernel, columns, halves), name='hom...  5.55 us
  transfers between devices with their start and end apart: 4, of which 2 were waited for; matrix products, arithmetic and copies ran while one was open for 6% of the time, Pallas kernels for 9%

profile of v6, /device:TPU:17, one launch (start us, length us, event | category | flops | bytes accessed | tf_op | source)
XLA Modules:
  0.0 70.7 jit_solution(7071380518926267935)
XLA Ops:
  0.0 5.7 %all-to-all-start = ((bf16[8,16,4,512]{3,2,1,0:T(4,128)(2,1)}), bf16[8,16,4,512]{3,2,1,0:T(4,128)(2,1)S(1)}, u32[]{:S(2)}, u32[]{:S(2)}) async-start(bf16[8,16,4,512]{3,2,1,0:T(4,128)(2,1)} %bitcast.11), calls=%async_computation | async-start | bytes 1048576 | tf_op jit(solution)/shard_map/all_to_all | solution.py:447
  5.7 0.0 copy-start.8
  5.7 1.4 %slice.15.wu_ref = bf16[512,1024]{1,0:T(8,128)(2,1)S(1)} slice(bf16[512,2048]{1,0:T(8,128)(2,1)} %param.16), slice={[0:512], [0:1024]} | slice | bytes 2097152 | tf_op jit(solution)/shard_map/slice | solution.py:453
  7.1 0.1 copy.15
  7.2 0.1 copy.17
  7.4 0.3 concatenate.3.wbc_ref
  7.7 10.4 %all-to-all-done = bf16[8,16,4,512]{3,2,1,0:T(4,128)(2,1)S(1)} async-done(((bf16[8,16,4,512]{3,2,1,0:T(4,128)(2,1)}), bf16[8,16,4,512]{3,2,1,0:T(4,128)(2,1)S(1)}, u32[]{:S(2)}, u32[]{:S(2)}) %all-to-all-start) | async-done | bytes 524320 | tf_op jit(solution)/shard_map/all_to_all | solution.py:447
  18.1 0.1 reshape.29.x_ref
  18.2 7.4 %row_scan.1 = bf16[8,2,256,128]{3,2,1,0:T(8,128)(2,1)} custom-call(bf16[8,64,512]{2,1,0:T(8,128)(2,1)S(1)} %reshape.29.x_ref, f32[1,512]{1,0:T(1,128)S(1)} %bitcast.9, bf16[512,1024]{1,0:T(8,128)(2,1)S(1)} %slice.15.wu_ref, bf16[512,256]{1,0:T(8,128)(2,1)S(1)} %concatenate.3.wbc_ref, f32[16,1024]{1,0:T(8,128)S(1)} %copy-done.6, f32[1,1024]{1,0:T(1,128)S(1)} %bitcast.8, ...), custom_call_target="tpu_custom_call" | custom-call | flops 8589934592 | bytes 4194304 | tf_op jit(solution)/shard_map/row_scan/pallas_call | solution.py:165
  25.7 0.0 copy-start.11
  25.7 0.0 slice-start
  25.7 7.3 %all-to-all-start.1 = ((bf16[16,256,128]{2,1,0:T(8,128)(2,1)}), bf16[16,256,128]{2,1,0:T(8,128)(2,1)}, u32[]{:S(2)}, u32[]{:S(2)}) async-start(bf16[16,256,128]{2,1,0:T(8,128)(2,1)} %bitcast.5), calls=%async_computation.1 | async-start | bytes 2097152 | tf_op jit(solution)/shard_map/all_to_all | solution.py:455
  32.9 0.0 copy-start.10
  33.0 0.1 reshape.31.refs_0_
  33.1 0.4 collective-permute-start
  33.5 0.1 copy.20.wm_ref
  33.7 0.1 tile.10
  33.8 0.1 tile.11
  33.9 0.9 %tile.12.rate_hbm = f32[16,16,128]{2,1,0:T(8,128)} reshape(f32[16,16,4,32]{3,2,1,0:T(4,128)S(1)} %tile.11) | data formatting | bytes 262144 | tf_op jit(solution)/shard_map/tile | solution.py:465
  34.8 1.1 %constant_dynamic-slice_fusion.1.wz_ref = bf16[512,512]{1,0:T(8,128)(2,1)S(1)} fusion(bf16[512,2048]{1,0:T(8,128)(2,1)} %param.16, s32[]{:T(128)S(6)} %select_n.14), kind=kLoop, calls=%fused_computation.1 | loop fusion | bytes 1048580 | tf_op jit(solution)/shard_map/dynamic_slice | solution.py:462
  35.9 0.0 collective-permute-done.refs_1_
  35.9 0.0 copy-start.9
  35.9 1.2 %copy-done.9 = bf16[4,32,4096]{2,1,0:T(8,128)(2,1)S(1)} copy-done((bf16[4,32,4096]{2,1,0:T(8,128)(2,1)S(1)}, bf16[4,32,4096]{2,1,0:T(8,128)(2,1)}, u32[]{:S(2)}) %copy-start.9) | copy-done | bytes 1048600
  37.1 5.5 %home.1 = (f32[2,2048,128]{2,1,0:T(8,128)S(1)}, f32[2,8,32,16,128]{4,3,2,1,0:T(8,128)S(1)}) custom-call(f32[1,512]{1,0:T(1,128)S(1)} %bitcast.10, bf16[512,512]{1,0:T(8,128)(2,1)S(1)} %constant_dynamic-slice_fusion.1.wz_ref, bf16[512,32]{1,0:T(8,128)(2,1)S(1)} %copy.20.wm_ref, bf16[64,64]{1,0:T(8,128)(2,1)S(1)} %copy-done.10, ...), custom_call_target="tpu_custom_call" | custom-call | flops 1073741824 | bytes 8388608 | tf_op jit(solution)/shard_map/home/pallas_call | solution.py:228
  42.7 1.9 %copy-done.1 = f32[2,8,32,16,128]{4,3,2,1,0:T(8,128)} copy-done((f32[2,8,32,16,128]{4,3,2,1,0:T(8,128)}, f32[2,8,32,16,128]{4,3,2,1,0:T(8,128)S(1)}, u32[]{:S(2)}) %copy-start.1) | copy-done | bytes 4194328
  44.6 1.3 %copy-done.3 = f32[2,2048,128]{2,1,0:T(8,128)} copy-done((f32[2,2048,128]{2,1,0:T(8,128)}, f32[2,2048,128]{2,1,0:T(8,128)S(1)}, u32[]{:S(2)}) %copy-start.3) | copy-done | bytes 2097176
  46.0 11.7 %all-to-all-done.1.y_hbm = bf16[16,256,128]{2,1,0:T(8,128)(2,1)} async-done(((bf16[16,256,128]{2,1,0:T(8,128)(2,1)}), bf16[16,256,128]{2,1,0:T(8,128)(2,1)}, u32[]{:S(2)}, u32[]{:S(2)}) %all-to-all-start.1) | async-done | bytes 1048608 | tf_op jit(solution)/shard_map/all_to_all | solution.py:455
  57.7 8.8 %col_scan.1 = (bf16[8,256,128]{2,1,0:T(8,128)(2,1)}, bf16[8,256,128]{2,1,0:T(8,128)(2,1)}) custom-call(s32[1]{0:T(128)} %bitcast.1.core_ref.group_ref, bf16[16,256,128]{2,1,0:T(8,128)(2,1)} %all-to-all-done.1.y_hbm, f32[2,128,16,128]{3,2,1,0:T(8,128)} %bitcast.7, f32[2,8,32,16,128]{4,3,2,1,0:T(8,128)} %copy-done.1, f32[16,16,128]{2,1,0:T(8,128)} %tile.12.rate_hbm), custom_call_target="tpu_custom_call" | custom-call | flops 41943040 | bytes 8388608 | tf_op jit(solution)/shard_map/col_scan/pallas_call | solution.py:347
  66.5 0.9 %collective-permute-start.1 = (bf16[8,256,128]{2,1,0:T(8,128)(2,1)}, bf16[8,256,128]{2,1,0:T(8,128)(2,1)S(1)}, u32[]{:S(2)}, u32[]{:S(2)}) collective-permute-start(bf16[8,256,128]{2,1,0:T(8,128)(2,1)} %get-tuple-element.11), channel_id=1, source_target_pairs={{0,1},{1,0},{2,3},{3,2},{4,5},{5,4},{6,7},{7,6},{8,9},{9,8},{10,11... | collective-permute-start | bytes 1572872 | tf_op jit(solution)/shard_map/ppermute | solution.py:473
  67.4 1.0 %copy-done.5 = bf16[8,256,128]{2,1,0:T(8,128)(2,1)S(1)} copy-done((bf16[8,256,128]{2,1,0:T(8,128)(2,1)S(1)}, bf16[8,256,128]{2,1,0:T(8,128)(2,1)}, u32[]{:S(2)}) %copy-start.5) | copy-done | bytes 524312
  68.4 0.7 %last.2.refs_0_ = f32[512,512]{1,0:T(8,128)S(1)} custom-call(s32[1]{0:T(128)} %bitcast.1.core_ref.group_ref, bf16[8,256,128]{2,1,0:T(8,128)(2,1)S(1)} %copy-done.5, bf16[1024,512]{1,0:T(8,128)(2,1)S(1)} %copy-done.2, bf16[512,512]{1,0:T(8,128)(2,1)S(1)} %copy-done.4), custom_call_target="tpu_custom_call" | custom-call | flops 268435456 | bytes 2097152 | tf_op jit(solution)/shard_map/last/pallas_call | solution.py:400
  69.2 1.6 %last.3 = bf16[128,4,512]{2,1,0:T(4,128)(2,1)} custom-call(s32[1]{0:T(128)} %bitcast.group_ref, bf16[8,256,128]{2,1,0:T(8,128)(2,1)S(1)} %collective-permute-done.1.part_ref, bf16[1024,512]{1,0:T(8,128)(2,1)S(1)} %copy-done.2, bf16[512,512]{1,0:T(8,128)(2,1)S(1)} %copy-done.4, f32[512,512]{1,0:T(8,128)S(1)} %last.2.refs_0_), custom_call_target="tpu_custom_call" | custom-call | flops 268435456 | bytes 2097152 | tf_op jit(solution)/shard_map/last/pallas_call | solution.py:400
  (23 shorter events, 0.1 us)
Async XLA Ops:
  0.0 33.7 %copy-start = (f32[16,1024]{1,0:T(8,128)S(1)}, f32[16,1024]{1,0:T(8,128)}, u32[]{:S(2)}) copy-start(f32[16,1024]{1,0:T(8,128)} %param.19) | copy-start | bytes 196612
  0.0 7.1 %copy-start.12 = (bf16[512,64]{0,1:T(8,128)(2,1)S(1)}, bf16[512,64]{0,1:T(8,128)(2,1)}, u32[]{:S(2)}) copy-start(bf16[512,64]{0,1:T(8,128)(2,1)} %param.17) | copy-start | bytes 196612
  0.0 18.1 %all-to-all-start = ((bf16[8,16,4,512]{3,2,1,0:T(4,128)(2,1)}), bf16[8,16,4,512]{3,2,1,0:T(4,128)(2,1)S(1)}, u32[]{:S(2)}, u32[]{:S(2)}) async-start(bf16[8,16,4,512]{3,2,1,0:T(4,128)(2,1)} %bitcast.11), calls=%async_computation | async-start | bytes 1048576 | tf_op jit(solution)/shard_map/all_to_all | solution.py:447
  5.7 12.5 %copy-start.4 = (bf16[512,512]{1,0:T(8,128)(2,1)S(1)}, bf16[512,512]{1,0:T(8,128)(2,1)}, u32[]{:S(2)}) copy-start(bf16[512,512]{1,0:T(8,128)(2,1)} %constant.36.clone.lane_ref) | copy-start | bytes 1572868
  5.7 12.5 %copy-start.6 = (f32[16,1024]{1,0:T(8,128)S(1)}, f32[16,1024]{1,0:T(8,128)}, u32[]{:S(2)}) copy-start(f32[16,1024]{1,0:T(8,128)} %rate_ref.1) | copy-start | bytes 196612
  5.7 12.5 %copy-start.7 = (f32[1024]{0:T(1024)S(1)}, f32[1024]{0:T(1024)}, u32[]{:S(2)}) copy-start(f32[1024]{0:T(1024)} %param.20) | copy-start | bytes 12292
  5.7 12.5 %copy-start.8 = (f32[512]{0:T(512)S(1)}, f32[512]{0:T(512)}, u32[]{:S(2)}) copy-start(f32[512]{0:T(512)} %param.15) | copy-start | bytes 6148
  25.7 7.3 %copy-start.11 = (bf16[128,4,512]{2,1,0:T(4,128)(2,1)S(1)}, bf16[128,4,512]{2,1,0:T(4,128)(2,1)}, u32[]{:S(2)}) copy-start(bf16[128,4,512]{2,1,0:T(4,128)(2,1)} %param.14) | copy-start | bytes 1572868
  25.7 7.8 %slice-start = ((bf16[512,64]{0,1:T(8,128)(2,1)}), bf16[512,32]{0,1:T(8,128)(2,1)S(1)}, s32[]{:S(2)}) async-start(bf16[512,64]{0,1:T(8,128)(2,1)} %param.17), calls=%async_computation.2 | async-start | bytes 65536 | tf_op jit(solution)/shard_map/slice | solution.py:463
  25.7 32.0 %all-to-all-start.1 = ((bf16[16,256,128]{2,1,0:T(8,128)(2,1)}), bf16[16,256,128]{2,1,0:T(8,128)(2,1)}, u32[]{:S(2)}, u32[]{:S(2)}) async-start(bf16[16,256,128]{2,1,0:T(8,128)(2,1)} %bitcast.5), calls=%async_computation.1 | async-start | bytes 2097152 | tf_op jit(solution)/shard_map/all_to_all | solution.py:455
  32.9 3.0 %copy-start.10 = (bf16[64,64]{1,0:T(8,128)(2,1)S(1)}, bf16[64,64]{1,0:T(8,128)(2,1)}, u32[]{:S(2)}) copy-start(bf16[64,64]{1,0:T(8,128)(2,1)} %constant.37.clone.order_ref) | copy-start | bytes 24580
  33.1 2.8 %collective-permute-start = (bf16[512,512]{1,0:T(8,128)(2,1)S(1)}, bf16[512,512]{1,0:T(8,128)(2,1)S(1)}, u32[]{:S(2)}, u32[]{:S(2)}) collective-permute-start(bf16[512,512]{1,0:T(8,128)(2,1)S(1)} %reshape.31.refs_0_), channel_id=1, source_target_pairs={{0,1},{1,0},{2,3},{3,2},{4,5},{5,4},{6,7},{7,6},{8,9},{9,8},{10,11... | collective-permute-start | bytes 1572872 | tf_op jit(solution)/shard_map/ppermute | solution.py:459
  35.9 1.2 %copy-start.9 = (bf16[4,32,4096]{2,1,0:T(8,128)(2,1)S(1)}, bf16[4,32,4096]{2,1,0:T(8,128)(2,1)}, u32[]{:S(2)}) copy-start(bf16[4,32,4096]{2,1,0:T(8,128)(2,1)} %constant.38.clone.table_ref) | copy-start | bytes 3145732
  42.7 1.9 %copy-start.1 = (f32[2,8,32,16,128]{4,3,2,1,0:T(8,128)}, f32[2,8,32,16,128]{4,3,2,1,0:T(8,128)S(1)}, u32[]{:S(2)}) copy-start(f32[2,8,32,16,128]{4,3,2,1,0:T(8,128)S(1)} %get-tuple-element.10.mix_hbm) | copy-start | bytes 12582916
  44.6 1.3 %copy-start.3 = (f32[2,2048,128]{2,1,0:T(8,128)}, f32[2,2048,128]{2,1,0:T(8,128)S(1)}, u32[]{:S(2)}) copy-start(f32[2,2048,128]{2,1,0:T(8,128)S(1)} %get-tuple-element.9) | copy-start | bytes 6291460
  57.7 9.7 %copy-start.2 = (bf16[1024,512]{1,0:T(8,128)(2,1)S(1)}, bf16[1024,512]{1,0:T(8,128)(2,1)}, u32[]{:S(2)}) copy-start(bf16[1024,512]{1,0:T(8,128)(2,1)} %w_ref.3) | copy-start | bytes 3145732
  66.5 2.7 %collective-permute-start.1 = (bf16[8,256,128]{2,1,0:T(8,128)(2,1)}, bf16[8,256,128]{2,1,0:T(8,128)(2,1)S(1)}, u32[]{:S(2)}, u32[]{:S(2)}) collective-permute-start(bf16[8,256,128]{2,1,0:T(8,128)(2,1)} %get-tuple-element.11), channel_id=1, source_target_pairs={{0,1},{1,0},{2,3},{3,2},{4,5},{5,4},{6,7},{7,6},{8,9},{9,8},{10,11... | collective-permute-start | bytes 1572872 | tf_op jit(solution)/shard_map/ppermute | solution.py:473
  67.4 1.0 %copy-start.5 = (bf16[8,256,128]{2,1,0:T(8,128)(2,1)S(1)}, bf16[8,256,128]{2,1,0:T(8,128)(2,1)}, u32[]{:S(2)}) copy-start(bf16[8,256,128]{2,1,0:T(8,128)(2,1)} %get-tuple-element.12.part_ref) | copy-start | bytes 1572868

commit v7 on v5

--- a/solution.py
+++ b/solution.py
@@ -75,7 +75,7 @@
     mix = dot(normed[...], wbc_ref[...]).astype(BF16).astype(F32)
     b_scr[...] = mix[:, :2 * state]
     c_scr[...] = mix[:, LANES:LANES + 2 * state]
-    chunk = 128
+    chunk = 256
     pieces = []
     at = 0
     for lag in range(steps):

time: 71.4 us -> 71.3 us (level)
  no operation moved by 1% of the time
where the time goes in v7:
time: 71.3 us; the launch traced here: 70.9 us
  Pallas kernels  24.1 us (34%)
  waiting for transfers between devices  22.1 us (31%)
  starting transfers between devices  14.3 us (20%)
  local copies, waits for them, and re-layouts  10 us (14%)
    all_to_all x1, waiting for transfers between devices, per_device(): lax.all_to_all(row_mixed, both, split_axis=0, concat_axis=0, tiled=True)  11.7 us
    all_to_all x1, waiting for transfers between devices, per_device(): lax.all_to_all(tokens.reshape(parts, items, columns, features), 'rows', s...  10.4 us
    pallas_call x1, Pallas kernels, col_scan(): pl.pallas_call(functools.partial(col_kernel, state, halves), name='col_sc...  8.91 us
    pallas_call x1, Pallas kernels, row_scan(): pl.pallas_call(functools.partial(row_kernel, parts, items, columns, halve...  7.37 us
    all_to_all x1, starting transfers between devices, per_device(): lax.all_to_all(row_mixed, both, split_axis=0, concat_axis=0, tiled=True)  7.26 us
    all_to_all x1, starting transfers between devices, per_device(): lax.all_to_all(tokens.reshape(parts, items, columns, features), 'rows', s...  5.71 us
    unnamed x27, local copies, waits for them, and re-layouts  5.69 us
    pallas_call x1, Pallas kernels, home(): pl.pallas_call(functools.partial(home_kernel, columns, halves), name='hom...  5.55 us
  transfers between devices with their start and end apart: 4, of which 2 were waited for; matrix products, arithmetic and copies ran while one was open for 6% of the time, Pallas kernels for 9%

profile of v7, /device:TPU:17, one launch (start us, length us, event | category | flops | bytes accessed | tf_op | source)
XLA Modules:
  0.0 70.9 jit_solution(16939490863667646346)
XLA Ops:
  0.0 5.7 %all-to-all-start = ((bf16[8,16,4,512]{3,2,1,0:T(4,128)(2,1)}), bf16[8,16,4,512]{3,2,1,0:T(4,128)(2,1)S(1)}, u32[]{:S(2)}, u32[]{:S(2)}) async-start(bf16[8,16,4,512]{3,2,1,0:T(4,128)(2,1)} %bitcast.11), calls=%async_computation | async-start | bytes 1048576 | tf_op jit(solution)/shard_map/all_to_all | solution.py:432
  5.7 0.0 copy-start.8
  5.7 1.4 %slice.15.wu_ref = bf16[512,1024]{1,0:T(8,128)(2,1)S(1)} slice(bf16[512,2048]{1,0:T(8,128)(2,1)} %param.16), slice={[0:512], [0:1024]} | slice | bytes 2097152 | tf_op jit(solution)/shard_map/slice | solution.py:438
  7.1 0.1 copy.15
  7.2 0.1 copy.17
  7.4 0.3 concatenate.3.wbc_ref
  7.7 10.4 %all-to-all-done = bf16[8,16,4,512]{3,2,1,0:T(4,128)(2,1)S(1)} async-done(((bf16[8,16,4,512]{3,2,1,0:T(4,128)(2,1)}), bf16[8,16,4,512]{3,2,1,0:T(4,128)(2,1)S(1)}, u32[]{:S(2)}, u32[]{:S(2)}) %all-to-all-start) | async-done | bytes 524320 | tf_op jit(solution)/shard_map/all_to_all | solution.py:432
  18.1 0.1 reshape.29.x_ref
  18.2 7.4 %row_scan.1 = bf16[8,2,256,128]{3,2,1,0:T(8,128)(2,1)} custom-call(bf16[8,64,512]{2,1,0:T(8,128)(2,1)S(1)} %reshape.29.x_ref, f32[1,512]{1,0:T(1,128)S(1)} %bitcast.9, bf16[512,1024]{1,0:T(8,128)(2,1)S(1)} %slice.15.wu_ref, bf16[512,256]{1,0:T(8,128)(2,1)S(1)} %concatenate.3.wbc_ref, f32[16,1024]{1,0:T(8,128)S(1)} %copy-done.6, f32[1,1024]{1,0:T(1,128)S(1)} %bitcast.8, ...), custom_call_target="tpu_custom_call" | custom-call | flops 8589934592 | bytes 4194304 | tf_op jit(solution)/shard_map/row_scan/pallas_call | solution.py:166
  25.6 0.0 copy-start.11
  25.6 0.0 slice-start
  25.7 7.3 %all-to-all-start.1 = ((bf16[16,256,128]{2,1,0:T(8,128)(2,1)}), bf16[16,256,128]{2,1,0:T(8,128)(2,1)}, u32[]{:S(2)}, u32[]{:S(2)}) async-start(bf16[16,256,128]{2,1,0:T(8,128)(2,1)} %bitcast.5), calls=%async_computation.1 | async-start | bytes 2097152 | tf_op jit(solution)/shard_map/all_to_all | solution.py:440
  32.9 0.0 copy-start.10
  32.9 0.1 reshape.31.refs_0_
  33.1 0.4 collective-permute-start
  33.5 0.1 copy.20.wm_ref
  33.6 0.1 tile.10
  33.7 0.1 tile.11
  33.9 0.9 %tile.12.rate_hbm = f32[16,16,128]{2,1,0:T(8,128)} reshape(f32[16,16,4,32]{3,2,1,0:T(4,128)S(1)} %tile.11) | data formatting | bytes 262144 | tf_op jit(solution)/shard_map/tile | solution.py:450
  34.8 1.1 %constant_dynamic-slice_fusion.1.wz_ref = bf16[512,512]{1,0:T(8,128)(2,1)S(1)} fusion(bf16[512,2048]{1,0:T(8,128)(2,1)} %param.16, s32[]{:T(128)S(6)} %select_n.14), kind=kLoop, calls=%fused_computation.1 | loop fusion | bytes 1048580 | tf_op jit(solution)/shard_map/dynamic_slice | solution.py:447
  35.9 0.0 collective-permute-done.refs_1_
  35.9 0.0 copy-start.9
  35.9 1.2 %copy-done.9 = bf16[4,32,4096]{2,1,0:T(8,128)(2,1)S(1)} copy-done((bf16[4,32,4096]{2,1,0:T(8,128)(2,1)S(1)}, bf16[4,32,4096]{2,1,0:T(8,128)(2,1)}, u32[]{:S(2)}) %copy-start.9) | copy-done | bytes 1048600
  37.1 5.5 %home.1 = (f32[2,2048,128]{2,1,0:T(8,128)S(1)}, f32[2,8,32,16,128]{4,3,2,1,0:T(8,128)S(1)}) custom-call(f32[1,512]{1,0:T(1,128)S(1)} %bitcast.10, bf16[512,512]{1,0:T(8,128)(2,1)S(1)} %constant_dynamic-slice_fusion.1.wz_ref, bf16[512,32]{1,0:T(8,128)(2,1)S(1)} %copy.20.wm_ref, bf16[64,64]{1,0:T(8,128)(2,1)S(1)} %copy-done.10, ...), custom_call_target="tpu_custom_call" | custom-call | flops 1073741824 | bytes 8388608 | tf_op jit(solution)/shard_map/home/pallas_call | solution.py:229
  42.7 1.9 %copy-done.1 = f32[2,8,32,16,128]{4,3,2,1,0:T(8,128)} copy-done((f32[2,8,32,16,128]{4,3,2,1,0:T(8,128)}, f32[2,8,32,16,128]{4,3,2,1,0:T(8,128)S(1)}, u32[]{:S(2)}) %copy-start.1) | copy-done | bytes 4194328
  44.6 1.3 %copy-done.3 = f32[2,2048,128]{2,1,0:T(8,128)} copy-done((f32[2,2048,128]{2,1,0:T(8,128)}, f32[2,2048,128]{2,1,0:T(8,128)S(1)}, u32[]{:S(2)}) %copy-start.3) | copy-done | bytes 2097176
  45.9 11.7 %all-to-all-done.1.y_hbm = bf16[16,256,128]{2,1,0:T(8,128)(2,1)} async-done(((bf16[16,256,128]{2,1,0:T(8,128)(2,1)}), bf16[16,256,128]{2,1,0:T(8,128)(2,1)}, u32[]{:S(2)}, u32[]{:S(2)}) %all-to-all-start.1) | async-done | bytes 1048608 | tf_op jit(solution)/shard_map/all_to_all | solution.py:440
  57.7 8.9 %col_scan.1 = (bf16[8,256,128]{2,1,0:T(8,128)(2,1)}, bf16[8,256,128]{2,1,0:T(8,128)(2,1)}) custom-call(s32[1]{0:T(128)} %bitcast.1.core_ref.group_ref, bf16[16,256,128]{2,1,0:T(8,128)(2,1)} %all-to-all-done.1.y_hbm, f32[2,128,16,128]{3,2,1,0:T(8,128)} %bitcast.7, f32[2,8,32,16,128]{4,3,2,1,0:T(8,128)} %copy-done.1, f32[16,16,128]{2,1,0:T(8,128)} %tile.12.rate_hbm), custom_call_target="tpu_custom_call" | custom-call | flops 41943040 | bytes 8388608 | tf_op jit(solution)/shard_map/col_scan/pallas_call | solution.py:332
  66.6 0.9 %collective-permute-start.1 = (bf16[8,256,128]{2,1,0:T(8,128)(2,1)}, bf16[8,256,128]{2,1,0:T(8,128)(2,1)S(1)}, u32[]{:S(2)}, u32[]{:S(2)}) collective-permute-start(bf16[8,256,128]{2,1,0:T(8,128)(2,1)} %get-tuple-element.11), channel_id=1, source_target_pairs={{0,1},{1,0},{2,3},{3,2},{4,5},{5,4},{6,7},{7,6},{8,9},{9,8},{10,11... | collective-permute-start | bytes 1572872 | tf_op jit(solution)/shard_map/ppermute | solution.py:458
  67.5 1.0 %copy-done.5 = bf16[8,256,128]{2,1,0:T(8,128)(2,1)S(1)} copy-done((bf16[8,256,128]{2,1,0:T(8,128)(2,1)S(1)}, bf16[8,256,128]{2,1,0:T(8,128)(2,1)}, u32[]{:S(2)}) %copy-start.5) | copy-done | bytes 524312
  68.6 0.7 %last.2.refs_0_ = f32[512,512]{1,0:T(8,128)S(1)} custom-call(s32[1]{0:T(128)} %bitcast.1.core_ref.group_ref, bf16[8,256,128]{2,1,0:T(8,128)(2,1)S(1)} %copy-done.5, bf16[1024,512]{1,0:T(8,128)(2,1)S(1)} %copy-done.2, bf16[512,512]{1,0:T(8,128)(2,1)S(1)} %copy-done.4), custom_call_target="tpu_custom_call" | custom-call | flops 268435456 | bytes 2097152 | tf_op jit(solution)/shard_map/last/pallas_call | solution.py:385
  69.3 1.6 %last.3 = bf16[128,4,512]{2,1,0:T(4,128)(2,1)} custom-call(s32[1]{0:T(128)} %bitcast.group_ref, bf16[8,256,128]{2,1,0:T(8,128)(2,1)S(1)} %collective-permute-done.1.part_ref, bf16[1024,512]{1,0:T(8,128)(2,1)S(1)} %copy-done.2, bf16[512,512]{1,0:T(8,128)(2,1)S(1)} %copy-done.4, f32[512,512]{1,0:T(8,128)S(1)} %last.2.refs_0_), custom_call_target="tpu_custom_call" | custom-call | flops 268435456 | bytes 2097152 | tf_op jit(solution)/shard_map/last/pallas_call | solution.py:385
  (23 shorter events, 0.1 us)
Async XLA Ops:
  0.0 33.6 %copy-start = (f32[16,1024]{1,0:T(8,128)S(1)}, f32[16,1024]{1,0:T(8,128)}, u32[]{:S(2)}) copy-start(f32[16,1024]{1,0:T(8,128)} %param.19) | copy-start | bytes 196612
  0.0 7.1 %copy-start.12 = (bf16[512,64]{0,1:T(8,128)(2,1)S(1)}, bf16[512,64]{0,1:T(8,128)(2,1)}, u32[]{:S(2)}) copy-start(bf16[512,64]{0,1:T(8,128)(2,1)} %param.17) | copy-start | bytes 196612
  0.0 18.1 %all-to-all-start = ((bf16[8,16,4,512]{3,2,1,0:T(4,128)(2,1)}), bf16[8,16,4,512]{3,2,1,0:T(4,128)(2,1)S(1)}, u32[]{:S(2)}, u32[]{:S(2)}) async-start(bf16[8,16,4,512]{3,2,1,0:T(4,128)(2,1)} %bitcast.11), calls=%async_computation | async-start | bytes 1048576 | tf_op jit(solution)/shard_map/all_to_all | solution.py:432
  5.7 12.5 %copy-start.4 = (bf16[512,512]{1,0:T(8,128)(2,1)S(1)}, bf16[512,512]{1,0:T(8,128)(2,1)}, u32[]{:S(2)}) copy-start(bf16[512,512]{1,0:T(8,128)(2,1)} %constant.36.clone.lane_ref) | copy-start | bytes 1572868
  5.7 12.5 %copy-start.6 = (f32[16,1024]{1,0:T(8,128)S(1)}, f32[16,1024]{1,0:T(8,128)}, u32[]{:S(2)}) copy-start(f32[16,1024]{1,0:T(8,128)} %rate_ref.1) | copy-start | bytes 196612
  5.7 12.5 %copy-start.7 = (f32[1024]{0:T(1024)S(1)}, f32[1024]{0:T(1024)}, u32[]{:S(2)}) copy-start(f32[1024]{0:T(1024)} %param.20) | copy-start | bytes 12292
  5.7 12.5 %copy-start.8 = (f32[512]{0:T(512)S(1)}, f32[512]{0:T(512)}, u32[]{:S(2)}) copy-start(f32[512]{0:T(512)} %param.15) | copy-start | bytes 6148
  25.6 7.3 %copy-start.11 = (bf16[128,4,512]{2,1,0:T(4,128)(2,1)S(1)}, bf16[128,4,512]{2,1,0:T(4,128)(2,1)}, u32[]{:S(2)}) copy-start(bf16[128,4,512]{2,1,0:T(4,128)(2,1)} %param.14) | copy-start | bytes 1572868
  25.6 7.9 %slice-start = ((bf16[512,64]{0,1:T(8,128)(2,1)}), bf16[512,32]{0,1:T(8,128)(2,1)S(1)}, s32[]{:S(2)}) async-start(bf16[512,64]{0,1:T(8,128)(2,1)} %param.17), calls=%async_computation.2 | async-start | bytes 65536 | tf_op jit(solution)/shard_map/slice | solution.py:448
  25.7 32.0 %all-to-all-start.1 = ((bf16[16,256,128]{2,1,0:T(8,128)(2,1)}), bf16[16,256,128]{2,1,0:T(8,128)(2,1)}, u32[]{:S(2)}, u32[]{:S(2)}) async-start(bf16[16,256,128]{2,1,0:T(8,128)(2,1)} %bitcast.5), calls=%async_computation.1 | async-start | bytes 2097152 | tf_op jit(solution)/shard_map/all_to_all | solution.py:440
  32.9 3.0 %copy-start.10 = (bf16[64,64]{1,0:T(8,128)(2,1)S(1)}, bf16[64,64]{1,0:T(8,128)(2,1)}, u32[]{:S(2)}) copy-start(bf16[64,64]{1,0:T(8,128)(2,1)} %constant.37.clone.order_ref) | copy-start | bytes 24580
  33.1 2.8 %collective-permute-start = (bf16[512,512]{1,0:T(8,128)(2,1)S(1)}, bf16[512,512]{1,0:T(8,128)(2,1)S(1)}, u32[]{:S(2)}, u32[]{:S(2)}) collective-permute-start(bf16[512,512]{1,0:T(8,128)(2,1)S(1)} %reshape.31.refs_0_), channel_id=1, source_target_pairs={{0,1},{1,0},{2,3},{3,2},{4,5},{5,4},{6,7},{7,6},{8,9},{9,8},{10,11... | collective-permute-start | bytes 1572872 | tf_op jit(solution)/shard_map/ppermute | solution.py:444
  35.9 1.2 %copy-start.9 = (bf16[4,32,4096]{2,1,0:T(8,128)(2,1)S(1)}, bf16[4,32,4096]{2,1,0:T(8,128)(2,1)}, u32[]{:S(2)}) copy-start(bf16[4,32,4096]{2,1,0:T(8,128)(2,1)} %constant.38.clone.table_ref) | copy-start | bytes 3145732
  42.7 1.9 %copy-start.1 = (f32[2,8,32,16,128]{4,3,2,1,0:T(8,128)}, f32[2,8,32,16,128]{4,3,2,1,0:T(8,128)S(1)}, u32[]{:S(2)}) copy-start(f32[2,8,32,16,128]{4,3,2,1,0:T(8,128)S(1)} %get-tuple-element.10.mix_hbm) | copy-start | bytes 12582916
  44.6 1.3 %copy-start.3 = (f32[2,2048,128]{2,1,0:T(8,128)}, f32[2,2048,128]{2,1,0:T(8,128)S(1)}, u32[]{:S(2)}) copy-start(f32[2,2048,128]{2,1,0:T(8,128)S(1)} %get-tuple-element.9) | copy-start | bytes 6291460
  57.7 9.8 %copy-start.2 = (bf16[1024,512]{1,0:T(8,128)(2,1)S(1)}, bf16[1024,512]{1,0:T(8,128)(2,1)}, u32[]{:S(2)}) copy-start(bf16[1024,512]{1,0:T(8,128)(2,1)} %w_ref.3) | copy-start | bytes 3145732
  66.6 2.7 %collective-permute-start.1 = (bf16[8,256,128]{2,1,0:T(8,128)(2,1)}, bf16[8,256,128]{2,1,0:T(8,128)(2,1)S(1)}, u32[]{:S(2)}, u32[]{:S(2)}) collective-permute-start(bf16[8,256,128]{2,1,0:T(8,128)(2,1)} %get-tuple-element.11), channel_id=1, source_target_pairs={{0,1},{1,0},{2,3},{3,2},{4,5},{5,4},{6,7},{7,6},{8,9},{9,8},{10,11... | collective-permute-start | bytes 1572872 | tf_op jit(solution)/shard_map/ppermute | solution.py:458
  67.5 1.0 %copy-start.5 = (bf16[8,256,128]{2,1,0:T(8,128)(2,1)S(1)}, bf16[8,256,128]{2,1,0:T(8,128)(2,1)}, u32[]{:S(2)}) copy-start(bf16[8,256,128]{2,1,0:T(8,128)(2,1)} %get-tuple-element.12.part_ref) | copy-start | bytes 1572868
